TPU v7x, 128 devices: a whole 4x4x4 slice. The times are simulated.
128 devices in a mesh: dp: 16 (over y_hi, z, core), seq: 8 (over x, y_lo).
Axes of the slice: x: 4, y: 4 (y_hi: 2, y_lo: 2; y = y_hi * 2 + y_lo), z: 4, core: 2. Of those that a mesh axis runs over, the one named last changes fastest.
Arguments:
- hidden_in: bfloat16 [32, 1024, 1024], P('dp', 'seq'), may hold values from -6 to 6
- out_cotangent: bfloat16 [32, 1024, 1024], P('dp', 'seq'), may hold values from -6 to 6
- slot_lengths: int32 [32], P('dp'), may hold values from 512 to 1024, as said below
- position_ids: int32 [32, 1024], P('dp', 'seq'), may hold values from 0 to 1534, as said below
- attn_gain: bfloat16 [1024], P('dp'), may hold values from 0.25 to 1.75
- w_query: bfloat16 [1024, 2048], P('dp'), may hold values from -0.1875 to 0.1875
- key_weight: bfloat16 [1024, 1024], P('dp'), may hold values from -0.1875 to 0.1875
- value_weight: bfloat16 [1024, 1024], P('dp'), may hold values from -0.1875 to 0.1875
- query_gain: bfloat16 [128], P('dp'), may hold values from 0.25 to 1.75
- key_gain: bfloat16 [128], P('dp'), may hold values from 0.25 to 1.75
- w_output: bfloat16 [2048, 1024], P('dp'), may hold values from -0.375 to 0.375
- ffn_gain: bfloat16 [1024], P('dp'), may hold values from 0.25 to 1.75
- w_gate: bfloat16 [1024, 3072], P('dp'), may hold values from -0.1875 to 0.1875
- w_up: bfloat16 [1024, 3072], P('dp'), may hold values from -0.1875 to 0.1875
- w_down: bfloat16 [3072, 1024], P('dp'), may hold values from -0.109375 to 0.109375
Outputs:
- layer_out: bfloat16 [32, 1024, 1024], P('dp', 'seq')
- input_grad: float32 [32, 1024, 1024], P('dp', 'seq')
- grad_attn_gain: float32 [1024], P('dp')
- grad_query: float32 [1024, 2048], P('dp')
- grad_key: float32 [1024, 1024], P('dp')
- grad_value: float32 [1024, 1024], P('dp')
- grad_query_gain: float32 [128], P('dp')
- grad_key_gain: float32 [128], P('dp')
- grad_output: float32 [2048, 1024], P('dp')
- grad_ffn_gain: float32 [1024], P('dp')
- grad_gate: float32 [1024, 3072], P('dp')
- grad_up: float32 [1024, 3072], P('dp')
- grad_down: float32 [3072, 1024], P('dp')
Inputs may be any that keep to these rules, and one draw needn't show every extreme that they name: `slot_lengths`: in the 2 slots that one index of dp holds, one slot, which one drawn from the seed, is full. `position_ids`: in each slot positions start at 0 and rise by 1 or 2 from token to token; the last is 1534.
All inputs are finite; a program needn't handle non-finite values.
Results may differ from a plain program's by a relative error of at most 0.03.
Values may be sent and summed in bfloat16 or wider, within the bound.
A program may use at most 320 MiB of HBM per device.

v0:
```python
import math

import jax
import jax.numpy as jnp
from jax import lax
from jax.sharding import PartitionSpec as P

epsilon = 1e-06
rope_base = 1000000.0


def as_sent(array):

    def short(part):
        return part.astype(jnp.bfloat16) if part.dtype == jnp.float32 else part

    return jax.tree.map(short, array)


def rms_scale(values, gain_vec):
    return (
        values * lax.rsqrt(jnp.mean(values * values, axis=-1, keepdims=True) + epsilon) * gain_vec
    )


def rotary_tables(position_vector, head_width):
    half_width = head_width // 2
    frequency = jnp.exp(
        jnp.arange(half_width, dtype=jnp.float32) * (-2.0 * math.log(rope_base) / head_width)
    )
    angles = position_vector.astype(jnp.float32)[:, None] * frequency[None, :]
    cos_half = jnp.cos(angles)
    sin_half = jnp.sin(angles)
    return (
        jnp.concatenate([cos_half, cos_half], axis=-1),
        jnp.concatenate([sin_half, sin_half], axis=-1),
    )


def rotate_heads(values, cos_tab, sin_tab):
    half_width = values.shape[-1] // 2
    turned = jnp.concatenate([-values[..., half_width:], values[..., :half_width]], axis=-1)
    return values * cos_tab[:, None, :] + turned * sin_tab[:, None, :]


def head_norm_rope(flat_rows, gain_vec, cos_tab, sin_tab, head_count):
    shaped = flat_rows.reshape(flat_rows.shape[0], head_count, -1)
    return rotate_heads(rms_scale(shaped, gain_vec), cos_tab, sin_tab)


def gated_unit(gate_proj, up_proj):
    return jax.nn.silu(gate_proj) * up_proj


def product(left, right):
    return jnp.dot(left, right, preferred_element_type=jnp.float32)


def cross_rows(left, right):
    return lax.dot_general(
        left, right, (((0,), (0,)), ((), ())), preferred_element_type=jnp.float32
    )


def times_trans(left, right):
    return lax.dot_general(
        left, right, (((1,), (1,)), ((), ())), preferred_element_type=jnp.float32
    )


def block_scores(query_part, keys_in, first_row, score_scale):
    scores = (
        jnp.einsum("qkgd,skd->kgqs", query_part, keys_in, preferred_element_type=jnp.float32)
        * score_scale
    )
    query_order = first_row + jnp.arange(query_part.shape[0], dtype=jnp.int32)
    key_order = jnp.arange(keys_in.shape[0], dtype=jnp.int32)
    allowed = key_order[None, :] <= query_order[:, None]
    return jnp.where(allowed, scores, -1e30)


def block_layout(queries):
    slot_len = queries.shape[0]
    block_len = min(512, slot_len)
    block_count = slot_len // block_len
    block_starts = jnp.arange(block_count, dtype=jnp.int32) * block_len
    return (block_len, block_count, block_starts)


def attend_forward(queries, keys_in, values_in):
    slot_len, q_count, head_width = queries.shape
    key_value_count = keys_in.shape[1]
    group_size = q_count // key_value_count
    score_scale = head_width ** (-0.5)
    block_len, block_count, block_starts = block_layout(queries)
    query_blocks = queries.reshape(block_count, block_len, key_value_count, group_size, head_width)

    def one_block(block_args):
        query_part, first_row = block_args
        scores = block_scores(query_part, keys_in, first_row, score_scale)
        row_max = jnp.max(scores, axis=-1, keepdims=True)
        shifted = jnp.exp(scores - row_max)
        row_sum = jnp.sum(shifted, axis=-1, keepdims=True)
        prob_tab = (shifted / row_sum).astype(jnp.bfloat16)
        attended = jnp.einsum(
            "kgqs,skd->qkgd", prob_tab, values_in, preferred_element_type=jnp.float32
        )
        return (attended.astype(jnp.bfloat16), (row_max + jnp.log(row_sum))[..., 0])

    attended, log_sums = lax.map(one_block, (query_blocks, block_starts))
    return (attended.reshape(slot_len, q_count, head_width), log_sums)


def attend_backward(queries, keys_in, values_in, grad_heads, log_sums):
    slot_len, q_count, head_width = queries.shape
    key_value_count = keys_in.shape[1]
    group_size = q_count // key_value_count
    score_scale = head_width ** (-0.5)
    block_len, block_count, block_starts = block_layout(queries)
    query_blocks = queries.reshape(block_count, block_len, key_value_count, group_size, head_width)
    grad_blocks = grad_heads.reshape(
        block_count, block_len, key_value_count, group_size, head_width
    )

    def one_turn(accum, block_args):
        query_part, grad_part, log_part, first_row = block_args
        scores = block_scores(query_part, keys_in, first_row, score_scale)
        prob_tab = jnp.exp(scores - log_part[..., None])
        grad_prob = jnp.einsum(
            "qkgd,skd->kgqs", grad_part, values_in, preferred_element_type=jnp.float32
        )
        row_dot = jnp.sum(prob_tab * grad_prob, axis=-1, keepdims=True)
        grad_score = (prob_tab * (grad_prob - row_dot) * score_scale).astype(jnp.bfloat16)
        grad_query = jnp.einsum(
            "kgqs,skd->qkgd", grad_score, keys_in, preferred_element_type=jnp.float32
        ).astype(jnp.bfloat16)
        grad_key = accum[0] + jnp.einsum(
            "kgqs,qkgd->skd", grad_score, query_part, preferred_element_type=jnp.float32
        )
        grad_value = accum[1] + jnp.einsum(
            "kgqs,qkgd->skd",
            prob_tab.astype(jnp.bfloat16),
            grad_part,
            preferred_element_type=jnp.float32,
        )
        return ((grad_key, grad_value), grad_query)

    zero_kv = jnp.zeros((slot_len, key_value_count, head_width), jnp.float32)
    (grad_key, grad_value), grad_query = lax.scan(
        one_turn, (zero_kv, zero_kv), (query_blocks, grad_blocks, log_sums, block_starts)
    )
    return (
        grad_query.reshape(slot_len, q_count, head_width),
        grad_key.astype(jnp.bfloat16),
        grad_value.astype(jnp.bfloat16),
    )


def micro_turn(gathered, totals, slot_args):
    x_block, cot_block, length_now, pos_block = slot_args
    (
        g_attn,
        w_query,
        key_weight,
        value_weight,
        g_query,
        g_key,
        w_output,
        g_ffn,
        w_gate,
        w_up,
        w_down,
    ) = gathered
    head_width = g_query.shape[0]
    q_count = w_query.shape[1] // head_width
    key_value_count = key_weight.shape[1] // head_width
    tok_rows = x_block.shape[0]
    slot_index = lax.axis_index("seq") * tok_rows + jnp.arange(tok_rows, dtype=jnp.int32)
    is_valid = (slot_index < length_now)[:, None]
    cos_tab, sin_tab = rotary_tables(pos_block, head_width)
    x_float = x_block.astype(jnp.float32)
    normed, pull_attn = jax.vjp(rms_scale, x_float, g_attn.astype(jnp.float32))
    x_in = normed.astype(jnp.bfloat16)
    query_flat = product(x_in, w_query)
    key_flat = product(x_in, key_weight)
    query_rot, pull_query = jax.vjp(
        lambda flat_rows, gain_vec: head_norm_rope(flat_rows, gain_vec, cos_tab, sin_tab, q_count),
        query_flat,
        g_query.astype(jnp.float32),
    )
    key_rot, pull_key = jax.vjp(
        lambda flat_rows, gain_vec: head_norm_rope(
            flat_rows, gain_vec, cos_tab, sin_tab, key_value_count
        ),
        key_flat,
        g_key.astype(jnp.float32),
    )
    value_rows = (
        product(x_in, value_weight)
        .astype(jnp.bfloat16)
        .reshape(tok_rows, key_value_count, head_width)
    )
    query_heads, key_heads, value_heads = (
        lax.all_to_all(
            query_rot.astype(jnp.bfloat16), "seq", split_axis=1, concat_axis=0, tiled=True
        ),
        lax.all_to_all(
            key_rot.astype(jnp.bfloat16), "seq", split_axis=1, concat_axis=0, tiled=True
        ),
        lax.all_to_all(value_rows, "seq", split_axis=1, concat_axis=0, tiled=True),
    )
    attended_heads, log_sums = attend_forward(query_heads, key_heads, value_heads)
    context_rows = lax.all_to_all(
        attended_heads, "seq", split_axis=0, concat_axis=1, tiled=True
    ).reshape(tok_rows, q_count * head_width)
    residual = x_float + product(context_rows, w_output)
    mid_norm, pull_ffn = jax.vjp(rms_scale, residual, g_ffn.astype(jnp.float32))
    mid_in = mid_norm.astype(jnp.bfloat16)
    gate_proj = product(mid_in, w_gate)
    up_proj = product(mid_in, w_up)
    unit_out, pull_unit = jax.vjp(gated_unit, gate_proj, up_proj)
    unit_in = unit_out.astype(jnp.bfloat16)
    result = residual + product(unit_in, w_down)
    out_block = jnp.where(is_valid, result, 0.0).astype(jnp.bfloat16)
    d_result = jnp.where(is_valid, cot_block.astype(jnp.float32), 0.0)
    d_branch = d_result.astype(jnp.bfloat16)
    grad_down = cross_rows(unit_in, d_branch)
    d_unit = times_trans(d_branch, w_down)
    d_gate, d_up = pull_unit(d_unit)
    d_gate_low = d_gate.astype(jnp.bfloat16)
    d_up_low = d_up.astype(jnp.bfloat16)
    grad_gate = cross_rows(mid_in, d_gate_low)
    grad_up = cross_rows(mid_in, d_up_low)
    d_mid = times_trans(d_gate_low, w_gate) + times_trans(d_up_low, w_up)
    d_res_norm, grad_ffn_gain = pull_ffn(d_mid)
    d_residual = d_result + d_res_norm
    d_attn = d_residual.astype(jnp.bfloat16)
    grad_output = cross_rows(context_rows, d_attn)
    d_attended = (
        times_trans(d_attn, w_output).astype(jnp.bfloat16).reshape(tok_rows, q_count, head_width)
    )
    grad_heads = lax.all_to_all(d_attended, "seq", split_axis=1, concat_axis=0, tiled=True)
    dq_heads, dk_heads, dv_heads = attend_backward(
        query_heads, key_heads, value_heads, grad_heads, log_sums
    )
    dq_rows, dk_rows, dv_rows = (
        lax.all_to_all(dq_heads, "seq", split_axis=0, concat_axis=1, tiled=True),
        lax.all_to_all(dk_heads, "seq", split_axis=0, concat_axis=1, tiled=True),
        lax.all_to_all(dv_heads, "seq", split_axis=0, concat_axis=1, tiled=True),
    )
    d_query_flat, grad_query_gain = pull_query(dq_rows.astype(jnp.float32))
    d_key_flat, grad_key_gain = pull_key(dk_rows.astype(jnp.float32))
    d_query_low = d_query_flat.astype(jnp.bfloat16)
    d_key_low = d_key_flat.astype(jnp.bfloat16)
    d_value_low = dv_rows.reshape(tok_rows, key_value_count * head_width)
    grad_query = cross_rows(x_in, d_query_low)
    grad_key = cross_rows(x_in, d_key_low)
    grad_value = cross_rows(x_in, d_value_low)
    d_x_in = (
        times_trans(d_query_low, w_query)
        + times_trans(d_key_low, key_weight)
        + times_trans(d_value_low, value_weight)
    )
    d_x_norm, grad_attn_gain = pull_attn(d_x_in)
    d_input = d_residual + d_x_norm
    grads_now = (
        grad_attn_gain,
        grad_query,
        grad_key,
        grad_value,
        grad_query_gain,
        grad_key_gain,
        grad_output,
        grad_ffn_gain,
        grad_gate,
        grad_up,
        grad_down,
    )
    return (jax.tree.map(jnp.add, totals, grads_now), (out_block, d_input))


def per_device(
    hidden_in,
    out_cotangent,
    slot_lengths,
    position_ids,
    attn_gain,
    w_query,
    key_weight,
    value_weight,
    query_gain,
    key_gain,
    w_output,
    ffn_gain,
    w_gate,
    w_up,
    w_down,
):
    shards = (
        attn_gain,
        w_query,
        key_weight,
        value_weight,
        query_gain,
        key_gain,
        w_output,
        ffn_gain,
        w_gate,
        w_up,
        w_down,
    )
    dp_count = lax.axis_size("dp")
    zero_grads = tuple(
        (
            jnp.zeros((weight_shard.shape[0] * dp_count,) + weight_shard.shape[1:], jnp.float32)
            for weight_shard in shards
        )
    )

    def scan_turn(totals, slot_args):
        fresh = (
            lax.all_gather(shards[0], "dp", axis=0, tiled=True),
            lax.all_gather(shards[1], "dp", axis=0, tiled=True),
            lax.all_gather(shards[2], "dp", axis=0, tiled=True),
            lax.all_gather(shards[3], "dp", axis=0, tiled=True),
            lax.all_gather(shards[4], "dp", axis=0, tiled=True),
            lax.all_gather(shards[5], "dp", axis=0, tiled=True),
            lax.all_gather(shards[6], "dp", axis=0, tiled=True),
            lax.all_gather(shards[7], "dp", axis=0, tiled=True),
            lax.all_gather(shards[8], "dp", axis=0, tiled=True),
            lax.all_gather(shards[9], "dp", axis=0, tiled=True),
            lax.all_gather(shards[10], "dp", axis=0, tiled=True),
        )
        return micro_turn(fresh, totals, slot_args)

    summed, (out_blocks, input_grads) = lax.scan(
        scan_turn, zero_grads, (hidden_in, out_cotangent, slot_lengths, position_ids)
    )
    owned = jax.tree.map(
        lambda part: part.astype(jnp.float32),
        lax.psum_scatter(as_sent(summed), "dp", scatter_dimension=0, tiled=True),
    )
    owned = jax.tree.map(lambda part: part.astype(jnp.float32), lax.psum(as_sent(owned), "seq"))
    return (out_blocks, input_grads) + tuple(owned)


def solution(mesh):
    in_specs = (
        P("dp", "seq", None),
        P("dp", "seq", None),
        P("dp"),
        P("dp", "seq"),
        P("dp"),
        P("dp", None),
        P("dp", None),
        P("dp", None),
        P("dp"),
        P("dp"),
        P("dp", None),
        P("dp"),
        P("dp", None),
        P("dp", None),
        P("dp", None),
    )
    out_specs = (
        P("dp", "seq", None),
        P("dp", "seq", None),
        P("dp"),
        P("dp", None),
        P("dp", None),
        P("dp", None),
        P("dp"),
        P("dp"),
        P("dp", None),
        P("dp"),
        P("dp", None),
        P("dp", None),
        P("dp", None),
    )
    return jax.shard_map(
        per_device, mesh=mesh, in_specs=in_specs, out_specs=out_specs, check_vma=False
    )
```

profile of v0, /device:TPU:0, one launch (start us, length us, event | category | flops | bytes accessed | tf_op | source)
XLA Modules:
  0.0 1831.3 jit_solution(2463709311332314598)
XLA Ops:
  8.1 1105.8 %while.66 = (s32[]{:T(128)}, f32[1024]{0:T(1024)}, f32[1024,2048]{1,0:T(8,128)}, f32[1024,1024]{1,0:T(8,128)}, f32[1024,1024]{1,0:T(8,128)}, /*index=5*/f32[128]...) while((s32[]{:T(128)}, f32[1024]{0:T(1024)}, ...), condition=%wide.region_20.21_spmd.clone, body=%wide.region_0.20_spmd.clone.sunk | while | flops 14049545216 | bytes 651706624 | solution.py:336
  19.0 40.0 %all-reduce.21 = (bf16[1024]{0:T(1024)(128)(2,1)S(1)}, bf16[128]{0:T(256)(128)(2,1)S(1)}, bf16[128]{0:T(256)(128)(2,1)S(1)}, bf16[1024]{0:T(1024)(128)(2,1)S(1)}) all-reduce(bf16[1024]{0:T(1024)(128)(2,1)S(1)} %dynamic-update-slice.12, bf16[128]{0:T(256)(128)(2,1)S(1)} %dynamic-update-slice.13, ...), channel_id=1, replica_groups=mesh['dp'=16,'seq'=8] {'dp'}, use_global_device_ids=true, to_apply=%add.4 | all-reduce | flops 2304 | bytes 9216 | tf_op jit(solution)/shard_map/while
  71.5 47.9 %all-gather.8.cloned.1.call-done = bf16[1024,2048]{1,0:T(8,128)(2,1)} async-done(((bf16[64,2048]{1,0:T(8,128)(2,1)}), bf16[1024,2048]{1,0:T(8,128)(2,1)}) %all-gather.8.cloned.1.call-update) | async-done | bytes 4194320 | tf_op jit(solution)/shard_map/while/body/eval_jaxpr/all_gather | solution.py:323
  135.6 31.5 %all-gather.12.cloned.1.call-done = bf16[1024,1024]{1,0:T(8,128)(2,1)} async-done(((bf16[64,1024]{1,0:T(8,128)(2,1)}), bf16[1024,1024]{1,0:T(8,128)(2,1)}) %all-gather.12.cloned.1.call-update) | async-done | bytes 2097168 | tf_op jit(solution)/shard_map/while/body/eval_jaxpr/all_gather | solution.py:325
  229.4 61.4 %all-gather.18.cloned.1.call-done = bf16[3072,1024]{1,0:T(8,128)(2,1)} async-done(((bf16[192,1024]{1,0:T(8,128)(2,1)}), bf16[3072,1024]{1,0:T(8,128)(2,1)}) %all-gather.18.cloned.1.call-update) | async-done | bytes 6291472 | tf_op jit(solution)/shard_map/while/body/eval_jaxpr/all_gather | solution.py:332
  297.1 58.0 %all-gather.16.cloned.1.call-done = bf16[1024,3072]{1,0:T(8,128)(2,1)} async-done(((bf16[64,3072]{1,0:T(8,128)(2,1)}), bf16[1024,3072]{1,0:T(8,128)(2,1)}) %all-gather.16.cloned.1.call-update) | async-done | bytes 6291472 | tf_op jit(solution)/shard_map/while/body/eval_jaxpr/all_gather | solution.py:330
  360.1 59.5 %all-gather.20.cloned.1.call-done = bf16[1024,3072]{1,0:T(8,128)(2,1)} async-done(((bf16[64,3072]{1,0:T(8,128)(2,1)}), bf16[1024,3072]{1,0:T(8,128)(2,1)}) %all-gather.20.cloned.1.call-update) | async-done | bytes 6291472 | tf_op jit(solution)/shard_map/while/body/eval_jaxpr/all_gather | solution.py:331
  464.4 26.8 %while.68 = (s32[]{:T(128)}, f32[1024,1,128]{0,2,1:T(8,128)}, f32[1024,1,128]{0,2,1:T(8,128)}, bf16[2,512,1,2,128]{4,1,0,3,2:T(8,128)(2,1)}, bf16[2,512,1,2,128]...) while((s32[]{:T(128)}, f32[1024,1,128]{0,2,1:T(8,128)}, ...), condition=%wide.region_12.12_spmd.clone, body=%wide.region_10.11_spmd.clone.sunk | while | flops 1360133632 | bytes 77628752 | solution.py:149
  559.1 34.0 %all-reduce.21 = (bf16[1024]{0:T(1024)(128)(2,1)S(1)}, bf16[128]{0:T(256)(128)(2,1)S(1)}, bf16[128]{0:T(256)(128)(2,1)S(1)}, bf16[1024]{0:T(1024)(128)(2,1)S(1)}) all-reduce(bf16[1024]{0:T(1024)(128)(2,1)S(1)} %dynamic-update-slice.12, bf16[128]{0:T(256)(128)(2,1)S(1)} %dynamic-update-slice.13, ...), channel_id=1, replica_groups=mesh['dp'=16,'seq'=8] {'dp'}, use_global_device_ids=true, to_apply=%add.4 | all-reduce | flops 2304 | bytes 9216 | tf_op jit(solution)/shard_map/while
  608.1 47.8 %all-gather.8.cloned.1.call-done = bf16[1024,2048]{1,0:T(8,128)(2,1)} async-done(((bf16[64,2048]{1,0:T(8,128)(2,1)}), bf16[1024,2048]{1,0:T(8,128)(2,1)}) %all-gather.8.cloned.1.call-update) | async-done | bytes 4194320 | tf_op jit(solution)/shard_map/while/body/eval_jaxpr/all_gather | solution.py:323
  672.1 31.4 %all-gather.12.cloned.1.call-done = bf16[1024,1024]{1,0:T(8,128)(2,1)} async-done(((bf16[64,1024]{1,0:T(8,128)(2,1)}), bf16[1024,1024]{1,0:T(8,128)(2,1)}) %all-gather.12.cloned.1.call-update) | async-done | bytes 2097168 | tf_op jit(solution)/shard_map/while/body/eval_jaxpr/all_gather | solution.py:325
  765.4 61.4 %all-gather.18.cloned.1.call-done = bf16[3072,1024]{1,0:T(8,128)(2,1)} async-done(((bf16[192,1024]{1,0:T(8,128)(2,1)}), bf16[3072,1024]{1,0:T(8,128)(2,1)}) %all-gather.18.cloned.1.call-update) | async-done | bytes 6291472 | tf_op jit(solution)/shard_map/while/body/eval_jaxpr/all_gather | solution.py:332
  833.1 58.2 %all-gather.16.cloned.1.call-done = bf16[1024,3072]{1,0:T(8,128)(2,1)} async-done(((bf16[64,3072]{1,0:T(8,128)(2,1)}), bf16[1024,3072]{1,0:T(8,128)(2,1)}) %all-gather.16.cloned.1.call-update) | async-done | bytes 6291472 | tf_op jit(solution)/shard_map/while/body/eval_jaxpr/all_gather | solution.py:330
  896.3 59.3 %all-gather.20.cloned.1.call-done = bf16[1024,3072]{1,0:T(8,128)(2,1)} async-done(((bf16[64,3072]{1,0:T(8,128)(2,1)}), bf16[1024,3072]{1,0:T(8,128)(2,1)}) %all-gather.20.cloned.1.call-update) | async-done | bytes 6291472 | tf_op jit(solution)/shard_map/while/body/eval_jaxpr/all_gather | solution.py:331
  1017.7 26.8 %while.68 = (s32[]{:T(128)}, f32[1024,1,128]{0,2,1:T(8,128)}, f32[1024,1,128]{0,2,1:T(8,128)}, bf16[2,512,1,2,128]{4,1,0,3,2:T(8,128)(2,1)}, bf16[2,512,1,2,128]...) while((s32[]{:T(128)}, f32[1024,1,128]{0,2,1:T(8,128)}, ...), condition=%wide.region_12.12_spmd.clone, body=%wide.region_10.11_spmd.clone.sunk | while | flops 1360133632 | bytes 77628752 | solution.py:149
  1159.5 28.8 %reduce-scatter.10.cloned.1.call-done = bf16[64,1024]{1,0:T(8,128)(2,1)} async-done(((bf16[1024,1024]{1,0:T(8,128)(2,1)}), bf16[64,1024]{1,0:T(8,128)(2,1)}) %reduce-scatter.10.cloned.1.call-update) | async-done | bytes 131088 | tf_op jit(solution)/shard_map/reduce_scatter | solution.py:341
  1188.3 74.2 %reduce-scatter.12.cloned.1.call-done = bf16[64,1024]{1,0:T(8,128)(2,1)} async-done(((bf16[1024,1024]{1,0:T(8,128)(2,1)}), bf16[64,1024]{1,0:T(8,128)(2,1)}) %reduce-scatter.12.cloned.1.call-update) | async-done | bytes 131088 | tf_op jit(solution)/shard_map/reduce_scatter | solution.py:341
  1262.5 83.5 %reduce-scatter.14.cloned.1.call-done = bf16[128,1024]{1,0:T(8,128)(2,1)} async-done(((bf16[2048,1024]{1,0:T(8,128)(2,1)}), bf16[128,1024]{1,0:T(8,128)(2,1)}) %reduce-scatter.14.cloned.1.call-update) | async-done | bytes 262160 | tf_op jit(solution)/shard_map/reduce_scatter | solution.py:341
  1346.0 83.9 %reduce-scatter.8.cloned.1.call-done = bf16[64,2048]{1,0:T(8,128)(2,1)} async-done(((bf16[1024,2048]{1,0:T(8,128)(2,1)}), bf16[64,2048]{1,0:T(8,128)(2,1)}) %reduce-scatter.8.cloned.1.call-update) | async-done | bytes 262160 | tf_op jit(solution)/shard_map/reduce_scatter | solution.py:341
  1429.9 92.6 %reduce-scatter.16.cloned.1.call-done = bf16[64,3072]{1,0:T(8,128)(2,1)} async-done(((bf16[1024,3072]{1,0:T(8,128)(2,1)}), bf16[64,3072]{1,0:T(8,128)(2,1)}) %reduce-scatter.16.cloned.1.call-update) | async-done | bytes 393232 | tf_op jit(solution)/shard_map/reduce_scatter | solution.py:341
  1522.5 93.3 %reduce-scatter.18.cloned.1.call-done = bf16[64,3072]{1,0:T(8,128)(2,1)} async-done(((bf16[1024,3072]{1,0:T(8,128)(2,1)}), bf16[64,3072]{1,0:T(8,128)(2,1)}) %reduce-scatter.18.cloned.1.call-update) | async-done | bytes 393232 | tf_op jit(solution)/shard_map/reduce_scatter | solution.py:341
  1615.8 92.5 %reduce-scatter.20.cloned.1.call-done = bf16[192,1024]{1,0:T(8,128)(2,1)} async-done(((bf16[3072,1024]{1,0:T(8,128)(2,1)}), bf16[192,1024]{1,0:T(8,128)(2,1)}) %reduce-scatter.20.cloned.1.call-update) | async-done | bytes 393232 | tf_op jit(solution)/shard_map/reduce_scatter | solution.py:341
  1710.3 39.6 %all-reduce.17 = (bf16[1024]{0:T(1024)(128)(2,1)S(1)}, bf16[128]{0:T(256)(128)(2,1)S(1)}, bf16[128]{0:T(256)(128)(2,1)S(1)}, bf16[1024]{0:T(1024)(128)(2,1)S(1)}) all-reduce(bf16[1024]{0:T(1024)(128)(2,1)S(1)} %convert_element_type.251, bf16[128]{0:T(256)(128)(2,1)S(1)} %convert_element_type.259, ...), channel_id=2, replica_groups=mesh['dp'=16,'seq'=8] {'dp'}, use_global_device_ids=true, to_apply=%region_21.22.clone | all-reduce | flops 2304 | bytes 9216
  1771.2 42.9 %all-reduce.24.cloned.1.call-done = (bf16[64,2048]{1,0:T(8,128)(2,1)}, bf16[64,1024]{1,0:T(8,128)(2,1)}, bf16[64,1024]{1,0:T(8,128)(2,1)}, bf16[128,1024]{1,0:T(...) async-done(((bf16[64,2048]{1,0:T(8,128)(2,1)}, bf16[64,1024]{1,0:T(8,128)(2,1)}, bf16[64,1024]{1,0:T(8,128)(2,1)}, ...) | async-done | bytes 1966096 | tf_op jit(solution)/shard_map/psum | solution.py:343
  (703 shorter events, 604.3 us)
Async XLA Ops:
  8.4 53.5 %all-gather.10.cloned.1.call-start = ((), (), s32[]{:S(2)}) async-start(), calls=%async_computation.24 | async-start | bytes 2228224 | tf_op jit(solution)/shard_map/while/body/eval_jaxpr/all_gather | solution.py:324
  9.1 110.2 %all-gather.8.cloned.1.call-start = ((), (), s32[]{:S(2)}) async-start(), calls=%async_computation.23 | async-start | bytes 4456448 | tf_op jit(solution)/shard_map/while/body/eval_jaxpr/all_gather | solution.py:323
  9.9 157.3 %all-gather.12.cloned.1.call-start = ((), (), s32[]{:S(2)}) async-start(), calls=%async_computation.25 | async-start | bytes 2228224 | tf_op jit(solution)/shard_map/while/body/eval_jaxpr/all_gather | solution.py:325
  10.6 215.6 %all-gather.14.cloned.1.call-start = ((), (), s32[]{:S(2)}) async-start(), calls=%async_computation.26 | async-start | bytes 4456448 | tf_op jit(solution)/shard_map/while/body/eval_jaxpr/all_gather | solution.py:328
  11.2 279.7 %all-gather.18.cloned.1.call-start = ((), (), s32[]{:S(2)}) async-start(), calls=%async_computation.28 | async-start | bytes 6684672 | tf_op jit(solution)/shard_map/while/body/eval_jaxpr/all_gather | solution.py:332
  11.8 343.4 %all-gather.16.cloned.1.call-start = ((), (), s32[]{:S(2)}) async-start(), calls=%async_computation.27 | async-start | bytes 6684672 | tf_op jit(solution)/shard_map/while/body/eval_jaxpr/all_gather | solution.py:330
  12.3 407.2 %all-gather.20.cloned.1.call-start = ((), (), s32[]{:S(2)}) async-start(), calls=%async_computation.29 | async-start | bytes 6684672 | tf_op jit(solution)/shard_map/while/body/eval_jaxpr/all_gather | solution.py:331
  67.2 64.2 %all-to-all-start.1 = ((bf16[128,8,128]{0,2,1:T(8,128)(2,1)}), bf16[128,8,128]{0,2,1:T(8,128)(2,1)S(1)}, u32[]{:S(2)}, u32[]{:S(2)}) async-start(bf16[128,8,128]{0,2,1:T(8,128)(2,1)} %fusion.304), calls=%async_computation.1 | async-start | bytes 524288 | tf_op jit(solution)/shard_map/while/body/eval_jaxpr/all_to_all | solution.py:207
  548.4 50.0 %all-gather.10.cloned.1.call-start = ((), (), s32[]{:S(2)}) async-start(), calls=%async_computation.24 | async-start | bytes 2228224 | tf_op jit(solution)/shard_map/while/body/eval_jaxpr/all_gather | solution.py:324
  549.2 106.7 %all-gather.8.cloned.1.call-start = ((), (), s32[]{:S(2)}) async-start(), calls=%async_computation.23 | async-start | bytes 4456448 | tf_op jit(solution)/shard_map/while/body/eval_jaxpr/all_gather | solution.py:323
  549.9 153.6 %all-gather.12.cloned.1.call-start = ((), (), s32[]{:S(2)}) async-start(), calls=%async_computation.25 | async-start | bytes 2228224 | tf_op jit(solution)/shard_map/while/body/eval_jaxpr/all_gather | solution.py:325
  550.5 211.8 %all-gather.14.cloned.1.call-start = ((), (), s32[]{:S(2)}) async-start(), calls=%async_computation.26 | async-start | bytes 4456448 | tf_op jit(solution)/shard_map/while/body/eval_jaxpr/all_gather | solution.py:328
  551.2 275.6 %all-gather.18.cloned.1.call-start = ((), (), s32[]{:S(2)}) async-start(), calls=%async_computation.28 | async-start | bytes 6684672 | tf_op jit(solution)/shard_map/while/body/eval_jaxpr/all_gather | solution.py:332
  551.8 339.5 %all-gather.16.cloned.1.call-start = ((), (), s32[]{:S(2)}) async-start(), calls=%async_computation.27 | async-start | bytes 6684672 | tf_op jit(solution)/shard_map/while/body/eval_jaxpr/all_gather | solution.py:330
  552.5 403.0 %all-gather.20.cloned.1.call-start = ((), (), s32[]{:S(2)}) async-start(), calls=%async_computation.29 | async-start | bytes 6684672 | tf_op jit(solution)/shard_map/while/body/eval_jaxpr/all_gather | solution.py:331
  603.8 64.1 %all-to-all-start.1 = ((bf16[128,8,128]{0,2,1:T(8,128)(2,1)}), bf16[128,8,128]{0,2,1:T(8,128)(2,1)S(1)}, u32[]{:S(2)}, u32[]{:S(2)}) async-start(bf16[128,8,128]{0,2,1:T(8,128)(2,1)} %fusion.304), calls=%async_computation.1 | async-start | bytes 524288 | tf_op jit(solution)/shard_map/while/body/eval_jaxpr/all_to_all | solution.py:207
  1114.0 74.3 %reduce-scatter.10.cloned.1.call-start = ((), (), s32[]{:S(2)}) async-start(), calls=%async_computation.16 | async-start | bytes 2228224 | tf_op jit(solution)/shard_map/reduce_scatter | solution.py:341
  1117.9 144.6 %reduce-scatter.12.cloned.1.call-start = ((), (), s32[]{:S(2)}) async-start(), calls=%async_computation.17 | async-start | bytes 2228224 | tf_op jit(solution)/shard_map/reduce_scatter | solution.py:341
  1121.9 224.2 %reduce-scatter.14.cloned.1.call-start = ((), (), s32[]{:S(2)}) async-start(), calls=%async_computation.18 | async-start | bytes 4456448 | tf_op jit(solution)/shard_map/reduce_scatter | solution.py:341
  1128.0 302.0 %reduce-scatter.8.cloned.1.call-start = ((), (), s32[]{:S(2)}) async-start(), calls=%async_computation.15 | async-start | bytes 4456448 | tf_op jit(solution)/shard_map/reduce_scatter | solution.py:341
  1134.2 388.3 %reduce-scatter.16.cloned.1.call-start = ((), (), s32[]{:S(2)}) async-start(), calls=%async_computation.19 | async-start | bytes 6684672 | tf_op jit(solution)/shard_map/reduce_scatter | solution.py:341
  1142.8 473.0 %reduce-scatter.18.cloned.1.call-start = ((), (), s32[]{:S(2)}) async-start(), calls=%async_computation.20 | async-start | bytes 6684672 | tf_op jit(solution)/shard_map/reduce_scatter | solution.py:341
  1151.1 557.2 %reduce-scatter.20.cloned.1.call-start = ((), (), s32[]{:S(2)}) async-start(), calls=%async_computation.21 | async-start | bytes 6684672 | tf_op jit(solution)/shard_map/reduce_scatter | solution.py:341
  1159.5 654.6 %all-reduce.24.cloned.1.call-start = ((), (), s32[]{:S(2)}) async-start(), calls=%async_computation.22 | async-start | bytes 3932160 | tf_op jit(solution)/shard_map/psum | solution.py:343
  (164 other events, 5374.3 us)
Sparse Core Ops, SparseCore 0:
  11.7 50.1 all-gather.9
  64.3 54.9 all-gather.7
  121.8 45.2 all-gather.11
  169.5 56.7 all-gather.13
  228.6 62.2 all-gather.17
  293.2 61.9 all-gather.15
  357.6 61.9 all-gather.19
  551.7 46.6 all-gather.9
  600.9 54.8 all-gather.7
  658.2 45.2 all-gather.11
  706.0 56.2 all-gather.13
  764.6 62.2 all-gather.17
  829.3 61.9 all-gather.15
  893.6 61.9 all-gather.19
Sparse Core Ops, SparseCore 1:
  1118.3 69.9 reduce-scatter.9
  1192.6 69.9 reduce-scatter.11
  1266.4 79.6 reduce-scatter.13
  1350.6 79.3 reduce-scatter.7
  1434.1 88.3 reduce-scatter.15
  1527.3 88.4 reduce-scatter.17
  1619.8 88.4 reduce-scatter.19
  1711.6 102.4 all-reduce.23
where the time goes:
time: 1840 us; the launch traced here: 1830 us
  waiting for transfers between devices  1200 us (65%)
  matrix products  228 us (12%)
  blocking collectives  132 us (7%)
  other arithmetic  99.7 us (5%)
  starting transfers between devices  74.1 us (4%)
  local copies, waits for them, and re-layouts  70.4 us (4%)
    reduce_scatter x7, waiting for transfers between devices, per_device(): lax.psum_scatter(as_sent(summed), 'dp', scatter_dimension=0, tiled=True)  549 us
    all_gather x2, waiting for transfers between devices, scan_turn(): lax.all_gather(shards[10], 'dp', axis=0, tiled=True)  123 us
    all_gather x2, waiting for transfers between devices, scan_turn(): lax.all_gather(shards[9], 'dp', axis=0, tiled=True)  119 us
    all_gather x2, waiting for transfers between devices, scan_turn(): lax.all_gather(shards[8], 'dp', axis=0, tiled=True)  116 us
    all_gather x2, waiting for transfers between devices, scan_turn(): lax.all_gather(shards[1], 'dp', axis=0, tiled=True)  95.6 us
    dot_general x14, matrix products, cross_rows(): lax.dot_general(left, right, (((0,), (0,)), ((), ())), preferred_element_...  93.7 us
    while x2, blocking collectives  74 us
    all_gather x2, waiting for transfers between devices, scan_turn(): lax.all_gather(shards[3], 'dp', axis=0, tiled=True)  62.9 us
  transfers between devices with their start and end apart: 38, of which 28 were waited for; matrix products, arithmetic and copies ran while one was open for 14% of the time, Pallas kernels for 0%

commit v1 on v0

v1 whole, which is shorter than its diff:
```python
import math

import jax
import jax.numpy as jnp
from jax import lax
from jax.sharding import PartitionSpec as P

epsilon = 1e-06
rope_base = 1000000.0
bf16 = jnp.bfloat16
f32 = jnp.float32


def product(left, right):
    return jnp.dot(left, right, preferred_element_type=f32)


def cross_rows(left, right):
    return lax.dot_general(left, right, (((0,), (0,)), ((), ())), preferred_element_type=f32)


def times_trans(left, right):
    return lax.dot_general(left, right, (((1,), (1,)), ((), ())), preferred_element_type=f32)


def rotary_tables(positions, width):
    half = width // 2
    frequency = jnp.exp(jnp.arange(half, dtype=f32) * (-2.0 * math.log(rope_base) / width))
    angles = positions.astype(f32)[:, None] * frequency[None, :]
    cos_half, sin_half = jnp.cos(angles), jnp.sin(angles)
    return (
        jnp.concatenate([cos_half, cos_half], axis=-1),
        jnp.concatenate([sin_half, sin_half], axis=-1),
    )


def turn(v):
    half = v.shape[-1] // 2
    return jnp.concatenate([-v[..., half:], v[..., :half]], axis=-1)


def turn_back(v):
    half = v.shape[-1] // 2
    return jnp.concatenate([v[..., half:], -v[..., :half]], axis=-1)


def inverse_rms(v):
    return lax.rsqrt(jnp.mean(v * v, axis=-1, keepdims=True) + epsilon)


def rms_back(v, gain, grad):
    r = inverse_rms(v)
    ge = gain * grad
    dv = r * ge - v * (r * r * r) * jnp.mean(v * ge, axis=-1, keepdims=True)
    return dv, grad * v * r


def attend_forward(q, k, v):
    rows, heads, width = q.shape
    kv = k.shape[1]
    q = q.reshape(rows, kv, heads // kv, width)
    scores = jnp.einsum("qkgd,skd->kgqs", q, k, preferred_element_type=f32) * width ** (-0.5)
    order = jnp.arange(rows, dtype=jnp.int32)
    scores = jnp.where(order[None, :] <= order[:, None], scores, -1e30)
    top = jnp.max(scores, axis=-1, keepdims=True)
    shifted = jnp.exp(scores - top)
    total = jnp.sum(shifted, axis=-1, keepdims=True)
    prob = (shifted / total).astype(bf16)
    out = jnp.einsum("kgqs,skd->qkgd", prob, v, preferred_element_type=f32)
    return out.astype(bf16).reshape(rows, heads, width), top + jnp.log(total)


def attend_backward(q, k, v, grad, lse):
    rows, heads, width = q.shape
    kv = k.shape[1]
    scale = width ** (-0.5)
    q = q.reshape(rows, kv, heads // kv, width)
    grad = grad.reshape(rows, kv, heads // kv, width)
    scores = jnp.einsum("qkgd,skd->kgqs", q, k, preferred_element_type=f32) * scale
    order = jnp.arange(rows, dtype=jnp.int32)
    scores = jnp.where(order[None, :] <= order[:, None], scores, -1e30)
    prob = jnp.exp(scores - lse)
    d_prob = jnp.einsum("qkgd,skd->kgqs", grad, v, preferred_element_type=f32)
    row_dot = jnp.sum(prob * d_prob, axis=-1, keepdims=True)
    d_score = (prob * (d_prob - row_dot) * scale).astype(bf16)
    dq = jnp.einsum("kgqs,skd->qkgd", d_score, k, preferred_element_type=f32)
    dk = jnp.einsum("kgqs,qkgd->skd", d_score, q, preferred_element_type=f32)
    dv = jnp.einsum("kgqs,qkgd->skd", prob.astype(bf16), grad, preferred_element_type=f32)
    return dq.astype(bf16).reshape(rows, heads, width), dk.astype(bf16), dv.astype(bf16)


def to_heads(rows_in, slots):
    parts = rows_in.reshape(slots, -1, rows_in.shape[1] // 128, 128)
    return lax.all_to_all(parts, "seq", split_axis=2, concat_axis=1, tiled=True)


def to_rows(heads_in):
    out = lax.all_to_all(heads_in, "seq", split_axis=1, concat_axis=2, tiled=True)
    return out.reshape(out.shape[0] * out.shape[1], -1)


def layer(hidden, cotangent, lengths, positions, gains, weights):
    g_attn, g_query, g_key, g_ffn = [g.astype(f32) for g in gains]
    w_query, w_key, w_value, w_output, w_gate, w_up, w_down = weights
    slots, tokens, width = hidden.shape
    rows = slots * tokens
    head = g_query.shape[0]
    hq, hkv = w_query.shape[1] // head, w_key.shape[1] // head
    index = lax.axis_index("seq") * tokens + jnp.arange(tokens, dtype=jnp.int32)
    valid = (index[None, :] < lengths[:, None]).reshape(rows, 1)
    cos, sin = rotary_tables(positions.reshape(rows), head)
    cos, sin = cos[:, None, :], sin[:, None, :]
    x = hidden.reshape(rows, width).astype(f32)
    x_in = (x * inverse_rms(x) * g_attn).astype(bf16)
    q_flat = product(x_in, w_query).reshape(rows, hq, head)
    k_flat = product(x_in, w_key).reshape(rows, hkv, head)
    v_rows = product(x_in, w_value).astype(bf16)

    def rope(v):
        return v * cos + turn(v) * sin

    q_rows = rope(q_flat * inverse_rms(q_flat) * g_query).astype(bf16).reshape(rows, -1)
    k_rows = rope(k_flat * inverse_rms(k_flat) * g_key).astype(bf16).reshape(rows, -1)
    q, k, v = to_heads(q_rows, slots), to_heads(k_rows, slots), to_heads(v_rows, slots)
    attended, lse = zip(*[attend_forward(q[i], k[i], v[i]) for i in range(slots)])
    context = to_rows(jnp.stack(attended))
    residual = x + product(context, w_output)
    mid_in = (residual * inverse_rms(residual) * g_ffn).astype(bf16)
    gate, up = product(mid_in, w_gate), product(mid_in, w_up)
    sig = 1.0 / (1.0 + jnp.exp(-gate))
    silu = gate * sig
    unit = (silu * up).astype(bf16)
    result = residual + product(unit, w_down)
    out = jnp.where(valid, result, 0.0).astype(bf16)
    d_result = jnp.where(valid, cotangent.reshape(rows, width).astype(f32), 0.0)
    d_branch = d_result.astype(bf16)
    grad_down = cross_rows(unit, d_branch)
    d_unit = times_trans(d_branch, w_down)
    d_gate = (d_unit * up * sig * (1.0 + gate * (1.0 - sig))).astype(bf16)
    d_up = (d_unit * silu).astype(bf16)
    grad_gate, grad_up = cross_rows(mid_in, d_gate), cross_rows(mid_in, d_up)
    d_mid = times_trans(d_gate, w_gate) + times_trans(d_up, w_up)
    dv_mid, dg_ffn = rms_back(residual, g_ffn, d_mid)
    d_residual = d_result + dv_mid
    d_attn = d_residual.astype(bf16)
    grad_output = cross_rows(context, d_attn)
    d_attended = times_trans(d_attn, w_output).astype(bf16)
    grad_heads = to_heads(d_attended, slots)
    back = [attend_backward(q[i], k[i], v[i], grad_heads[i], lse[i]) for i in range(slots)]
    dq, dk, dv = [to_rows(jnp.stack(part)) for part in zip(*back)]

    def head_back(flat, gain, grad):
        grad = grad.reshape(flat.shape).astype(f32)
        grad = grad * cos + turn_back(grad * sin)
        d_flat, dg = rms_back(flat, gain, grad)
        return d_flat.astype(bf16).reshape(rows, -1), jnp.sum(dg, axis=(0, 1))

    d_query, dg_query = head_back(q_flat, g_query, dq)
    d_key, dg_key = head_back(k_flat, g_key, dk)
    grad_query, grad_key, grad_value = (
        cross_rows(x_in, d_query),
        cross_rows(x_in, d_key),
        cross_rows(x_in, dv),
    )
    d_x_in = (
        times_trans(d_query, w_query) + times_trans(d_key, w_key) + times_trans(dv, w_value)
    )
    dv_x, dg_attn = rms_back(x, g_attn, d_x_in)
    d_input = d_residual + dv_x
    gain_grads = (jnp.sum(dg_attn, axis=0), dg_query, dg_key, jnp.sum(dg_ffn, axis=0))
    weight_grads = (
        grad_query,
        grad_key,
        grad_value,
        grad_output,
        grad_gate,
        grad_up,
        grad_down,
    )
    shape = (slots, tokens, width)
    return out.reshape(shape), d_input.reshape(shape), gain_grads, weight_grads


def per_device(
    hidden_in,
    out_cotangent,
    slot_lengths,
    position_ids,
    attn_gain,
    w_query,
    key_weight,
    value_weight,
    query_gain,
    key_gain,
    w_output,
    ffn_gain,
    w_gate,
    w_up,
    w_down,
):
    def gather(shard):
        return lax.all_gather(shard, "dp", axis=0, tiled=True)

    gains = [gather(g) for g in (attn_gain, query_gain, key_gain, ffn_gain)]
    shards = (w_query, key_weight, value_weight, w_output, w_gate, w_up, w_down)
    weights = [gather(w) for w in shards]
    out, d_input, gain_grads, weight_grads = layer(
        hidden_in, out_cotangent, slot_lengths, position_ids, gains, weights
    )

    def owned(part):
        part = lax.psum_scatter(part.astype(bf16), "dp", scatter_dimension=0, tiled=True)
        return lax.psum(part, "seq").astype(f32)

    dg_attn, dg_query, dg_key, dg_ffn = [owned(g) for g in gain_grads]
    gq, gk, gv, go, gg, gu, gd = [owned(g) for g in weight_grads]
    return (out, d_input, dg_attn, gq, gk, gv, dg_query, dg_key, go, dg_ffn, gg, gu, gd)


def solution(mesh):
    slots, rows, vector, matrix = P("dp", "seq", None), P("dp", "seq"), P("dp"), P("dp", None)
    in_specs = (
        slots,
        slots,
        vector,
        rows,
        vector,
        matrix,
        matrix,
        matrix,
        vector,
        vector,
        matrix,
        vector,
        matrix,
        matrix,
        matrix,
    )
    out_specs = (
        slots,
        slots,
        vector,
        matrix,
        matrix,
        matrix,
        vector,
        vector,
        matrix,
        vector,
        matrix,
        matrix,
        matrix,
    )
    return jax.shard_map(
        per_device, mesh=mesh, in_specs=in_specs, out_specs=out_specs, check_vma=False
    )
```

time: 1840 us -> 1250 us (0.68)
  waiting for transfers between devices: 1200 us -> 811 us
  matrix products: 228 us -> 118 us
  starting transfers between devices: 74.1 us -> 26.7 us
  other arithmetic: 99.7 us -> 57.8 us
    all_gather x14 -> x7, waiting for transfers between devices: 556 us -> 241 us  [gather(): return lax.all_gather(shard, 'dp', axis=0, tiled=True)]
    while x2 -> x0, blocking collectives: 74 us -> none
    dot_general x14 -> x7, matrix products: 93.7 us -> 27.1 us  [cross_rows(): lax.dot_general(left, right, (((0,), (0,)), ((), ())), preferred_element_...]
    reduce_scatter x7, waiting for transfers between devices: 549 us -> 493 us  [owned(): lax.psum_scatter(part.astype(bf16), 'dp', scatter_dimension=0, tiled=True)]
    convert_element_type x52 -> x24, other arithmetic: 73 us -> 22.8 us  [the longest x11 13.7 us: owned(): return lax.psum(part, 'seq').astype(f32)]
    all_to_all x16 -> x6, starting transfers between devices: 73.2 us -> 25.8 us  [the longest x4 17.4 us: to_heads(): return lax.all_to_all(parts, 'seq', split_axis=2, concat_axis=1, tiled=True)]
    unnamed x1 -> x2, blocking collectives: 39.6 us -> 79.7 us
    all_to_all x0 -> x2, blocking collectives: none -> 31.8 us  [to_rows(): lax.all_to_all(heads_in, 'seq', split_axis=1, concat_axis=2, tiled=True)]
  transfers between devices with their start and end apart: 38 -> 21, of which waited for: 28 -> 16; matrix products, arithmetic and copies ran while one was open for 14% -> 15% of each run, Pallas kernels for 0% -> 0%
where the time goes in v1:
time: 1250 us; the launch traced here: 1240 us
  waiting for transfers between devices  811 us (65%)
  blocking collectives  132 us (11%)
  matrix products  118 us (9%)
  local copies, waits for them, and re-layouts  78.8 us (6%)
  other arithmetic  57.8 us (5%)
  starting transfers between devices  26.7 us (2%)
  between operations  18.1 us (1%)
    reduce_scatter x7, waiting for transfers between devices, owned(): lax.psum_scatter(part.astype(bf16), 'dp', scatter_dimension=0, tiled=True)  493 us
    all_gather x7, waiting for transfers between devices, gather(): return lax.all_gather(shard, 'dp', axis=0, tiled=True)  241 us
    unnamed x2, blocking collectives  79.7 us
    all_to_all x2, blocking collectives, to_rows(): lax.all_to_all(heads_in, 'seq', split_axis=1, concat_axis=2, tiled=True)  31.8 us
    dot_general x7, matrix products, product(): return jnp.dot(left, right, preferred_element_type=f32)  31.2 us
    psum x1, waiting for transfers between devices, owned(): return lax.psum(part, 'seq').astype(f32)  31.1 us
    all_to_all x4, waiting for transfers between devices, to_heads(): return lax.all_to_all(parts, 'seq', split_axis=2, concat_axis=1, tiled=True)  28 us
    dot_general x7, matrix products, cross_rows(): lax.dot_general(left, right, (((0,), (0,)), ((), ())), preferred_element_...  27.1 us
  transfers between devices with their start and end apart: 21, of which 16 were waited for; matrix products, arithmetic and copies ran while one was open for 15% of the time, Pallas kernels for 0%

profile of v1, /device:TPU:0, one launch (start us, length us, event | category | flops | bytes accessed | tf_op | source)
XLA Modules:
  0.0 1242.2 jit_solution(2346554819604630759)
XLA Ops:
  19.9 40.1 %all-reduce.9 = (bf16[1024]{0:T(1024)(128)(2,1)S(1)}, bf16[128]{0:T(256)(128)(2,1)S(1)}, bf16[128]{0:T(256)(128)(2,1)S(1)}, bf16[1024]{0:T(1024)(128)(2,1)S(1)}) all-reduce(bf16[1024]{0:T(1024)(128)(2,1)S(1)} %dynamic-update-slice, bf16[128]{0:T(256)(128)(2,1)S(1)} %dynamic-update-slice.1, ...), channel_id=1, replica_groups=mesh['dp'=16,'seq'=8] {'dp'}, use_global_device_ids=true, to_apply=%add | all-reduce | flops 2304 | bytes 9216
  70.8 40.7 %all-gather.10.cloned.1.call-done = bf16[1024,1024]{1,0:T(8,128)(2,1)} async-done(((bf16[64,1024]{1,0:T(8,128)(2,1)}), bf16[1024,1024]{1,0:T(8,128)(2,1)}) %all-gather.10.cloned.1.call-update) | async-done | bytes 2097168 | tf_op jit(solution)/shard_map/all_gather | solution.py:202
  119.3 48.8 %all-gather.12.cloned.1.call-done = bf16[1024,2048]{1,0:T(8,128)(2,1)} async-done(((bf16[64,2048]{1,0:T(8,128)(2,1)}), bf16[1024,2048]{1,0:T(8,128)(2,1)}) %all-gather.12.cloned.1.call-update) | async-done | bytes 4194320 | tf_op jit(solution)/shard_map/all_gather | solution.py:202
  243.9 14.1 %all-to-all-done.3 = bf16[2,1024,2,128]{3,2,0,1:T(2,128)(2,1)} async-done(((bf16[2,1024,2,128]{3,2,0,1:T(2,128)(2,1)}), bf16[2,1024,2,128]{3,2,0,1:T(2,128)(2,1)}, u32[]{:S(2)}, u32[]{:S(2)}) %all-to-all-start.3) | async-done | bytes 1048608 | tf_op jit(solution)/shard_map/all_to_all | solution.py:98
  269.9 35.3 %all-gather.18.cloned.1.call-done = bf16[1024,3072]{1,0:T(8,128)(2,1)} async-done(((bf16[64,3072]{1,0:T(8,128)(2,1)}), bf16[1024,3072]{1,0:T(8,128)(2,1)}) %all-gather.18.cloned.1.call-update) | async-done | bytes 6291472 | tf_op jit(solution)/shard_map/all_gather | solution.py:202
  311.6 57.9 %all-gather.16.cloned.1.call-done = bf16[1024,3072]{1,0:T(8,128)(2,1)} async-done(((bf16[64,3072]{1,0:T(8,128)(2,1)}), bf16[1024,3072]{1,0:T(8,128)(2,1)}) %all-gather.16.cloned.1.call-update) | async-done | bytes 6291472 | tf_op jit(solution)/shard_map/all_gather | solution.py:202
  375.9 58.0 %all-gather.20.cloned.1.call-done = bf16[3072,1024]{1,0:T(8,128)(2,1)} async-done(((bf16[192,1024]{1,0:T(8,128)(2,1)}), bf16[3072,1024]{1,0:T(8,128)(2,1)}) %all-gather.20.cloned.1.call-update) | async-done | bytes 6291472 | tf_op jit(solution)/shard_map/all_gather | solution.py:202
  433.9 8.9 multiply_convert_fusion
  457.8 17.3 %all-to-all-done.4 = bf16[2,128,16,128]{3,1,0,2:T(8,128)(2,1)} async-done(((bf16[2,128,16,128]{3,1,0,2:T(8,128)(2,1)}), bf16[2,128,16,128]{3,1,0,2:T(8,128)(2,1)}, u32[]{:S(2)}, u32[]{:S(2)}) %all-to-all-start.4) | async-done | bytes 1048608 | tf_op jit(solution)/shard_map/all_to_all | solution.py:94
  481.7 8.3 fusion.4
  498.8 8.8 fusion.18
  507.6 8.1 fusion
  521.3 7.4 fusion.19
  534.7 14.6 %all_to_all.108 = bf16[2,1024,1,128]{3,0,2,1:T(2,128)(2,1)} all-to-all(bf16[2,1024,1,128]{3,0,2,1:T(2,128)(2,1)} %copy.177), channel_id=1, replica_groups=mesh['dp'=16,'seq'=8] {'seq'}, dimensions={1} | all-to-all | bytes 1048576 | tf_op jit(solution)/shard_map/all_to_all | solution.py:98
  572.9 17.2 %all_to_all.109 = bf16[2,1024,2,128]{3,2,0,1:T(2,128)(2,1)S(1)} all-to-all(bf16[2,1024,2,128]{3,2,0,1:T(2,128)(2,1)} %copy.171), channel_id=1, replica_groups=mesh['dp'=16,'seq'=8] {'seq'}, dimensions={1} | all-to-all | bytes 2097152 | tf_op jit(solution)/shard_map/all_to_all | solution.py:98
  625.1 46.5 %reduce-scatter.10.cloned.1.call-done = bf16[64,1024]{1,0:T(8,128)(2,1)} async-done(((bf16[1024,1024]{1,0:T(8,128)(2,1)}), bf16[64,1024]{1,0:T(8,128)(2,1)}) %reduce-scatter.10.cloned.1.call-update) | async-done | bytes 131088 | tf_op jit(solution)/shard_map/reduce_scatter | solution.py:212
  671.6 83.5 %reduce-scatter.14.cloned.1.call-done = bf16[128,1024]{1,0:T(8,128)(2,1)} async-done(((bf16[2048,1024]{1,0:T(8,128)(2,1)}), bf16[128,1024]{1,0:T(8,128)(2,1)}) %reduce-scatter.14.cloned.1.call-update) | async-done | bytes 262160 | tf_op jit(solution)/shard_map/reduce_scatter | solution.py:212
  755.1 84.0 %reduce-scatter.8.cloned.1.call-done = bf16[64,2048]{1,0:T(8,128)(2,1)} async-done(((bf16[1024,2048]{1,0:T(8,128)(2,1)}), bf16[64,2048]{1,0:T(8,128)(2,1)}) %reduce-scatter.8.cloned.1.call-update) | async-done | bytes 262160 | tf_op jit(solution)/shard_map/reduce_scatter | solution.py:212
  839.1 92.7 %reduce-scatter.18.cloned.1.call-done = bf16[64,3072]{1,0:T(8,128)(2,1)} async-done(((bf16[1024,3072]{1,0:T(8,128)(2,1)}), bf16[64,3072]{1,0:T(8,128)(2,1)}) %reduce-scatter.18.cloned.1.call-update) | async-done | bytes 393232 | tf_op jit(solution)/shard_map/reduce_scatter | solution.py:212
  931.8 93.3 %reduce-scatter.16.cloned.1.call-done = bf16[64,3072]{1,0:T(8,128)(2,1)} async-done(((bf16[1024,3072]{1,0:T(8,128)(2,1)}), bf16[64,3072]{1,0:T(8,128)(2,1)}) %reduce-scatter.16.cloned.1.call-update) | async-done | bytes 393232 | tf_op jit(solution)/shard_map/reduce_scatter | solution.py:212
  1025.1 92.6 %reduce-scatter.20.cloned.1.call-done = bf16[192,1024]{1,0:T(8,128)(2,1)} async-done(((bf16[3072,1024]{1,0:T(8,128)(2,1)}), bf16[192,1024]{1,0:T(8,128)(2,1)}) %reduce-scatter.20.cloned.1.call-update) | async-done | bytes 393232 | tf_op jit(solution)/shard_map/reduce_scatter | solution.py:212
  1128.4 39.6 %all-reduce.8 = (bf16[1024]{0:T(1024)(128)(2,1)S(1)}, bf16[128]{0:T(256)(128)(2,1)S(1)}, bf16[128]{0:T(256)(128)(2,1)S(1)}, bf16[1024]{0:T(1024)(128)(2,1)S(1)}) all-reduce(bf16[1024]{0:T(1024)(128)(2,1)S(1)} %get-tuple-element.19, bf16[128]{0:T(256)(128)(2,1)S(1)} %get-tuple-element.13, ...), channel_id=2, replica_groups=mesh['dp'=16,'seq'=8] {'dp'}, use_global_device_ids=true, to_apply=%region_15.16.clone | all-reduce | flops 2304 | bytes 9216
  1168.4 20.6 %all-reduce.10 = (bf16[64]{0:T(256)(128)(2,1)S(1)}, bf16[8]{0:T(256)(128)(2,1)S(1)}, bf16[8]{0:T(256)(128)(2,1)S(1)}, bf16[64]{0:T(256)(128)(2,1)S(1)}) all-reduce(bf16[64]{0:T(256)(128)(2,1)S(1)} %dynamic-slice.5, bf16[8]{0:T(256)(128)(2,1)S(1)} %dynamic-slice.7, ...), channel_id=1, replica_groups=mesh['dp'=16,'seq'=8] {'seq'}, use_global_device_ids=true, to_apply=%region_16.17 | all-reduce | flops 144 | bytes 576 | tf_op jit(solution)/shard_map/psum | solution.py:213
  1192.4 31.1 %all-reduce.14.cloned.1.call-done = (bf16[64,2048]{1,0:T(8,128)(2,1)}, bf16[64,1024]{1,0:T(8,128)(2,1)}, bf16[64,1024]{1,0:T(8,128)(2,1)}, bf16[128,1024]{1,0:T(...) async-done(((bf16[64,2048]{1,0:T(8,128)(2,1)}, bf16[64,1024]{1,0:T(8,128)(2,1)}, bf16[64,1024]{1,0:T(8,128)(2,1)}, ...) | async-done | bytes 1966096 | tf_op jit(solution)/shard_map/psum | solution.py:213
  (289 shorter events, 254.5 us)
Async XLA Ops:
  7.2 55.9 %all-gather.8.cloned.1.call-start = ((), (), s32[]{:S(2)}) async-start(), calls=%async_computation.15 | async-start | bytes 2228224 | tf_op jit(solution)/shard_map/all_gather | solution.py:202
  7.9 103.5 %all-gather.10.cloned.1.call-start = ((), (), s32[]{:S(2)}) async-start(), calls=%async_computation.16 | async-start | bytes 2228224 | tf_op jit(solution)/shard_map/all_gather | solution.py:202
  8.7 159.4 %all-gather.12.cloned.1.call-start = ((), (), s32[]{:S(2)}) async-start(), calls=%async_computation.17 | async-start | bytes 4456448 | tf_op jit(solution)/shard_map/all_gather | solution.py:202
  9.4 254.6 %all-gather.14.cloned.1.call-start = ((), (), s32[]{:S(2)}) async-start(), calls=%async_computation.18 | async-start | bytes 4456448 | tf_op jit(solution)/shard_map/all_gather | solution.py:202
  10.0 295.2 %all-gather.18.cloned.1.call-start = ((), (), s32[]{:S(2)}) async-start(), calls=%async_computation.20 | async-start | bytes 6684672 | tf_op jit(solution)/shard_map/all_gather | solution.py:202
  10.6 358.9 %all-gather.16.cloned.1.call-start = ((), (), s32[]{:S(2)}) async-start(), calls=%async_computation.19 | async-start | bytes 6684672 | tf_op jit(solution)/shard_map/all_gather | solution.py:202
  11.1 422.8 %all-gather.20.cloned.1.call-start = ((), (), s32[]{:S(2)}) async-start(), calls=%async_computation.21 | async-start | bytes 6684672 | tf_op jit(solution)/shard_map/all_gather | solution.py:202
  61.2 54.1 %copy-start.6 = (bf16[2,128,1024]{2,1,0:T(8,128)(2,1)}, bf16[2,128,1024]{2,1,0:T(8,128)(2,1)S(1)}, u32[]{:S(2)}) copy-start(bf16[2,128,1024]{2,1,0:T(8,128)(2,1)S(1)} %fusion.75) | copy-start | bytes 1572868
  66.4 113.5 %all-to-all-start = ((bf16[2,128,8,128]{3,1,0,2:T(8,128)(2,1)}), bf16[2,128,8,128]{3,1,0,2:T(8,128)(2,1)}, u32[]{:S(2)}, u32[]{:S(2)}) async-start(bf16[2,128,8,128]{3,1,0,2:T(8,128)(2,1)} %copy.151), calls=%async_computation | async-start | bytes 1048576 | tf_op jit(solution)/shard_map/all_to_all | solution.py:94
  179.8 14.3 %all-to-all-start.1 = ((bf16[2,128,8,128]{1,0,3,2:T(2,128)(2,1)}), bf16[2,128,8,128]{1,0,3,2:T(2,128)(2,1)}, u32[]{:S(2)}, u32[]{:S(2)}) async-start(bf16[2,128,8,128]{1,0,3,2:T(2,128)(2,1)} %reshape_reshape.8), calls=%async_computation.1 | async-start | bytes 1048576 | tf_op jit(solution)/shard_map/all_to_all | solution.py:94
  194.2 20.7 %all-to-all-start.2 = ((bf16[2,128,16,128]{1,0,3,2:T(2,128)(2,1)}), bf16[2,128,16,128]{1,0,3,2:T(2,128)(2,1)}, u32[]{:S(2)}, u32[]{:S(2)}) async-start(bf16[2,128,16,128]{1,0,3,2:T(2,128)(2,1)} %reshape_reshape.9), calls=%async_computation.2 | async-start | bytes 2097152 | tf_op jit(solution)/shard_map/all_to_all | solution.py:94
  237.5 20.5 %all-to-all-start.3 = ((bf16[2,1024,2,128]{3,2,0,1:T(2,128)(2,1)}), bf16[2,1024,2,128]{3,2,0,1:T(2,128)(2,1)}, u32[]{:S(2)}, u32[]{:S(2)}) async-start(bf16[2,1024,2,128]{3,2,0,1:T(2,128)(2,1)} %copy.161), calls=%async_computation.3 | async-start | bytes 2097152 | tf_op jit(solution)/shard_map/all_to_all | solution.py:98
  453.5 21.7 %all-to-all-start.4 = ((bf16[2,128,16,128]{3,1,0,2:T(8,128)(2,1)}), bf16[2,128,16,128]{3,1,0,2:T(8,128)(2,1)}, u32[]{:S(2)}, u32[]{:S(2)}) async-start(bf16[2,128,16,128]{3,1,0,2:T(8,128)(2,1)} %copy.163), calls=%async_computation.4 | async-start | bytes 2097152 | tf_op jit(solution)/shard_map/all_to_all | solution.py:94
  494.5 21.2 %all-to-all-start.7 = ((bf16[2,1024,1,128]{3,0,2,1:T(2,128)(2,1)}), bf16[2,1024,1,128]{3,0,2,1:T(2,128)(2,1)}, u32[]{:S(2)}, u32[]{:S(2)}) async-start(bf16[2,1024,1,128]{3,0,2,1:T(2,128)(2,1)} %copy.183), calls=%async_computation.7 | async-start | bytes 1048576 | tf_op jit(solution)/shard_map/all_to_all | solution.py:98
  498.7 126.4 %reduce-scatter.12.cloned.1.call-start = ((), (), s32[]{:S(2)}) async-start(), calls=%async_computation.24 | async-start | bytes 2228224 | tf_op jit(solution)/shard_map/reduce_scatter | solution.py:212
  521.2 150.3 %reduce-scatter.10.cloned.1.call-start = ((), (), s32[]{:S(2)}) async-start(), calls=%async_computation.23 | async-start | bytes 2228224 | tf_op jit(solution)/shard_map/reduce_scatter | solution.py:212
  560.5 194.5 %reduce-scatter.14.cloned.1.call-start = ((), (), s32[]{:S(2)}) async-start(), calls=%async_computation.25 | async-start | bytes 4456448 | tf_op jit(solution)/shard_map/reduce_scatter | solution.py:212
  565.5 273.6 %reduce-scatter.8.cloned.1.call-start = ((), (), s32[]{:S(2)}) async-start(), calls=%async_computation.22 | async-start | bytes 4456448 | tf_op jit(solution)/shard_map/reduce_scatter | solution.py:212
  605.2 326.5 %reduce-scatter.18.cloned.1.call-start = ((), (), s32[]{:S(2)}) async-start(), calls=%async_computation.27 | async-start | bytes 6684672 | tf_op jit(solution)/shard_map/reduce_scatter | solution.py:212
  611.3 413.8 %reduce-scatter.16.cloned.1.call-start = ((), (), s32[]{:S(2)}) async-start(), calls=%async_computation.26 | async-start | bytes 6684672 | tf_op jit(solution)/shard_map/reduce_scatter | solution.py:212
  617.3 500.4 %reduce-scatter.20.cloned.1.call-start = ((), (), s32[]{:S(2)}) async-start(), calls=%async_computation.28 | async-start | bytes 6684672 | tf_op jit(solution)/shard_map/reduce_scatter | solution.py:212
  623.4 494.4 %copy-start.21 = (f32[256,1024]{1,0:T(8,128)S(1)}, f32[256,1024]{1,0:T(8,128)}, u32[]{:S(2)}) copy-start(f32[256,1024]{1,0:T(8,128)} %copy-done.19) | copy-start | bytes 3145732
  623.4 600.0 %all-reduce.14.cloned.1.call-start = ((), (), s32[]{:S(2)}) async-start(), calls=%async_computation.29 | async-start | bytes 3932160 | tf_op jit(solution)/shard_map/psum | solution.py:213
  1125.5 65.6 %copy-start.10 = (f32[256,1024]{1,0:T(8,128)S(1)}, f32[256,1024]{1,0:T(8,128)}, u32[]{:S(2)}) copy-start(f32[256,1024]{1,0:T(8,128)} %copy-done.9) | copy-start | bytes 3145732
  (54 other events, 239.4 us)
Sparse Core Ops, SparseCore 0:
  10.5 50.1 all-gather.7
  63.1 48.2 all-gather.9
  113.9 54.1 all-gather.11
  170.4 59.9 all-gather.13
  232.7 72.3 all-gather.17
  307.5 61.9 all-gather.15
  371.9 61.9 all-gather.19
  521.3 75.0 reduce-scatter.11
  600.9 70.6 reduce-scatter.9
  675.4 79.6 reduce-scatter.13
  759.6 79.4 reduce-scatter.7
  843.1 88.5 reduce-scatter.17
  936.5 88.5 reduce-scatter.15
  1029.1 88.5 reduce-scatter.19
  1121.0 102.4 all-reduce.13

commit v2 on v1

--- a/solution.py
+++ b/solution.py
@@ -1,14 +1,670 @@
+import functools
 import math
 
 import jax
 import jax.numpy as jnp
 from jax import lax
+from jax.experimental import pallas as pl
+from jax.experimental.pallas import tpu as pltpu
 from jax.sharding import PartitionSpec as P
 
 epsilon = 1e-06
 rope_base = 1000000.0
 bf16 = jnp.bfloat16
 f32 = jnp.float32
+
+
+MESH = pl.DeviceIdType.MESH
+SHARD_ROWS = (64, 128, 64, 192)
+COLUMNS = (4096, 1024, 6144, 1024)
+THIRDS = ((640, 640, 768), (256, 128, 128), (1024, 1024, 1024), (128, 256, 128))
+
+
+class Place:
+    def __init__(self):
+        dp, seq = lax.axis_index("dp"), lax.axis_index("seq")
+        x, y_lo = seq // 2, seq % 2
+        y_hi, z, core = dp // 8, (dp // 2) % 4, dp % 2
+        self.dp, self.seq, self.x, self.y_lo = dp, seq, x, y_lo
+        self.y_hi, self.z, self.core = y_hi, z, core
+        self.z_up, self.z_down, self.z_far = (z + 1) % 4, (z + 3) % 4, (z + 2) % 4
+        self.color = (x + y_lo + y_hi) % 2
+        self.to_z_up = (y_hi * 8 + self.z_up * 2 + core, seq)
+        self.to_z_down = (y_hi * 8 + self.z_down * 2 + core, seq)
+        self.to_x_up = (dp, ((x + 1) % 4) * 2 + y_lo)
+        self.to_x_down = (dp, ((x + 3) % 4) * 2 + y_lo)
+        self.to_pair = (dp, x * 2 + 1 - y_lo)
+        self.to_cross = ((1 - y_hi) * 8 + z * 2 + core, x * 2 + 1 - y_lo)
+        self.to_core = (y_hi * 8 + z * 2 + 1 - core, seq)
+
+    def torus(self):
+        return (
+            self.to_z_up,
+            self.to_z_down,
+            self.to_x_up,
+            self.to_x_down,
+            self.to_pair,
+            self.to_cross,
+            self.to_core,
+        )
+
+
+def greet(peers):
+    barrier = pltpu.get_barrier_semaphore()
+    for peer in peers:
+        pl.semaphore_signal(barrier, inc=1, device_id=peer, device_id_type=MESH)
+    pl.semaphore_wait(barrier, len(peers))
+
+
+GATHER_KINDS = (
+    "own_up",
+    "own_down",
+    "on_up",
+    "on_down",
+    "cross_own",
+    "cross_up",
+    "cross_down",
+    "cross_far",
+    "other_up",
+    "other_down",
+    "other_on_up",
+    "other_on_down",
+) + tuple(f"share_{n}_{s}" for n in range(3) for s in ("up", "down", "far", "other"))
+GATHER_KINDS += tuple(f"core_{s}" for s in ("own", "up", "down", "far", "other"))
+KIND_AT = {kind: at for at, kind in enumerate(GATHER_KINDS)}
+KINDS = len(GATHER_KINDS)
+
+
+class Gather:
+    def __init__(self, place, buffers, send_sem, recv_sem):
+        self.place, self.buffers, self.send_sem, self.recv_sem = place, buffers, send_sem, recv_sem
+        self.sent = []
+
+    def region(self, g, kind, receiving):
+        p = self.place
+        rows, cols = SHARD_ROWS[g], COLUMNS[g]
+        half = cols // 2
+        here, there = p.y_hi, 1 - p.y_hi
+        whole, top, low = pl.ds(0, rows), pl.ds(0, rows // 2), pl.ds(rows // 2, rows // 2)
+        low_first = pl.ds(rows // 2, rows // 4)
+        low_last = pl.ds(rows // 2 + rows // 4, rows // 4)
+        color = p.color
+        if kind.startswith("share") and receiving:
+            color = 1 - color
+        first = color * half
+        mine = pl.ds(pl.multiple_of(first, 128), half)
+        below, above = p.z_down, p.z_up
+        z, far = p.z, p.z_far
+        buf = self.buffers[g]
+
+        def at(y, zz, r, c):
+            return buf.at[y, zz, p.core, r, c]
+
+        if kind == "own_up":
+            return at(here, below if receiving else z, whole, mine), p.to_z_up
+        if kind == "own_down":
+            return at(here, above if receiving else z, whole, mine), p.to_z_down
+        if kind == "on_up":
+            return at(here, far if receiving else below, top, mine), p.to_z_up
+        if kind == "on_down":
+            return at(here, far if receiving else above, low, mine), p.to_z_down
+        if kind.startswith("cross"):
+            y = there if receiving else here
+            which = kind[6:]
+            if which == "own":
+                return at(y, z, whole, mine), p.to_cross
+            return at(y, {"up": above, "down": below, "far": far}[which], top, mine), p.to_cross
+        if kind == "other_up":
+            return at(there, below if receiving else z, low, mine), p.to_z_up
+        if kind == "other_down":
+            return at(there, above if receiving else z, low, mine), p.to_z_down
+        if kind == "other_on_up":
+            return at(there, far if receiving else below, low_first, mine), p.to_z_up
+        if kind == "other_on_down":
+            return at(there, far if receiving else above, low_last, mine), p.to_z_down
+        if kind.startswith("share"):
+            _, n, which = kind.split("_")
+            n = int(n)
+            start = sum(THIRDS[g][:n])
+            part = pl.ds(pl.multiple_of(first + start, 128), THIRDS[g][n])
+            to = (p.to_x_up, p.to_x_down, p.to_pair)[n]
+            if which == "other":
+                return buf.at[there, :, p.core, :, part], to
+            return at(here, {"up": above, "down": below, "far": far}[which], whole, part), to
+        which = kind[5:]
+        core = 1 - p.core if receiving else p.core
+        if which == "other":
+            return buf.at[there, :, core], p.to_core
+        return buf.at[here, {"own": z, "up": above, "down": below, "far": far}[which], core], p.to_core
+
+    def copy(self, g, kind, receiving=False):
+        region, to = self.region(g, kind, receiving)
+        at = KIND_AT[kind]
+        return pltpu.make_async_remote_copy(
+            src_ref=region,
+            dst_ref=region,
+            send_sem=self.send_sem.at[g, at],
+            recv_sem=self.recv_sem.at[g, at],
+            device_id=to,
+            device_id_type=MESH,
+        )
+
+    def send(self, g, *kinds):
+        for kind in kinds:
+            self.copy(g, kind).start()
+            self.sent.append((g, kind))
+
+    def take(self, g, *kinds):
+        for kind in kinds:
+            self.copy(g, kind, True).wait_recv()
+
+    def share(self, g, which):
+        self.send(g, *(f"share_{n}_{which}" for n in range(3)))
+
+    def taken(self, g, which):
+        self.take(g, *(f"share_{n}_{which}" for n in range(3)))
+
+    def phase(self, number, g):
+        if number == 0:
+            self.send(g, "own_up", "own_down", "cross_own", "core_own")
+        elif number == 1:
+            self.take(g, "own_up", "own_down")
+            self.send(g, "on_up", "on_down", "cross_up", "cross_down")
+            self.share(g, "up")
+            self.share(g, "down")
+        elif number == 2:
+            self.take(g, "cross_own")
+            self.send(g, "other_up", "other_down")
+            self.take(g, "on_up", "on_down")
+            self.send(g, "cross_far")
+            self.share(g, "far")
+        elif number == 3:
+            self.take(g, "other_up", "other_down")
+            self.send(g, "other_on_up", "other_on_down")
+        elif number == 4:
+            self.take(g, "cross_up", "cross_down", "cross_far", "other_on_up", "other_on_down")
+            self.share(g, "other")
+        elif number == 5:
+            for which in ("up", "down", "far"):
+                self.taken(g, which)
+                self.send(g, f"core_{which}")
+        elif number == 6:
+            self.taken(g, "other")
+            self.send(g, "core_other")
+        else:
+            self.take(g, "core_own", "core_up", "core_down", "core_far", "core_other")
+
+    def finish(self):
+        for g, kind in self.sent:
+            self.copy(g, kind).wait_send()
+        self.sent = []
+
+
+def own_places(place, buffers):
+    mine = [buf.at[place.y_hi, place.z, place.core] for buf in buffers]
+    return (
+        mine[0].at[:, pl.ds(0, 2048)],
+        mine[0].at[:, pl.ds(2048, 1024)],
+        mine[0].at[:, pl.ds(3072, 1024)],
+        mine[1],
+        mine[2].at[:, pl.ds(0, 3072)],
+        mine[2].at[:, pl.ds(3072, 3072)],
+        mine[3],
+    )
+
+
+class GatherSmall:
+    def __init__(self, place, buffer, send_sem, recv_sem):
+        self.place, self.buffer, self.send_sem, self.recv_sem = place, buffer, send_sem, recv_sem
+
+    def copy(self, step, receiving=False):
+        p, buf = self.place, self.buffer
+        if step == 0:
+            region, to = buf.at[p.y_hi, p.z, 1 - p.core if receiving else p.core], p.to_core
+        elif step == 1:
+            region, to = buf.at[1 - p.y_hi if receiving else p.y_hi, p.z], p.to_cross
+        elif step == 2:
+            region, to = buf.at[:, p.z_down if receiving else p.z], p.to_z_up
+        elif step == 3:
+            region, to = buf.at[:, p.z_up if receiving else p.z], p.to_z_down
+        else:
+            region, to = buf.at[:, p.z_far if receiving else p.z_down], p.to_z_up
+        return pltpu.make_async_remote_copy(
+            src_ref=region,
+            dst_ref=region,
+            send_sem=self.send_sem.at[step],
+            recv_sem=self.recv_sem.at[step],
+            device_id=to,
+            device_id_type=MESH,
+        )
+
+    def start(self, step):
+        self.copy(step).start()
+
+    def take(self, step):
+        self.copy(step, True).wait_recv()
+
+    def finish(self):
+        for step in range(5):
+            self.copy(step).wait_send()
+
+
+ORDER = (
+    (0, 0),
+    (0, 1),
+    (1, 0),
+    (2, 0),
+    (0, 2),
+    (3, 0),
+    (1, 1),
+    (4, 0),
+    (2, 1),
+    (5, 0),
+    (3, 1),
+    (0, 3),
+    (1, 2),
+    (4, 1),
+    (6, 0),
+    (2, 2),
+    (5, 1),
+    (3, 2),
+    (1, 3),
+    (4, 2),
+    (6, 1),
+    (2, 3),
+    (5, 2),
+    (3, 3),
+    (4, 3),
+    (6, 2),
+    (5, 3),
+    (6, 3),
+    (7, 0),
+    (7, 1),
+    (7, 2),
+    (7, 3),
+)
+
+
+def gather_kernel(*refs):
+    shards, small = refs[:7], refs[7]
+    buffers, small_all = refs[8:12], refs[12]
+    send_sem, recv_sem, small_send, small_recv, local_sem = refs[13:]
+    place = Place()
+    copies = [
+        pltpu.make_async_copy(shard, there, local_sem.at[at])
+        for at, (shard, there) in enumerate(
+            zip(shards + (small,), own_places(place, buffers) + (small_all.at[place.y_hi, place.z, place.core],))
+        )
+    ]
+    for copy in copies:
+        copy.start()
+    greet(place.torus())
+    for copy in copies:
+        copy.wait()
+    gather = Gather(place, buffers, send_sem, recv_sem)
+    little = GatherSmall(place, small_all, small_send, small_recv)
+    little.start(0)
+    gather.phase(0, 0)
+    little.take(0)
+    little.start(1)
+    gather.phase(0, 1)
+    little.take(1)
+    little.start(2)
+    little.start(3)
+    little.take(2)
+    little.take(3)
+    little.start(4)
+    for number, g in ORDER[2:]:
+        gather.phase(number, g)
+    little.take(4)
+    gather.finish()
+    little.finish()
+
+
+def gather_all(shards, small):
+    shapes = [
+        jax.ShapeDtypeStruct((2, 4, 2, rows, cols), bf16) for rows, cols in zip(SHARD_ROWS, COLUMNS)
+    ] + [jax.ShapeDtypeStruct((2, 4, 2, 16, 128), bf16)]
+    return pl.pallas_call(
+        functools.partial(gather_kernel),
+        out_shape=shapes,
+        in_specs=[pl.BlockSpec(memory_space=pltpu.VMEM)] * 8,
+        out_specs=[pl.BlockSpec(memory_space=pl.ANY)] * 5,
+        scratch_shapes=[
+            pltpu.SemaphoreType.DMA((4, KINDS)),
+            pltpu.SemaphoreType.DMA((4, KINDS)),
+            pltpu.SemaphoreType.DMA((5,)),
+            pltpu.SemaphoreType.DMA((5,)),
+            pltpu.SemaphoreType.DMA((8,)),
+        ],
+        compiler_params=pltpu.CompilerParams(collective_id=1, has_side_effects=True),
+        name="gather_weights",
+    )(*shards, small)
+
+
+PART_ORDER = ("xyz", "yzx", "zxy")
+FREE = ((("yl", "yh", "z"), ("z",), ()), (("z", "x"), ("x",), ()), (("yl", "yh", "x"), ("yl", "yh"), ()))
+EXTENT = {"yl": 2, "yh": 2, "z": 4, "x": 4}
+
+
+def half_shape(part, step):
+    free = FREE[part][step]
+    first = EXTENT[free[0]] // 2
+    return ((first,) if first > 1 else ()) + tuple(EXTENT[d] for d in free[1:])
+
+
+def near_shape(part, step):
+    return tuple(EXTENT[d] for d in FREE[part][step])
+
+
+def reduce_scratch():
+    shapes = []
+    for g in range(4):
+        rows, half = SHARD_ROWS[g] // 4, COLUMNS[g] // 2
+        shapes.append(pltpu.VMEM((2, 2, 4, 4, rows, half), bf16))
+        shapes.append(pltpu.VMEM((2, 2, 4, 4, rows, half), bf16))
+        shapes.append(pltpu.VMEM((2, 4, rows, half), bf16))
+        for part in range(3):
+            tail = (rows, THIRDS[g][part])
+            for step in range(3):
+                if step < 2:
+                    shapes.append(pltpu.VMEM((2,) + half_shape(part, step) + tail, bf16))
+                else:
+                    shapes.append(pltpu.VMEM((1,) + tail, bf16))
+                shapes.append(pltpu.VMEM((2,) + near_shape(part, step) + tail, bf16))
+    return shapes
+
+
+SCRATCH_PER_GROUP = 3 + 18
+REDUCE_SEMS = 3 * 12 + 1 + 1 + 2 + 2
+
+
+def accumulate(dst, src):
+    lead = dst.shape[:-2]
+    count = 1
+    for n in lead:
+        count *= n
+    if not lead:
+        dst[...] = dst[...] + src[...]
+        return
+
+    def body(i, carry):
+        at, rest = [], i
+        for n in reversed(lead):
+            at.append(rest % n)
+            rest = rest // n
+        at = tuple(reversed(at))
+        dst.at[at][...] = dst.at[at][...] + src.at[at][...]
+        return carry
+
+    lax.fori_loop(0, count, body, 0)
+
+
+class Reduce:
+    def __init__(self, place, grads, scratch, send_sem, recv_sem, load_sem):
+        self.place, self.grads = place, grads
+        self.send_sem, self.recv_sem, self.load_sem = send_sem, recv_sem, load_sem
+        self.sent = []
+        self.groups = [scratch[g * SCRATCH_PER_GROUP : (g + 1) * SCRATCH_PER_GROUP] for g in range(4)]
+
+    def total(self, g):
+        return self.groups[g][0]
+
+    def from_core(self, g):
+        return self.groups[g][1]
+
+    def result(self, g):
+        return self.groups[g][2]
+
+    def halves(self, g, part, step):
+        return self.groups[g][3 + (part * 3 + step) * 2]
+
+    def nears(self, g, part, step):
+        return self.groups[g][4 + (part * 3 + step) * 2]
+
+    def cols(self, g, part):
+        return pl.ds(sum(THIRDS[g][:part]), THIRDS[g][part])
+
+    def moved(self, dim, by):
+        p = self.place
+        if dim == "x":
+            x = (p.x + by) % 4
+            return {"x": x}, (p.dp, x * 2 + p.y_lo)
+        if dim == "z":
+            z = (p.z + by) % 4
+            return {"z": z}, (p.y_hi * 8 + z * 2 + p.core, p.seq)
+        y = (p.y_hi * 2 + p.y_lo + by) % 4
+        return {"yl": y % 2, "yh": y // 2}, ((y // 2) * 8 + p.z * 2 + p.core, p.x * 2 + y % 2)
+
+    def chunk(self, g, part, step, by, half=None):
+        at = {}
+        for earlier in range(step):
+            at.update(self.moved(PART_ORDER[part][earlier], 0)[0])
+        at.update(self.moved(PART_ORDER[part][step], by)[0])
+        if half is not None:
+            cut = FREE[part][step][0]
+            size = EXTENT[cut] // 2
+            at[cut] = half if size == 1 else pl.ds(half * size, size)
+        index = tuple(at.get(name, slice(None)) for name in ("yl", "yh", "z", "x"))
+        return self.total(g).at[index + (slice(None), self.cols(g, part))]
+
+    def remote(self, g, sem, src, dst, to):
+        return pltpu.make_async_remote_copy(
+            src_ref=src,
+            dst_ref=dst,
+            send_sem=self.send_sem.at[g, sem],
+            recv_sem=self.recv_sem.at[g, sem],
+            device_id=to,
+            device_id_type=MESH,
+        )
+
+    def send(self, g, sem, src, dst, to):
+        copy = self.remote(g, sem, src, dst, to)
+        copy.start()
+        self.sent.append(copy)
+
+    def take(self, g, sem, dst):
+        self.remote(g, sem, dst, dst, self.place.to_core).wait_recv()
+
+    def begin(self, g):
+        p = self.place
+        self.send(g, 36, self.grads[g].at[:, :, :, 1 - p.core], self.from_core(g), p.to_core)
+        self.load(g).start()
+
+    def load(self, g):
+        return pltpu.make_async_copy(self.grads[g].at[:, :, :, self.place.core], self.total(g), self.load_sem.at[g])
+
+    def join_cores(self, g):
+        self.load(g).wait()
+        self.take(g, 36, self.from_core(g))
+        accumulate(self.total(g), self.from_core(g))
+
+    def send_far(self, g, step):
+        for part in range(3):
+            sem, dim = part * 12 + step * 4, PART_ORDER[part][step]
+            buf = self.halves(g, part, step)
+            up, down = self.moved(dim, 1)[1], self.moved(dim, 3)[1]
+            if step < 2:
+                self.send(g, sem, self.chunk(g, part, step, 2, 0), buf.at[0], up)
+                self.send(g, sem + 1, self.chunk(g, part, step, 2, 1), buf.at[1], down)
+            else:
+                self.send(g, sem, self.chunk(g, part, step, 2), buf.at[0], up)
+
+    def send_near(self, g, step):
+        for part in range(3):
+            sem, dim = part * 12 + step * 4, PART_ORDER[part][step]
+            buf, near = self.halves(g, part, step), self.nears(g, part, step)
+            up, down = self.moved(dim, 1)[1], self.moved(dim, 3)[1]
+            self.take(g, sem, buf.at[0])
+            accumulate(self.chunk(g, part, step, 1, 0 if step < 2 else None), buf.at[0])
+            self.send(g, sem + 2, self.chunk(g, part, step, 1), near.at[0], up)
+            if step < 2:
+                self.take(g, sem + 1, buf.at[1])
+                accumulate(self.chunk(g, part, step, 3, 1), buf.at[1])
+            self.send(g, sem + 3, self.chunk(g, part, step, 3), near.at[1], down)
+
+    def join_near(self, g, step):
+        for part in range(3):
+            sem, near = part * 12 + step * 4, self.nears(g, part, step)
+            for way in range(2):
+                self.take(g, sem + 2 + way, near.at[way])
+                accumulate(self.chunk(g, part, step, 0), near.at[way])
+
+    def stage(self, number, g):
+        p = self.place
+        result = self.result(g)
+        if number == 0:
+            self.join_cores(g)
+            self.send_far(g, 0)
+        elif number in (1, 3, 5):
+            self.send_near(g, number // 2)
+        elif number in (2, 4):
+            self.join_near(g, number // 2 - 1)
+            self.send_far(g, number // 2)
+        elif number == 6:
+            self.join_near(g, 2)
+            result.at[p.y_lo, p.x][...] = self.total(g).at[p.y_lo, p.y_hi, p.z, p.x][...]
+            mine = result.at[p.y_lo, p.x]
+            self.send(g, 37, mine, mine, p.to_pair)
+        elif number == 7:
+            self.take(g, 37, result.at[1 - p.y_lo, p.x])
+            mine = result.at[:, p.x]
+            self.send(g, 38, mine, mine, p.to_x_up)
+            self.send(g, 39, mine, mine, p.to_x_down)
+        elif number == 8:
+            below, above = (p.x + 3) % 4, (p.x + 1) % 4
+            self.take(g, 38, result.at[:, below])
+            self.send(g, 40, result.at[0, below], result.at[0, below], p.to_x_up)
+            self.take(g, 39, result.at[:, above])
+            self.send(g, 41, result.at[1, above], result.at[1, above], p.to_x_down)
+        else:
+            far = (p.x + 2) % 4
+            self.take(g, 40, result.at[0, far])
+            self.take(g, 41, result.at[1, far])
+
+    def finish(self):
+        for copy in self.sent:
+            copy.wait_send()
+        self.sent = []
+
+
+class ReduceSmall:
+    STEPS = (("core", 2), ("pair", 2), ("cross", 2), ("x", 4), ("z", 4))
+
+    def __init__(self, place, slots, send_sem, recv_sem):
+        self.place, self.slots, self.send_sem, self.recv_sem = place, slots, send_sem, recv_sem
+
+    def peers(self, step):
+        p = self.place
+        name, count = self.STEPS[step]
+        if count == 2:
+            mine, to = {
+                "core": (p.core, p.to_core),
+                "pair": (p.y_lo, p.to_pair),
+                "cross": (p.y_hi, p.to_cross),
+            }[name]
+            return mine, [(1 - mine, to)]
+        if name == "x":
+            return p.x, [((p.x + by) % 4, (p.dp, (p.x + by) % 4 * 2 + p.y_lo)) for by in (1, 2, 3)]
+        return p.z, [
+            ((p.z + by) % 4, (p.y_hi * 8 + (p.z + by) % 4 * 2 + p.core, p.seq)) for by in (1, 2, 3)
+        ]
+
+    def copies(self, step, receiving):
+        mine, peers = self.peers(step)
+        if receiving:
+            peers = peers[::-1]
+        for at, (place, to) in enumerate(peers):
+            slot = self.slots.at[step, place if receiving else mine]
+            yield pltpu.make_async_remote_copy(
+                src_ref=slot,
+                dst_ref=slot,
+                send_sem=self.send_sem.at[step, at],
+                recv_sem=self.recv_sem.at[step, at],
+                device_id=to,
+                device_id_type=MESH,
+            )
+
+    def put(self, step, values):
+        mine, _ = self.peers(step)
+        self.slots.at[step, mine][...] = values
+        for copy in self.copies(step, False):
+            copy.start()
+
+    def sum(self, step):
+        for copy in self.copies(step, True):
+            copy.wait_recv()
+        for copy in self.copies(step, False):
+            copy.wait_send()
+        total = self.slots[step, 0]
+        for at in range(1, self.STEPS[step][1]):
+            total = total + self.slots[step, at]
+        return total
+
+
+REDUCE_ORDER = (3, 2, 1, 0)
+
+
+def reduce_kernel(*refs):
+    grads, small = refs[:4], refs[4]
+    outs, small_out = refs[5:9], refs[9]
+    scratch = refs[10 : 10 + 4 * SCRATCH_PER_GROUP]
+    slots, send_sem, recv_sem, load_sem, small_send, small_recv, out_sem = refs[10 + 4 * SCRATCH_PER_GROUP :]
+    place = Place()
+    greet(
+        place.torus()
+        + (
+            (place.dp, (place.x + 2) % 4 * 2 + place.y_lo),
+            (place.y_hi * 8 + place.z_far * 2 + place.core, place.seq),
+        )
+    )
+    reduce = Reduce(place, grads, scratch, send_sem, recv_sem, load_sem)
+    little = ReduceSmall(place, slots, small_send, small_recv)
+    for g in REDUCE_ORDER:
+        reduce.begin(g)
+    little.put(0, small[...])
+    for slot in range(4 + 9):
+        for stage in range(10):
+            if 0 <= slot - stage < 4:
+                reduce.stage(stage, REDUCE_ORDER[slot - stage])
+                if stage == 9:
+                    g = REDUCE_ORDER[slot - stage]
+                    pltpu.make_async_copy(reduce.result(g), outs[g], out_sem.at[g]).start()
+        if slot < 4:
+            little.put(slot + 1, little.sum(slot))
+        elif slot == 4:
+            small_out[...] = little.sum(4)
+    reduce.finish()
+    for g in range(4):
+        pltpu.make_async_copy(reduce.result(g), outs[g], out_sem.at[g]).wait()
+
+
+def reduce_all(grads, small):
+    shapes = [
+        jax.ShapeDtypeStruct((2, 4, rows // 4, cols // 2), bf16) for rows, cols in zip(SHARD_ROWS, COLUMNS)
+    ] + [jax.ShapeDtypeStruct((24, 128), f32)]
+    vmem = pl.BlockSpec(memory_space=pltpu.VMEM)
+    hbm = pl.BlockSpec(memory_space=pl.ANY)
+    return pl.pallas_call(
+        functools.partial(reduce_kernel),
+        out_shape=shapes,
+        in_specs=[hbm] * 4 + [vmem],
+        out_specs=[hbm] * 4 + [vmem],
+        scratch_shapes=reduce_scratch()
+        + [
+            pltpu.VMEM((5, 4, 24, 128), f32),
+            pltpu.SemaphoreType.DMA((4, REDUCE_SEMS)),
+            pltpu.SemaphoreType.DMA((4, REDUCE_SEMS)),
+            pltpu.SemaphoreType.DMA((4,)),
+            pltpu.SemaphoreType.DMA((5, 3)),
+            pltpu.SemaphoreType.DMA((5, 3)),
+            pltpu.SemaphoreType.DMA((4,)),
+        ],
+        compiler_params=pltpu.CompilerParams(
+            collective_id=2, has_side_effects=True, vmem_limit_bytes=60 * 1024 * 1024
+        ),
+        name="reduce_grads",
+    )(*grads, small)
 
 
 def product(left, right):
@@ -198,22 +854,60 @@
     w_up,
     w_down,
 ):
-    def gather(shard):
-        return lax.all_gather(shard, "dp", axis=0, tiled=True)
-
-    gains = [gather(g) for g in (attn_gain, query_gain, key_gain, ffn_gain)]
+    dp = lax.axis_index("dp")
+    tile = jnp.zeros((16, 128), bf16)
+    for row, (gain, lane) in enumerate(
+        ((attn_gain, dp % 2 * 64), (query_gain, dp * 8), (key_gain, dp * 8), (ffn_gain, dp % 2 * 64))
+    ):
+        tile = lax.dynamic_update_slice(tile, gain[None, :], (row, lane))
     shards = (w_query, key_weight, value_weight, w_output, w_gate, w_up, w_down)
-    weights = [gather(w) for w in shards]
+    qkv, output, gate_up, down, small = gather_all(shards, tile)
+    qkv, gate_up = qkv.reshape(1024, 4096), gate_up.reshape(1024, 6144)
+    weights = (
+        qkv[:, :2048],
+        qkv[:, 2048:3072],
+        qkv[:, 3072:],
+        output.reshape(2048, 1024),
+        gate_up[:, :3072],
+        gate_up[:, 3072:],
+        down.reshape(3072, 1024),
+    )
+    small = small.astype(f32).reshape(8, 2, 16, 128)
+    gains = (
+        jnp.sum(small[:, :, 0], axis=1).reshape(1024),
+        jnp.sum(small[:, :, 1], axis=(0, 1)),
+        jnp.sum(small[:, :, 2], axis=(0, 1)),
+        jnp.sum(small[:, :, 3], axis=1).reshape(1024),
+    )
     out, d_input, gain_grads, weight_grads = layer(
         hidden_in, out_cotangent, slot_lengths, position_ids, gains, weights
     )
 
-    def owned(part):
-        part = lax.psum_scatter(part.astype(bf16), "dp", scatter_dimension=0, tiled=True)
-        return lax.psum(part, "seq").astype(f32)
-
-    dg_attn, dg_query, dg_key, dg_ffn = [owned(g) for g in gain_grads]
-    gq, gk, gv, go, gg, gu, gd = [owned(g) for g in weight_grads]
+    gq, gk, gv, go, gg, gu, gd = [part.astype(bf16) for part in weight_grads]
+    halves = (
+        (gq, jnp.concatenate([gk, gv], axis=1)),
+        (go[:, :512], go[:, 512:]),
+        (gg, gu),
+        (gd[:, :512], gd[:, 512:]),
+    )
+    grads = [
+        jnp.stack(pair).reshape(2, 2, 4, 2, 4, rows // 4, cols // 2)
+        for pair, rows, cols in zip(halves, SHARD_ROWS, COLUMNS)
+    ]
+    flat = jnp.concatenate(gain_grads)
+    flat = jnp.pad(flat, (0, 24 * 128 - flat.shape[0])).reshape(24, 128)
+    *sums, gains_sum = reduce_all(grads, flat)
+    qkv, output, gate_up, down = [
+        part.reshape(2, rows, cols // 2).astype(f32)
+        for part, rows, cols in zip(sums, SHARD_ROWS, COLUMNS)
+    ]
+    gq, gk, gv, gg, gu = qkv[0], qkv[1, :, :1024], qkv[1, :, 1024:], gate_up[0], gate_up[1]
+    go, gd = jnp.concatenate([output[0], output[1]], 1), jnp.concatenate([down[0], down[1]], 1)
+    gains_sum = gains_sum.reshape(-1)
+    dg_attn, dg_query, dg_key, dg_ffn = [
+        lax.dynamic_slice(gains_sum, (start + dp * size,), (size,))
+        for start, size in ((0, 64), (1024, 8), (1152, 8), (1280, 64))
+    ]
     return (out, d_input, dg_attn, gq, gk, gv, dg_query, dg_key, go, dg_ffn, gg, gu, gd)
 
 

time: 1250 us -> 509 us (0.41)
  waiting for transfers between devices: 811 us -> 25.2 us
  Pallas kernels: 0 us -> 191 us
  blocking collectives: 132 us -> 0 us
  matrix products: 118 us -> 97.9 us
  between operations: 18.1 us -> 2.26 us
    reduce_scatter x7 -> x0, waiting for transfers between devices: 493 us -> none  [owned(): lax.psum_scatter(part.astype(bf16), 'dp', scatter_dimension=0, tiled=True)]
    all_gather x7 -> x0, waiting for transfers between devices: 241 us -> none  [gather(): return lax.all_gather(shard, 'dp', axis=0, tiled=True)]
    pallas_call x0 -> x2, Pallas kernels: none -> 191 us  [the longest x1 103 us: reduce_all(): pl.pallas_call(functools.partial(reduce_kernel), out_shape=shapes, in_spe...]
    unnamed x2 -> x0, blocking collectives: 79.7 us -> none
    all_to_all x2 -> x0, blocking collectives: 31.8 us -> none  [to_rows(): lax.all_to_all(heads_in, 'seq', split_axis=1, concat_axis=2, tiled=True)]
    psum x1 -> x0, waiting for transfers between devices: 31.1 us -> none  [owned(): return lax.psum(part, 'seq').astype(f32)]
    psum x1 -> x0, blocking collectives: 20.6 us -> none  [owned(): return lax.psum(part, 'seq').astype(f32)]
    all_to_all x4, waiting for transfers between devices: 28 us -> 15 us  [to_heads(): return lax.all_to_all(parts, 'seq', split_axis=2, concat_axis=1, tiled=True)]
  transfers between devices with their start and end apart: 21 -> 8, of which waited for: 16 -> 4; matrix products, arithmetic and copies ran while one was open for 15% -> 20% of each run, Pallas kernels for 0% -> 0%
where the time goes in v2:
time: 509 us; the launch traced here: 500 us
  Pallas kernels  191 us (38%)
  matrix products  97.9 us (19%)
  local copies, waits for them, and re-layouts  89.5 us (18%)
  other arithmetic  55.8 us (11%)
  starting transfers between devices  37.4 us (7%)
  waiting for transfers between devices  25.2 us (5%)
    pallas_call x1, Pallas kernels, reduce_all(): pl.pallas_call(functools.partial(reduce_kernel), out_shape=shapes, in_spe...  103 us
    pallas_call x1, Pallas kernels, gather_all(): pl.pallas_call(functools.partial(gather_kernel), out_shape=shapes, in_spe...  88.5 us
    dot_general x7, matrix products, product(): return jnp.dot(left, right, preferred_element_type=f32)  27.6 us
    all_to_all x4, starting transfers between devices, to_rows(): lax.all_to_all(heads_in, 'seq', split_axis=1, concat_axis=2, tiled=True)  19.5 us
    unnamed x154, local copies, waits for them, and re-layouts  18.6 us
    another operation x4, other arithmetic, per_device(): jnp.stack(pair).reshape(2, 2, 4, 2, 4, rows // 4, cols // 2)  18.1 us
    all_to_all x4, starting transfers between devices, to_heads(): return lax.all_to_all(parts, 'seq', split_axis=2, concat_axis=1, tiled=True)  17.9 us
    dot_general x4, local copies, waits for them, and re-layouts, product(): return jnp.dot(left, right, preferred_element_type=f32)  17.3 us
  transfers between devices with their start and end apart: 8, of which 4 were waited for; matrix products, arithmetic and copies ran while one was open for 20% of the time, Pallas kernels for 0%

profile of v2, /device:TPU:0, one launch (start us, length us, event | category | flops | bytes accessed | tf_op | source)
XLA Modules:
  0.0 499.5 jit_solution(10179885721950334583)
XLA Ops:
  4.5 88.5 %gather_weights.1 = (bf16[2,4,2,64,4096]{4,3,2,1,0:T(8,128)(2,1)}, bf16[2,4,2,128,1024]{4,3,2,1,0:T(8,128)(2,1)}, bf16[2,4,2,64,6144]{4,3,2,1,0:T(8,128)(2,1)}, ...) custom-call(bf16[64,2048]{1,0:T(8,128)(2,1)} %refs_0_.1, bf16[64,1024]{1,0:T(8,128)(2,1)} %refs_1_.1, ...), custom_call_target="tpu_custom_call" | custom-call | tf_op jit(solution)/shard_map/gather_weights/pallas_call | solution.py:328
  109.7 4.8 slice_bitcast_fusion
  114.5 6.5 %copy.159 = bf16[2048,1024]{1,0:T(8,128)(2,1)} copy(bf16[2048,1024]{0,1:T(8,128)(2,1)} %slice_bitcast_fusion) | data formatting | bytes 8388608 | tf_op jit(solution)/shard_map/dot_general | solution.py:671
  133.6 5.7 %all-to-all-start = ((bf16[2,128,8,128]{3,1,0,2:T(8,128)(2,1)}), bf16[2,128,8,128]{3,1,0,2:T(8,128)(2,1)S(1)}, u32[]{:S(2)}, u32[]{:S(2)}) async-start(bf16[2,128,8,128]{3,1,0,2:T(8,128)(2,1)} %copy.155), calls=%async_computation | async-start | bytes 1048576 | tf_op jit(solution)/shard_map/all_to_all | solution.py:750
  142.2 7.0 %all-to-all-done = bf16[2,128,8,128]{3,1,0,2:T(8,128)(2,1)S(1)} async-done(((bf16[2,128,8,128]{3,1,0,2:T(8,128)(2,1)}), bf16[2,128,8,128]{3,1,0,2:T(8,128)(2,1)S(1)}, u32[]{:S(2)}, u32[]{:S(2)}) %all-to-all-start) | async-done | bytes 524320 | tf_op jit(solution)/shard_map/all_to_all | solution.py:750
  160.2 8.0 %all-to-all-done.2 = bf16[2,128,16,128]{1,0,3,2:T(2,128)(2,1)S(1)} async-done(((bf16[2,128,16,128]{1,0,3,2:T(2,128)(2,1)}), bf16[2,128,16,128]{1,0,3,2:T(2,128)(2,1)S(1)}, u32[]{:S(2)}, u32[]{:S(2)}) %all-to-all-start.2) | async-done | bytes 1048608 | tf_op jit(solution)/shard_map/all_to_all | solution.py:750
  190.7 6.3 %fusion.136 = f32[256,3072]{1,0:T(8,128)} fusion(bf16[256,1024]{1,0:T(8,128)(2,1)S(1)} %bitcast.433, bf16[3072,1024]{1,0:T(8,128)(2,1)} %bitcast.453), kind=kOutput, calls=%fused_computation.216 | convolution fusion | flops 1610612736 | bytes 9961472 | tf_op jit(solution)/shard_map/dot_general | solution.py:679
  197.1 8.3 %all-to-all-done.3 = bf16[2,1024,2,128]{3,2,0,1:T(2,128)(2,1)S(1)} async-done(((bf16[2,1024,2,128]{3,2,0,1:T(2,128)(2,1)}), bf16[2,1024,2,128]{3,2,0,1:T(2,128)(2,1)S(1)}, u32[]{:S(2)}, u32[]{:S(2)}) %all-to-all-start.3) | async-done | bytes 1048608 | tf_op jit(solution)/shard_map/all_to_all | solution.py:754
  211.1 4.7 fusion.14
  215.9 7.3 %multiply_convert_fusion.1 = (bf16[256,3072]{1,0:T(8,128)(2,1)S(1)}, bf16[256,3072]{1,0:T(8,128)(2,1)S(1)}, bf16[256,3072]{1,0:T(8,128)(2,1)}) fusion(f32[256,3072]{1,0:T(8,128)S(1)} %copy-done.60, f32[256,3072]{1,0:T(8,128)S(1)} %fusion.14, bf16[256,1024]{1,0:T(8,128)(2,1)S(1)} %multiply_convert_fusion.3, bf16[1024,6144]{1,0:T(8,128)(2,1)} %bitcast.448), kind=kOutput, calls=%fused_computation.59 | convolution fusion | flops 1622409216 | bytes 17825792 | tf_op jit(solution)/shard_map/dot_general | solution.py:671
  225.0 4.5 convolution_convert_fusion.1
  229.5 4.5 convolution_convert_fusion.2
  249.5 5.4 %fusion.56 = bf16[256,1024]{1,0:T(8,128)(2,1)} fusion(f32[256,1024]{1,0:T(8,128)S(1)} %get-tuple-element.103, bf16[256,3072]{1,0:T(8,128)(2,1)S(1)} %copy-done.20, bf16[3072,1024]{1,0:T(8,128)(2,1)} %bitcast.454, pred[256]{0:T(512)(128)(4,1)S(1)} %fusion.187), kind=kOutput, calls=%fused_computation.89 | convolution fusion | flops 1611399168 | bytes 9437440 | tf_op jit(solution)/shard_map/dot_general | solution.py:671
  267.6 5.6 %pad_maximum_fusion.refs_2_ = bf16[2,2,4,2,4,16,3072]{6,5,4,3,2,1,0:T(8,128)(2,1)} fusion(bf16[1,2,4,2,4,16,3072]{6,5,4,3,2,1,0:T(8,128)(2,1)S(1)} %bitcast.364, bf16[1,2,4,2,4,16,3072]{6,5,4,3,2,1,0:T(8,128)(2,1)S(1)} %bitcast.367), kind=kLoop, calls=%fused_computation | loop fusion | flops 6291456 | bytes 25165824 | tf_op jit(solution)/shard_map/stack | solution.py:894
  274.6 5.1 %fusion.91 = bf16[1,1024,1,128]{1,3,2,0:T(8,128)(2,1)S(1)} fusion(bf16[1024,2,128]{2,0,1:T(8,128)(2,1)S(1)} %bitcast.394, f32[1,2,1024,1024]{2,3,1,0:T(8,128)} %copy-done.1, f32[2,1024]{1,0:T(2,128)S(1)} %log_add_fusion.1), kind=kOutput, calls=%fused_computation.108 | convolution fusion | flops 541196288 | bytes 9183232 | tf_op jit(solution)/shard_map/kgqs,qkgd->skd/dot_general | solution.py:744
  279.8 8.3 %fusion.4 = (f32[2,1024]{1,0:T(2,128)S(1)}, f32[1024,1024,2]{1,0,2:T(8,128)}) fusion(f32[1,2,1024,1024]{2,3,1,0:T(8,128)} %copy-done.1, f32[2,1024]{1,0:T(2,128)S(1)} %log_add_fusion.1, bf16[1024,128,1]{1,0,2:T(8,128)(2,1)S(1)} %bitcast.422, bf16[1024,2,128]{2,0,1:T(8,128)(2,1)S(1)} %bitcast.395), kind=kOutput, calls=%fused_computation.12 | convolution fusion | flops 543160320 | bytes 17580032 | tf_op jit(solution)/shard_map/qkgd,skd->kgqs/dot_general | solution.py:739
  289.7 4.8 fusion
  295.6 6.0 %all-to-all-start.7 = ((bf16[2,1024,1,128]{3,0,2,1:T(2,128)(2,1)}), bf16[2,1024,1,128]{3,0,2,1:T(2,128)(2,1)S(1)}, u32[]{:S(2)}, u32[]{:S(2)}) async-start(bf16[2,1024,1,128]{3,0,2,1:T(2,128)(2,1)} %copy.187), calls=%async_computation.7 | async-start | bytes 1048576 | tf_op jit(solution)/shard_map/all_to_all | solution.py:754
  301.7 7.3 %fusion.26 = bf16[2,1024,1024]{1,2,0:T(8,128)(2,1)S(1)} fusion(f32[1024,1024,2]{1,0,2:T(8,128)} %get-tuple-element.108, f32[1,2,1024,1024]{2,3,1,0:T(8,128)} %copy-done.1, f32[2,1024]{1,0:T(2,128)S(1)} %get-tuple-element.107, f32[2,1024]{1,0:T(2,128)S(1)} %log_add_fusion.1), kind=kLoop, calls=%fused_computation.42 | loop fusion | flops 10485760 | bytes 20987904 | tf_op jit(solution)/shard_map/reshape.66
  324.2 5.7 %all-to-all-start.6 = ((bf16[2,1024,1,128]{3,0,2,1:T(2,128)(2,1)}), bf16[2,1024,1,128]{3,0,2,1:T(2,128)(2,1)S(1)}, u32[]{:S(2)}, u32[]{:S(2)}) async-start(bf16[2,1024,1,128]{3,0,2,1:T(2,128)(2,1)} %copy.181), calls=%async_computation.6 | async-start | bytes 1048576 | tf_op jit(solution)/shard_map/all_to_all | solution.py:754
  352.0 6.6 %copy.190 = bf16[1024,2048]{1,0:T(8,128)(2,1)} copy(bf16[1024,2048]{0,1:T(8,128)(2,1)} %pad_maximum_fusion.3) | data formatting | bytes 8388608 | tf_op jit(solution)/shard_map/concatenate | solution.py:888
  358.5 5.9 %copy.176 = f32[2,8,128,2,128]{2,0,4,3,1:T(2,128)} copy(bf16[2,8,128,2,128]{4,3,0,2,1:T(2,128)(2,1)} %bitcast.141) | data formatting | bytes 3145728 | tf_op jit(solution)/shard_map/convert_element_type | solution.py:809
  377.5 6.2 %pad_maximum_fusion.1.refs_0_ = bf16[2,2,4,2,4,16,2048]{6,5,4,3,2,1,0:T(8,128)(2,1)} fusion(bf16[1,2,4,2,4,16,2048]{6,5,4,3,2,1,0:T(8,128)(2,1)} %bitcast.374, bf16[1,2,4,2,4,16,2048]{6,5,4,3,2,1,0:T(8,128)(2,1)S(1)} %bitcast.368), kind=kLoop, calls=%fused_computation.1 | loop fusion | flops 4194304 | bytes 16777216 | tf_op jit(solution)/shard_map/stack | solution.py:894
  384.3 103.0 %reduce_grads.1 = (bf16[2,4,16,2048]{3,2,1,0:T(8,128)(2,1)}, bf16[2,4,32,512]{3,2,1,0:T(8,128)(2,1)}, bf16[2,4,16,3072]{3,2,1,0:T(8,128)(2,1)}, bf16[2,4,48,512]{3,2,1,0:T(8,128)(2,1)}, f32[24,128]{1,0:T(8,128)}) custom-call(bf16[2,2,4,2,4,16,2048]{6,5,4,3,2,1,0:T(8,128)(2,1)} %pad_maximum_fusion.1.refs_0_, ...), custom_call_target="tpu_custom_call" | custom-call | tf_op jit(solution)/shard_map/reduce_grads/pallas_call | solution.py:648
  (290 shorter events, 171.3 us)
Async XLA Ops:
  93.9 10.4 %copy-start.51 = (f32[128]{0:T(128)}, f32[128]{0:T(128)S(1)}, u32[]{:S(2)}) copy-start(f32[128]{0:T(128)S(1)} %get-tuple-element.43) | copy-start | bytes 1540
  93.9 33.1 %copy-start.46 = (f32[8,128]{1,0:T(8,128)}, f32[8,128]{1,0:T(8,128)S(1)}, u32[]{:S(2)}) copy-start(f32[8,128]{1,0:T(8,128)S(1)} %get-tuple-element.44) | copy-start | bytes 12292
  93.9 36.6 %copy-start.53 = (f32[128]{0:T(128)}, f32[128]{0:T(128)S(1)}, u32[]{:S(2)}) copy-start(f32[128]{0:T(128)S(1)} %get-tuple-element.42) | copy-start | bytes 1540
  95.2 31.8 %copy-start.55 = (f32[256]{0:T(256)}, f32[256]{0:T(256)S(1)}, u32[]{:S(2)}) copy-start(f32[256]{0:T(256)S(1)} %get-tuple-element.93) | copy-start | bytes 3076
  102.1 18.8 %copy-start.9 = (bf16[2,128,1024]{2,1,0:T(8,128)(2,1)}, bf16[2,128,1024]{2,1,0:T(8,128)(2,1)S(1)}, u32[]{:S(2)}) copy-start(bf16[2,128,1024]{2,1,0:T(8,128)(2,1)S(1)} %fusion.103) | copy-start | bytes 1572868
  104.3 26.2 %copy-start.16 = (f32[256,128]{0,1:T(8,128)}, f32[256,128]{0,1:T(8,128)S(1)}, u32[]{:S(2)}) copy-start(f32[256,128]{0,1:T(8,128)S(1)} %get-tuple-element.110) | copy-start | bytes 393220
  104.3 26.2 %copy-start.18 = (f32[256,128]{0,1:T(8,128)}, f32[256,128]{0,1:T(8,128)S(1)}, u32[]{:S(2)}) copy-start(f32[256,128]{0,1:T(8,128)S(1)} %get-tuple-element.111) | copy-start | bytes 393220
  105.5 28.1 %all-to-all-start.1 = ((bf16[2,128,8,128]{1,0,3,2:T(2,128)(2,1)}), bf16[2,128,8,128]{1,0,3,2:T(2,128)(2,1)}, u32[]{:S(2)}, u32[]{:S(2)}) async-start(bf16[2,128,8,128]{1,0,3,2:T(2,128)(2,1)} %reshape_reshape.8), calls=%async_computation.1 | async-start | bytes 1048576 | tf_op jit(solution)/shard_map/all_to_all | solution.py:750
  129.5 9.9 %copy-start.59 = (s32[2]{0:T(128)S(1)}, s32[2]{0:T(128)}, u32[]{:S(2)}) copy-start(s32[2]{0:T(128)} %param.17) | copy-start | bytes 28
  133.6 20.6 %copy-start.29 = (bf16[2,128,1024]{2,1,0:T(8,128)(2,1)S(1)}, bf16[2,128,1024]{2,1,0:T(8,128)(2,1)}, u32[]{:S(2)}) copy-start(bf16[2,128,1024]{2,1,0:T(8,128)(2,1)} %param.16) | copy-start | bytes 1572868
  133.6 15.6 %all-to-all-start = ((bf16[2,128,8,128]{3,1,0,2:T(8,128)(2,1)}), bf16[2,128,8,128]{3,1,0,2:T(8,128)(2,1)S(1)}, u32[]{:S(2)}, u32[]{:S(2)}) async-start(bf16[2,128,8,128]{3,1,0,2:T(8,128)(2,1)} %copy.155), calls=%async_computation | async-start | bytes 1048576 | tf_op jit(solution)/shard_map/all_to_all | solution.py:750
  149.3 18.9 %all-to-all-start.2 = ((bf16[2,128,16,128]{1,0,3,2:T(2,128)(2,1)}), bf16[2,128,16,128]{1,0,3,2:T(2,128)(2,1)S(1)}, u32[]{:S(2)}, u32[]{:S(2)}) async-start(bf16[2,128,16,128]{1,0,3,2:T(2,128)(2,1)} %reshape_reshape.9), calls=%async_computation.2 | async-start | bytes 2097152 | tf_op jit(solution)/shard_map/all_to_all | solution.py:750
  160.2 20.9 %copy-start.31 = (bf16[1,8,128,1,128]{4,2,0,1,3:T(8,128)(2,1)}, bf16[1,8,128,1,128]{4,2,0,1,3:T(8,128)(2,1)S(1)}, u32[]{:S(2)}) copy-start(bf16[1,8,128,1,128]{4,2,0,1,3:T(8,128)(2,1)S(1)} %get-tuple-element.75) | copy-start | bytes 786436
  187.2 18.2 %all-to-all-start.3 = ((bf16[2,1024,2,128]{3,2,0,1:T(2,128)(2,1)}), bf16[2,1024,2,128]{3,2,0,1:T(2,128)(2,1)S(1)}, u32[]{:S(2)}, u32[]{:S(2)}) async-start(bf16[2,1024,2,128]{3,2,0,1:T(2,128)(2,1)} %copy.165), calls=%async_computation.3 | async-start | bytes 2097152 | tf_op jit(solution)/shard_map/all_to_all | solution.py:754
  211.1 12.1 %slice-start.12 = ((s8[12582912]{0:T(1024)(128)(4,1)}), s8[4194304]{0:T(1024)(128)(4,1)S(1)}, s32[]{:S(2)}) async-start(s8[12582912]{0:T(1024)(128)(4,1)} %bitcast.449), calls=%async_computation.20 | async-start | bytes 8388608
  245.2 28.0 %all-to-all-start.4 = ((bf16[2,128,16,128]{3,1,0,2:T(8,128)(2,1)}), bf16[2,128,16,128]{3,1,0,2:T(8,128)(2,1)}, u32[]{:S(2)}, u32[]{:S(2)}) async-start(bf16[2,128,16,128]{3,1,0,2:T(8,128)(2,1)} %copy.167), calls=%async_computation.4 | async-start | bytes 2097152 | tf_op jit(solution)/shard_map/all_to_all | solution.py:750
  274.6 13.4 %slice-start = ((s8[8388608]{0:T(1024)(128)(4,1)}), s8[4194304]{0:T(1024)(128)(4,1)S(1)}, s32[]{:S(2)}) async-start(s8[8388608]{0:T(1024)(128)(4,1)} %bitcast.356), calls=%async_computation.8 | async-start | bytes 8388608
  295.6 28.5 %all-to-all-start.7 = ((bf16[2,1024,1,128]{3,0,2,1:T(2,128)(2,1)}), bf16[2,1024,1,128]{3,0,2,1:T(2,128)(2,1)S(1)}, u32[]{:S(2)}, u32[]{:S(2)}) async-start(bf16[2,1024,1,128]{3,0,2,1:T(2,128)(2,1)} %copy.187), calls=%async_computation.7 | async-start | bytes 1048576 | tf_op jit(solution)/shard_map/all_to_all | solution.py:754
  301.7 11.1 %slice-start.3 = ((s8[8388608]{0:T(1024)(128)(4,1)}), s8[4194304]{0:T(1024)(128)(4,1)S(1)}, s32[]{:S(2)}) async-start(s8[8388608]{0:T(1024)(128)(4,1)} %bitcast.358), calls=%async_computation.11 | async-start | bytes 8388608
  301.7 12.3 %slice-start.5 = ((s8[8388608]{0:T(1024)(128)(4,1)}), s8[4194304]{0:T(1024)(128)(4,1)S(1)}, s32[]{:S(2)}) async-start(s8[8388608]{0:T(1024)(128)(4,1)} %bitcast.360), calls=%async_computation.13 | async-start | bytes 8388608
  320.0 9.8 %copy-start.37 = (bf16[1,8,128,1,128]{4,2,1,3,0:T(8,128)(2,1)S(1)}, bf16[1,8,128,1,128]{4,2,1,3,0:T(8,128)(2,1)}, u32[]{:S(2)}) copy-start(bf16[1,8,128,1,128]{4,2,1,3,0:T(8,128)(2,1)} %copy.163) | copy-start | bytes 786436
  324.2 13.9 %all-to-all-start.6 = ((bf16[2,1024,1,128]{3,0,2,1:T(2,128)(2,1)}), bf16[2,1024,1,128]{3,0,2,1:T(2,128)(2,1)S(1)}, u32[]{:S(2)}, u32[]{:S(2)}) async-start(bf16[2,1024,1,128]{3,0,2,1:T(2,128)(2,1)} %copy.181), calls=%async_computation.6 | async-start | bytes 1048576 | tf_op jit(solution)/shard_map/all_to_all | solution.py:754
  335.0 11.8 %copy-start.19 = (f32[256,128]{0,1:T(8,128)S(1)}, f32[256,128]{0,1:T(8,128)}, u32[]{:S(2)}) copy-start(f32[256,128]{0,1:T(8,128)} %copy-done.18) | copy-start | bytes 393220
  338.1 20.5 %all-to-all-start.5 = ((bf16[2,1024,2,128]{3,2,0,1:T(2,128)(2,1)}), bf16[2,1024,2,128]{3,2,0,1:T(2,128)(2,1)}, u32[]{:S(2)}, u32[]{:S(2)}) async-start(bf16[2,1024,2,128]{3,2,0,1:T(2,128)(2,1)} %copy.175), calls=%async_computation.5 | async-start | bytes 2097152 | tf_op jit(solution)/shard_map/all_to_all | solution.py:754
  (60 other events, 244.4 us)

commit v3 on v2

--- a/solution.py
+++ b/solution.py
@@ -249,99 +249,6 @@
             self.copy(step).wait_send()
 
 
-ORDER = (
-    (0, 0),
-    (0, 1),
-    (1, 0),
-    (2, 0),
-    (0, 2),
-    (3, 0),
-    (1, 1),
-    (4, 0),
-    (2, 1),
-    (5, 0),
-    (3, 1),
-    (0, 3),
-    (1, 2),
-    (4, 1),
-    (6, 0),
-    (2, 2),
-    (5, 1),
-    (3, 2),
-    (1, 3),
-    (4, 2),
-    (6, 1),
-    (2, 3),
-    (5, 2),
-    (3, 3),
-    (4, 3),
-    (6, 2),
-    (5, 3),
-    (6, 3),
-    (7, 0),
-    (7, 1),
-    (7, 2),
-    (7, 3),
-)
-
-
-def gather_kernel(*refs):
-    shards, small = refs[:7], refs[7]
-    buffers, small_all = refs[8:12], refs[12]
-    send_sem, recv_sem, small_send, small_recv, local_sem = refs[13:]
-    place = Place()
-    copies = [
-        pltpu.make_async_copy(shard, there, local_sem.at[at])
-        for at, (shard, there) in enumerate(
-            zip(shards + (small,), own_places(place, buffers) + (small_all.at[place.y_hi, place.z, place.core],))
-        )
-    ]
-    for copy in copies:
-        copy.start()
-    greet(place.torus())
-    for copy in copies:
-        copy.wait()
-    gather = Gather(place, buffers, send_sem, recv_sem)
-    little = GatherSmall(place, small_all, small_send, small_recv)
-    little.start(0)
-    gather.phase(0, 0)
-    little.take(0)
-    little.start(1)
-    gather.phase(0, 1)
-    little.take(1)
-    little.start(2)
-    little.start(3)
-    little.take(2)
-    little.take(3)
-    little.start(4)
-    for number, g in ORDER[2:]:
-        gather.phase(number, g)
-    little.take(4)
-    gather.finish()
-    little.finish()
-
-
-def gather_all(shards, small):
-    shapes = [
-        jax.ShapeDtypeStruct((2, 4, 2, rows, cols), bf16) for rows, cols in zip(SHARD_ROWS, COLUMNS)
-    ] + [jax.ShapeDtypeStruct((2, 4, 2, 16, 128), bf16)]
-    return pl.pallas_call(
-        functools.partial(gather_kernel),
-        out_shape=shapes,
-        in_specs=[pl.BlockSpec(memory_space=pltpu.VMEM)] * 8,
-        out_specs=[pl.BlockSpec(memory_space=pl.ANY)] * 5,
-        scratch_shapes=[
-            pltpu.SemaphoreType.DMA((4, KINDS)),
-            pltpu.SemaphoreType.DMA((4, KINDS)),
-            pltpu.SemaphoreType.DMA((5,)),
-            pltpu.SemaphoreType.DMA((5,)),
-            pltpu.SemaphoreType.DMA((8,)),
-        ],
-        compiler_params=pltpu.CompilerParams(collective_id=1, has_side_effects=True),
-        name="gather_weights",
-    )(*shards, small)
-
-
 PART_ORDER = ("xyz", "yzx", "zxy")
 FREE = ((("yl", "yh", "z"), ("z",), ()), (("z", "x"), ("x",), ()), (("yl", "yh", "x"), ("yl", "yh"), ()))
 EXTENT = {"yl": 2, "yh": 2, "z": 4, "x": 4}
@@ -361,7 +268,6 @@
     shapes = []
     for g in range(4):
         rows, half = SHARD_ROWS[g] // 4, COLUMNS[g] // 2
-        shapes.append(pltpu.VMEM((2, 2, 4, 4, rows, half), bf16))
         shapes.append(pltpu.VMEM((2, 2, 4, 4, rows, half), bf16))
         shapes.append(pltpu.VMEM((2, 4, rows, half), bf16))
         for part in range(3):
@@ -375,8 +281,7 @@
     return shapes
 
 
-SCRATCH_PER_GROUP = 3 + 18
-REDUCE_SEMS = 3 * 12 + 1 + 1 + 2 + 2
+SCRATCH_PER_GROUP = 2 + 18
 
 
 def accumulate(dst, src):
@@ -410,17 +315,14 @@
     def total(self, g):
         return self.groups[g][0]
 
-    def from_core(self, g):
+    def result(self, g):
         return self.groups[g][1]
 
-    def result(self, g):
-        return self.groups[g][2]
-
     def halves(self, g, part, step):
+        return self.groups[g][2 + (part * 3 + step) * 2]
+
+    def nears(self, g, part, step):
         return self.groups[g][3 + (part * 3 + step) * 2]
-
-    def nears(self, g, part, step):
-        return self.groups[g][4 + (part * 3 + step) * 2]
 
     def cols(self, g, part):
         return pl.ds(sum(THIRDS[g][:part]), THIRDS[g][part])
@@ -466,18 +368,8 @@
     def take(self, g, sem, dst):
         self.remote(g, sem, dst, dst, self.place.to_core).wait_recv()
 
-    def begin(self, g):
-        p = self.place
-        self.send(g, 36, self.grads[g].at[:, :, :, 1 - p.core], self.from_core(g), p.to_core)
-        self.load(g).start()
-
     def load(self, g):
-        return pltpu.make_async_copy(self.grads[g].at[:, :, :, self.place.core], self.total(g), self.load_sem.at[g])
-
-    def join_cores(self, g):
-        self.load(g).wait()
-        self.take(g, 36, self.from_core(g))
-        accumulate(self.total(g), self.from_core(g))
+        return pltpu.make_async_copy(self.grads[g], self.total(g), self.load_sem.at[g])
 
     def send_far(self, g, step):
         for part in range(3):
@@ -514,7 +406,7 @@
         p = self.place
         result = self.result(g)
         if number == 0:
-            self.join_cores(g)
+            self.load(g).wait()
             self.send_far(g, 0)
         elif number in (1, 3, 5):
             self.send_near(g, number // 2)
@@ -602,239 +494,759 @@
         return total
 
 
-REDUCE_ORDER = (3, 2, 1, 0)
-
-
-def reduce_kernel(*refs):
-    grads, small = refs[:4], refs[4]
-    outs, small_out = refs[5:9], refs[9]
-    scratch = refs[10 : 10 + 4 * SCRATCH_PER_GROUP]
-    slots, send_sem, recv_sem, load_sem, small_send, small_recv, out_sem = refs[10 + 4 * SCRATCH_PER_GROUP :]
+SCALE = 128 ** (-0.5)
+OFFSETS = tuple((dx, dy) for dx in range(4) for dy in range(2) if (dx, dy) != (0, 0))
+
+
+def mm(left, right):
+    return jnp.dot(left, right, preferred_element_type=f32)
+
+
+def mm_nt(left, right):
+    return lax.dot_general(left, right, (((1,), (1,)), ((), ())), preferred_element_type=f32)
+
+
+def mm_tn(left, right):
+    return lax.dot_general(left, right, (((0,), (0,)), ((), ())), preferred_element_type=f32)
+
+
+def inv_rms(v):
+    return lax.rsqrt(jnp.mean(v * v, axis=-1, keepdims=True) + epsilon)
+
+
+class Exchange:
+    def __init__(self, place, send_sem, recv_sem):
+        self.place, self.send_sem, self.recv_sem, self.sent = place, send_sem, recv_sem, []
+
+    def partner(self, at, back=False):
+        dx, dy = OFFSETS[at]
+        x = (self.place.x + (4 - dx if back else dx)) % 4
+        return x * 2 + (self.place.y_lo + dy) % 2
+
+    def send(self, kind, src, dst):
+        for at in range(7):
+            partner = self.partner(at)
+            copy = pltpu.make_async_remote_copy(
+                src_ref=src(partner),
+                dst_ref=dst(self.place.seq),
+                send_sem=self.send_sem.at[kind, at],
+                recv_sem=self.recv_sem.at[kind, at],
+                device_id=(self.place.dp, partner),
+                device_id_type=MESH,
+            )
+            copy.start()
+            self.sent.append(copy)
+
+    def take(self, kind, dst):
+        for at in range(7):
+            partner = self.partner(at, back=True)
+            pltpu.make_async_remote_copy(
+                src_ref=dst(partner),
+                dst_ref=dst(partner),
+                send_sem=self.send_sem.at[kind, at],
+                recv_sem=self.recv_sem.at[kind, at],
+                device_id=(self.place.dp, partner),
+                device_id_type=MESH,
+            ).wait_recv()
+
+    def finish(self):
+        for copy in self.sent:
+            copy.wait_send()
+        self.sent = []
+
+
+def token_rows(seq):
+    return pl.ds(pl.multiple_of(seq * 128, 128), 128)
+
+
+def head_cols(seq, width):
+    return pl.ds(pl.multiple_of(seq * width, 128), width)
+
+
+def gain_rows(tile_ref):
+    tiles = tile_ref[...].astype(f32).reshape(8, 2, 16, 128)
+    pairs = tiles[:, 0] + tiles[:, 1]
+    total = pairs[0]
+    for at in range(1, 8):
+        total = total + pairs[at]
+
+    def wide(row):
+        return jnp.concatenate([pairs[at, row : row + 1, :] for at in range(8)], axis=-1)
+
+    return wide(0), total[1:2, :], total[2:3, :], wide(3)
+
+
+def causal_scores(q, k, first):
+    scores = mm_nt(q, k) * SCALE
+    row = first + lax.broadcasted_iota(jnp.int32, scores.shape, 0)
+    col = lax.broadcasted_iota(jnp.int32, scores.shape, 1)
+    return jnp.where(col <= row, scores, -1e30)
+
+
+FORWARD_IN = (
+    "w_query", "w_key", "w_value", "w_output", "w_gate", "w_up", "w_down", "gains",
+    "hidden", "cot", "cos", "sin", "valid",
+)
+FORWARD_OUT = (
+    "out", "d_residual", "d_attended", "dg_ffn", "x_in", "q_flat", "k_flat",
+    "total_output", "total_gate_up", "total_down", "weights_qkv", "q_heads", "k_heads", "v_heads", "gain_tiles",
+)
+FORWARD_SCRATCH = (
+    "buf_qkv", "buf_output", "buf_gate_up", "buf_down", "tiles", "rows", "core_down",
+    "q_in", "k_in", "v_in", "att", "context", "residual", "mid_in", "result", "d_mid", "d_branch",
+    "gather_send", "gather_recv", "small_send", "small_recv", "local_sem", "swap_send", "swap_recv", "out_sem",
+    "core_free", "core_send", "core_recv",
+)
+FF_TILE = 768
+
+
+def forward_kernel(*refs):
+    r = dict(zip(FORWARD_IN + FORWARD_OUT + FORWARD_SCRATCH, refs))
     place = Place()
+    me = place.seq
+    buffers = [r["buf_qkv"], r["buf_output"], r["buf_gate_up"], r["buf_down"]]
+    tiles = r["tiles"]
+    sources = [r[name] for name in FORWARD_IN[:8]]
+    copies = [
+        pltpu.make_async_copy(shard, there, r["local_sem"].at[at])
+        for at, (shard, there) in enumerate(
+            zip(sources, own_places(place, buffers) + (tiles.at[place.y_hi, place.z, place.core],))
+        )
+    ]
+    for copy in copies:
+        copy.start()
     greet(
         place.torus()
-        + (
-            (place.dp, (place.x + 2) % 4 * 2 + place.y_lo),
-            (place.y_hi * 8 + place.z_far * 2 + place.core, place.seq),
+        + tuple(
+            (place.dp, (place.x + dx) % 4 * 2 + (place.y_lo + dy) % 2)
+            for dx, dy in OFFSETS
+            if (dx, dy) not in ((1, 0), (3, 0), (0, 1))
         )
     )
-    reduce = Reduce(place, grads, scratch, send_sem, recv_sem, load_sem)
-    little = ReduceSmall(place, slots, small_send, small_recv)
-    for g in REDUCE_ORDER:
-        reduce.begin(g)
-    little.put(0, small[...])
-    for slot in range(4 + 9):
-        for stage in range(10):
-            if 0 <= slot - stage < 4:
-                reduce.stage(stage, REDUCE_ORDER[slot - stage])
-                if stage == 9:
-                    g = REDUCE_ORDER[slot - stage]
-                    pltpu.make_async_copy(reduce.result(g), outs[g], out_sem.at[g]).start()
-        if slot < 4:
-            little.put(slot + 1, little.sum(slot))
-        elif slot == 4:
-            small_out[...] = little.sum(4)
-    reduce.finish()
-    for g in range(4):
-        pltpu.make_async_copy(reduce.result(g), outs[g], out_sem.at[g]).wait()
-
-
-def reduce_all(grads, small):
-    shapes = [
-        jax.ShapeDtypeStruct((2, 4, rows // 4, cols // 2), bf16) for rows, cols in zip(SHARD_ROWS, COLUMNS)
-    ] + [jax.ShapeDtypeStruct((24, 128), f32)]
+    for copy in copies:
+        copy.wait()
+    gather = Gather(place, buffers, r["gather_send"], r["gather_recv"])
+    little = GatherSmall(place, tiles, r["small_send"], r["small_recv"])
+    swap = Exchange(place, r["swap_send"], r["swap_recv"])
+    saved = []
+
+    def save(name, src, dst=None):
+        at = len(saved)
+        copy = pltpu.make_async_copy(src, r[name] if dst is None else dst, r["out_sem"].at[at])
+        copy.start()
+        saved.append(copy)
+
+    def phases(*steps):
+        for number, g in steps:
+            gather.phase(number, g)
+
+    little.start(0)
+    phases((0, 0))
+    little.take(0)
+    little.start(1)
+    little.take(1)
+    little.start(2)
+    little.start(3)
+    little.take(2)
+    little.take(3)
+    little.start(4)
+    phases((1, 0), (0, 1), (2, 0), (3, 0), (0, 3), (4, 0), (5, 0), (1, 1), (6, 0))
+    little.take(4)
+    g_attn, g_query, g_key, g_ffn = gain_rows(tiles)
+    x = r["hidden"][...].reshape(256, 1024).astype(f32)
+    r["x_in"][...] = (x * inv_rms(x) * g_attn).astype(bf16)
+    phases((0, 2), (7, 0))
+    save("weights_qkv", buffers[0])
+    save("gain_tiles", tiles)
+
+    cos, sin = r["cos"], r["sin"]
+
+    def qkv_weights(first):
+        return buffers[0][:, :, :, :, pl.ds(pl.multiple_of(first, 128), 512)].reshape(1024, 512)
+
+    def head_tile(j, flat_ref, rows_ref, first, gain):
+        flat = mm(r["x_in"][...], qkv_weights(first + j * 512))
+        cols = pl.ds(pl.multiple_of(j * 512, 128), 512)
+        flat_ref[:, cols] = flat
+        done = []
+        for h in range(4):
+            v = flat[:, h * 128 : (h + 1) * 128]
+            v = v * inv_rms(v) * gain
+            done.append((v * cos[...] + pltpu.roll(v, 64, 1) * sin[...]).astype(bf16))
+        rows_ref[...] = jnp.concatenate(done, axis=-1).reshape(2, 128, 512)
+
+    def query_tile(j, carry):
+        head_tile(j, r["q_flat"], r["rows"].at[0, :, :, pl.ds(pl.multiple_of(j * 512, 128), 512)], 0, g_query)
+        return carry
+
+    def key_tile(j, carry):
+        head_tile(j, r["k_flat"], r["rows"].at[1, :, :, pl.ds(pl.multiple_of(j * 512, 128), 512)], 2048, g_key)
+        return carry
+
+    def value_tile(j, carry):
+        cols = pl.ds(pl.multiple_of(1024 + j * 512, 128), 512)
+        r["rows"][1, :, :, cols] = mm(r["x_in"][...], qkv_weights(3072 + j * 512)).astype(bf16).reshape(2, 128, 512)
+        return carry
+
+    def to_heads(kind, at, first, heads, width):
+        def cols(seq):
+            return pl.ds(pl.multiple_of(first + seq * width, 128), width)
+
+        swap.send(
+            kind,
+            lambda partner: r["rows"].at[at, :, :, cols(partner)],
+            lambda sender: r[heads].at[:, token_rows(sender), :],
+        )
+        r[heads][:, token_rows(me), :] = r["rows"][at, :, :, cols(me)]
+
+    lax.fori_loop(0, 4, query_tile, 0)
+    to_heads(0, 0, 0, "q_in", 256)
+    lax.fori_loop(0, 2, key_tile, 0)
+    to_heads(1, 1, 0, "k_in", 128)
+    lax.fori_loop(0, 2, value_tile, 0)
+    to_heads(2, 1, 1024, "v_in", 128)
+    phases((2, 1), (1, 3), (3, 1), (1, 2), (4, 1), (2, 3), (2, 2), (5, 1), (3, 3), (6, 1), (3, 2))
+    swap.take(0, lambda sender: r["q_in"].at[:, token_rows(sender), :])
+    swap.take(1, lambda sender: r["k_in"].at[:, token_rows(sender), :])
+    swap.take(2, lambda sender: r["v_in"].at[:, token_rows(sender), :])
+    save("q_heads", r["q_in"])
+    save("k_heads", r["k_in"])
+    save("v_heads", r["v_in"])
+
+    def attend(slot, head):
+        cols = slice(head * 128, (head + 1) * 128)
+        for block in range(4):
+            rows, upto = slice(block * 256, (block + 1) * 256), (block + 1) * 256
+            q = r["q_in"][slot, rows, cols]
+            scores = causal_scores(q, r["k_in"][slot, :upto, :], block * 256)
+            top = jnp.max(scores, axis=-1, keepdims=True)
+            shifted = jnp.exp(scores - top)
+            total = jnp.sum(shifted, axis=-1, keepdims=True)
+            prob = (shifted * (1.0 / total)).astype(bf16)
+            r["att"][slot, rows, cols] = mm(prob, r["v_in"][slot, :upto, :]).astype(bf16)
+
+    for slot in range(2):
+        attend(slot, 0)
+        attend(slot, 1)
+        swap.send(
+            3 + slot,
+            lambda partner: r["att"].at[slot, token_rows(partner), :],
+            lambda sender: r["context"].at[slot, :, head_cols(sender, 256)],
+        )
+        r["context"][slot, :, head_cols(me, 256)] = r["att"][slot, token_rows(me), :]
+        if slot == 0:
+            phases((4, 3), (4, 2))
+    phases((7, 1), (5, 3), (5, 2), (6, 3), (6, 2))
+    for slot in range(2):
+        swap.take(3 + slot, lambda sender: r["context"].at[slot, :, head_cols(sender, 256)])
+
+    for half in range(2):
+        cols = slice(half * 512, (half + 1) * 512)
+        weights = buffers[1][:, :, :, :, cols].reshape(2048, 512)
+        x = r["hidden"][:, :, cols].reshape(256, 512).astype(f32)
+        r["residual"][:, cols] = x + mm(r["context"][...].reshape(256, 2048), weights)
+    residual = r["residual"][...]
+    r["mid_in"][...] = (residual * inv_rms(residual) * g_ffn).astype(bf16)
+    d_result = jnp.where(r["valid"][...] > 0.5, r["cot"][...].reshape(256, 1024).astype(f32), 0.0)
+    r["d_branch"][...] = d_result.astype(bf16)
+    phases((7, 2), (7, 3))
+    gather.finish()
+    little.finish()
+    swap.finish()
+    for copy in saved:
+        copy.wait()
+    saved.clear()
+    pl.semaphore_signal(r["core_free"], inc=1, device_id=place.to_core, device_id_type=MESH)
+    pl.semaphore_wait(r["core_free"], 1)
+    core, other = place.core, 1 - place.core
+
+    def to_core(src, dst, *at):
+        return pltpu.make_async_remote_copy(
+            src_ref=src,
+            dst_ref=dst,
+            send_sem=r["core_send"].at[at],
+            recv_sem=r["core_recv"].at[at],
+            device_id=place.to_core,
+            device_id_type=MESH,
+        )
+
+    def ffn_copies(f):
+        here = pl.ds(pl.multiple_of(f * FF_TILE, 128), FF_TILE)
+        up = pl.ds(pl.multiple_of(3072 + f * FF_TILE, 128), FF_TILE)
+        y, z = f // 2, pl.ds(f % 2 * 2, 2)
+        return (
+            to_core(buffers[2].at[:, :, other, :, here], buffers[0].at[:, :, 0, :, here], f, 0),
+            to_core(buffers[2].at[:, :, other, :, up], buffers[0].at[:, :, 1, :, here], f, 1),
+            to_core(buffers[3].at[y, z, other], r["core_down"].at[y, z], f, 2),
+        )
+
+    def ffn_join(f):
+        here = pl.ds(pl.multiple_of(f * FF_TILE, 128), FF_TILE)
+        up = pl.ds(pl.multiple_of(3072 + f * FF_TILE, 128), FF_TILE)
+        y, z = f // 2, pl.ds(f % 2 * 2, 2)
+        for copy in ffn_copies(f):
+            copy.wait_recv()
+        buffers[2][:, :, core, :, here] = buffers[2][:, :, core, :, here] + buffers[0][:, :, 0, :, here]
+        buffers[2][:, :, core, :, up] = buffers[2][:, :, core, :, up] + buffers[0][:, :, 1, :, here]
+        buffers[3][y, z, core] = buffers[3][y, z, core] + r["core_down"][y, z]
+
+    r["result"][...] = residual
+    r["d_mid"][...] = jnp.zeros((256, 1024), f32)
+
+    def ffn_tile(f, carry):
+        def weights(first):
+            cols = pl.ds(pl.multiple_of(first + f * FF_TILE, 128), FF_TILE)
+            return cols, buffers[2][:, :, :, :, cols].reshape(1024, FF_TILE)
+
+        gate_cols, w_gate = weights(0)
+        up_cols, w_up = weights(3072)
+        y, z = f // 2, pl.ds(f % 2 * 2, 2)
+        w_down = buffers[3][y, z].reshape(FF_TILE, 1024)
+        mid, d_branch = r["mid_in"][...], r["d_branch"][...]
+        gate, up = mm(mid, w_gate), mm(mid, w_up)
+        sig = 1.0 / (1.0 + jnp.exp(-gate))
+        silu = gate * sig
+        unit = (silu * up).astype(bf16)
+        d_unit = mm_nt(d_branch, w_down)
+        d_gate = (d_unit * up * (sig * (1.0 + gate * (1.0 - sig)))).astype(bf16)
+        d_up = (d_unit * silu).astype(bf16)
+        r["result"][...] += mm(unit, w_down)
+        r["d_mid"][...] += mm_nt(d_gate, w_gate) + mm_nt(d_up, w_up)
+        shape = (4, 2, 64, FF_TILE)
+        for part in range(2):
+            mid_part = mid[:, part * 512 : (part + 1) * 512]
+            buffers[2][part, :, :, :, gate_cols] = mm_tn(mid_part, d_gate).astype(bf16).reshape(shape)
+            buffers[2][part, :, :, :, up_cols] = mm_tn(mid_part, d_up).astype(bf16).reshape(shape)
+        buffers[3][y, z] = mm_tn(unit, d_branch).astype(bf16).reshape(2, 2, 192, 1024)
+        for copy in ffn_copies(f):
+            copy.start()
+
+        @pl.when(f > 0)
+        def _():
+            ffn_join(f - 1)
+
+        return carry
+
+    lax.fori_loop(0, 3072 // FF_TILE, ffn_tile, 0)
+    valid = r["valid"][...] > 0.5
+    r["out"][...] = jnp.where(valid, r["result"][...], 0.0).astype(bf16).reshape(2, 128, 1024)
+
+    residual, d_mid = r["residual"][...], r["d_mid"][...]
+    scale = inv_rms(residual)
+    weighed = g_ffn * d_mid
+    d_norm = scale * weighed - residual * (scale * scale * scale) * jnp.mean(
+        residual * weighed, axis=-1, keepdims=True
+    )
+    r["dg_ffn"][...] = jnp.sum(d_mid * residual * scale, axis=0, keepdims=True)
+    d_result = jnp.where(valid, r["cot"][...].reshape(256, 1024).astype(f32), 0.0)
+    r["d_residual"][...] = d_result + d_norm
+    r["d_branch"][...] = r["d_residual"][...].astype(bf16)
+
+    def output_tile(j, carry):
+        y, z = j // 2, j % 2 * 2
+        cols = pl.ds(pl.multiple_of(j * 512, 128), 512)
+        d_attn = r["d_branch"][...]
+        weights = buffers[1][y, pl.ds(z, 2)].reshape(512, 1024)
+        r["d_attended"][:, :, cols] = mm_nt(d_attn, weights).astype(bf16).reshape(2, 128, 512)
+        context = r["context"][:, :, cols].reshape(256, 512)
+        buffers[1][y, pl.ds(z, 2)] = mm_tn(context, d_attn).astype(bf16).reshape(2, 2, 128, 1024)
+        for copy in output_copies(j):
+            copy.start()
+        return carry
+
+    def output_copies(j):
+        y, z = j // 2, j % 2
+        return tuple(
+            to_core(
+                buffers[1].at[y, z * 2 + k, other],
+                r["rows"].at[y, z, :, pl.ds(k * 1024, 1024)],
+                4 + j,
+                k,
+            )
+            for k in range(2)
+        )
+
+    lax.fori_loop(0, 4, output_tile, 0)
+    ffn_join(3)
+    for half in range(2):
+        save("total_gate_up", buffers[2].at[:, :, core, :, pl.ds(half * 3072, 3072)], r["total_gate_up"].at[half])
+        save("total_down", buffers[3].at[:, :, core, :, pl.ds(half * 512, 512)], r["total_down"].at[half])
+
+    def output_join(j, carry):
+        y, z = j // 2, j % 2
+        for k, copy in enumerate(output_copies(j)):
+            copy.wait_recv()
+            cols = slice(k * 1024, (k + 1) * 1024)
+            buffers[1][y, z * 2 + k, core] = buffers[1][y, z * 2 + k, core] + r["rows"][y, z, :, cols]
+        return carry
+
+    lax.fori_loop(0, 4, output_join, 0)
+    for half in range(2):
+        save("total_output", buffers[1].at[:, :, core, :, pl.ds(half * 512, 512)], r["total_output"].at[half])
+    for at in range(4):
+        for copy in ffn_copies(at) + output_copies(at):
+            copy.wait_send()
+    for copy in saved:
+        copy.wait()
+
+
+def forward(shards, gains, hidden, cot, cos, sin, valid):
+    def shape(*dims, dtype=bf16):
+        return jax.ShapeDtypeStruct(dims, dtype)
+
+    outs = {
+        "out": shape(2, 128, 1024),
+        "d_residual": shape(256, 1024, dtype=f32),
+        "d_attended": shape(2, 128, 2048),
+        "dg_ffn": shape(1, 1024, dtype=f32),
+        "x_in": shape(256, 1024),
+        "q_flat": shape(256, 2048, dtype=f32),
+        "k_flat": shape(256, 1024, dtype=f32),
+        "total_output": shape(2, 2, 4, 128, 512),
+        "total_gate_up": shape(2, 2, 4, 64, 3072),
+        "total_down": shape(2, 2, 4, 192, 512),
+        "weights_qkv": shape(2, 4, 2, 64, 4096),
+        "q_heads": shape(2, 1024, 256),
+        "k_heads": shape(2, 1024, 128),
+        "v_heads": shape(2, 1024, 128),
+        "gain_tiles": shape(2, 4, 2, 16, 128),
+    }
     vmem = pl.BlockSpec(memory_space=pltpu.VMEM)
     hbm = pl.BlockSpec(memory_space=pl.ANY)
-    return pl.pallas_call(
-        functools.partial(reduce_kernel),
-        out_shape=shapes,
-        in_specs=[hbm] * 4 + [vmem],
-        out_specs=[hbm] * 4 + [vmem],
-        scratch_shapes=reduce_scratch()
-        + [
-            pltpu.VMEM((5, 4, 24, 128), f32),
-            pltpu.SemaphoreType.DMA((4, REDUCE_SEMS)),
-            pltpu.SemaphoreType.DMA((4, REDUCE_SEMS)),
-            pltpu.SemaphoreType.DMA((4,)),
-            pltpu.SemaphoreType.DMA((5, 3)),
-            pltpu.SemaphoreType.DMA((5, 3)),
-            pltpu.SemaphoreType.DMA((4,)),
-        ],
+    scratch = {
+        "buf_qkv": (2, 4, 2, 64, 4096),
+        "buf_output": (2, 4, 2, 128, 1024),
+        "buf_gate_up": (2, 4, 2, 64, 6144),
+        "buf_down": (2, 4, 2, 192, 1024),
+        "tiles": (2, 4, 2, 16, 128),
+        "rows": (2, 2, 128, 2048),
+        "core_down": (2, 4, 192, 1024),
+        "q_in": (2, 1024, 256),
+        "k_in": (2, 1024, 128),
+        "v_in": (2, 1024, 128),
+        "att": (2, 1024, 256),
+        "context": (2, 128, 2048),
+        "residual": ((256, 1024), f32),
+        "mid_in": (256, 1024),
+        "result": ((256, 1024), f32),
+        "d_mid": ((256, 1024), f32),
+        "d_branch": (256, 1024),
+    }
+    dma = pltpu.SemaphoreType.DMA
+    sems = [dma((4, KINDS)), dma((4, KINDS)), dma((5,)), dma((5,)), dma((8,)), dma((5, 7)), dma((5, 7)), dma((6,))]
+    sems += [pltpu.SemaphoreType.REGULAR, dma((8, 3)), dma((8, 3))]
+    buffers = [
+        pltpu.VMEM(*(dims if isinstance(dims[0], tuple) else (dims, bf16))) for dims in scratch.values()
+    ]
+    results = pl.pallas_call(
+        functools.partial(forward_kernel),
+        out_shape=list(outs.values()),
+        in_specs=[vmem] * 13,
+        out_specs=[vmem] * 7 + [hbm] * 8,
+        scratch_shapes=buffers + sems,
         compiler_params=pltpu.CompilerParams(
-            collective_id=2, has_side_effects=True, vmem_limit_bytes=60 * 1024 * 1024
+            collective_id=1, has_side_effects=True, vmem_limit_bytes=63 * 1024 * 1024
         ),
-        name="reduce_grads",
-    )(*grads, small)
-
-
-def product(left, right):
-    return jnp.dot(left, right, preferred_element_type=f32)
-
-
-def cross_rows(left, right):
-    return lax.dot_general(left, right, (((0,), (0,)), ((), ())), preferred_element_type=f32)
-
-
-def times_trans(left, right):
-    return lax.dot_general(left, right, (((1,), (1,)), ((), ())), preferred_element_type=f32)
-
-
-def rotary_tables(positions, width):
-    half = width // 2
-    frequency = jnp.exp(jnp.arange(half, dtype=f32) * (-2.0 * math.log(rope_base) / width))
+        name="forward",
+    )(*shards, gains, hidden, cot, cos, sin, valid)
+    return dict(zip(outs, results))
+
+
+BACKWARD_IN = (
+    "total_output", "total_gate_up", "total_down", "weights_qkv", "d_attended", "q_heads", "k_heads", "v_heads",
+    "q_flat", "k_flat", "x_in", "hidden", "d_residual", "cos", "sin", "gain_tiles", "dg_ffn",
+)
+BACKWARD_OUT = ("d_input", "gains_sum", "sum_qkv", "sum_output", "sum_gate_up", "sum_down")
+BACKWARD_SCRATCH = (
+    "buf_qkv", "q_in", "k_in", "v_in", "grad_in", "dq", "dk", "dv", "dk_sum", "dv_sum", "dq_rows", "dk_rows", "dv_rows",
+    "q_flat_in", "k_flat_in", "x_in_in", "d_x", "dg_query", "dg_key", "slots",
+    "reduce_send", "reduce_recv", "load_sem", "small_send", "small_recv", "out_sem", "swap_send", "swap_recv", "in_sem",
+)
+FAR_STAGES = 10
+
+
+def backward_kernel(*refs):
+    names = BACKWARD_IN + BACKWARD_OUT
+    count = 4 * SCRATCH_PER_GROUP
+    r = dict(zip(names, refs))
+    scratch = refs[len(names) : len(names) + count]
+    r.update(zip(BACKWARD_SCRATCH, refs[len(names) + count :]))
+    place = Place()
+    me = place.seq
+    loads = {
+        name: pltpu.make_async_copy(r[name], r[there], r["in_sem"].at[at])
+        for at, (name, there) in enumerate(
+            (
+                ("q_heads", "q_in"),
+                ("k_heads", "k_in"),
+                ("v_heads", "v_in"),
+                ("q_flat", "q_flat_in"),
+                ("k_flat", "k_flat_in"),
+                ("x_in", "x_in_in"),
+                ("weights_qkv", "buf_qkv"),
+            )
+        )
+    }
+    grads = (None, r["total_output"], r["total_gate_up"], r["total_down"])
+    outs = (r["sum_qkv"], r["sum_output"], r["sum_gate_up"], r["sum_down"])
+    reduce = Reduce(place, grads, scratch, r["reduce_send"], r["reduce_recv"], r["load_sem"])
+    little = ReduceSmall(place, r["slots"], r["small_send"], r["small_recv"])
+    swap = Exchange(place, r["swap_send"], r["swap_recv"])
+    for name in ("q_heads", "k_heads", "v_heads"):
+        loads[name].start()
+    reduce.load(3).start()
+    greet(
+        place.torus()
+        + tuple(
+            (place.dp, (place.x + dx) % 4 * 2 + (place.y_lo + dy) % 2)
+            for dx, dy in OFFSETS
+            if (dx, dy) not in ((1, 0), (3, 0), (0, 1))
+        )
+        + ((place.y_hi * 8 + place.z_far * 2 + place.core, place.seq),)
+    )
+    own = []
+    for slot in range(2):
+        swap.send(
+            slot,
+            lambda partner: r["d_attended"].at[slot, :, head_cols(partner, 256)],
+            lambda sender: r["grad_in"].at[slot, token_rows(sender), :],
+        )
+        copy = pltpu.make_async_copy(
+            r["d_attended"].at[slot, :, head_cols(me, 256)], r["grad_in"].at[slot, token_rows(me), :], r["in_sem"].at[7 + slot]
+        )
+        copy.start()
+        own.append(copy)
+    reduce.load(2).start()
+    reduce.load(1).start()
+    for name in ("q_flat", "k_flat", "x_in", "weights_qkv"):
+        loads[name].start()
+
+    def stages(*steps):
+        for number, g in steps:
+            reduce.stage(number, g)
+            if number == 9:
+                pltpu.make_async_copy(reduce.result(g), outs[g], r["out_sem"].at[g]).start()
+
+    stages((0, 3), (0, 2))
+    for name in ("q_heads", "k_heads", "v_heads"):
+        loads[name].wait()
+
+    def attend_back(slot, head):
+        cols = slice(head * 128, (head + 1) * 128)
+        if head == 0:
+            r["dk_sum"][...] = jnp.zeros((1024, 128), f32)
+            r["dv_sum"][...] = jnp.zeros((1024, 128), f32)
+        for block in range(4):
+            rows, upto = slice(block * 256, (block + 1) * 256), (block + 1) * 256
+            q, grad = r["q_in"][slot, rows, cols], r["grad_in"][slot, rows, cols]
+            k, v = r["k_in"][slot, :upto, :], r["v_in"][slot, :upto, :]
+            scores = mm_nt(k, q) * SCALE
+            key = lax.broadcasted_iota(jnp.int32, scores.shape, 0)
+            query = block * 256 + lax.broadcasted_iota(jnp.int32, scores.shape, 1)
+            scores = jnp.where(key <= query, scores, -1e30)
+            shifted = jnp.exp(scores - jnp.max(scores, axis=0, keepdims=True))
+            prob = shifted * (1.0 / jnp.sum(shifted, axis=0, keepdims=True))
+            d_prob = mm_nt(v, grad)
+            dot = jnp.sum(prob * d_prob, axis=0, keepdims=True)
+            d_score = (prob * (d_prob - dot) * SCALE).astype(bf16)
+            r["dk_sum"][:upto, :] += mm(d_score, q)
+            r["dv_sum"][:upto, :] += mm(prob.astype(bf16), grad)
+            r["dq"][slot, rows, cols] = mm_tn(d_score, k).astype(bf16)
+
+    def to_rows(kind, slot, heads, rows, width):
+        swap.send(
+            kind,
+            lambda partner: r[heads].at[slot, token_rows(partner), :],
+            lambda sender: r[rows].at[slot, :, head_cols(sender, width)],
+        )
+        r[rows][slot, :, head_cols(me, width)] = r[heads][slot, token_rows(me), :]
+
+    between = (
+        ((1, 3), (0, 1)),
+        ((2, 3), (1, 2), (3, 3)),
+        ((4, 3), (2, 2), (1, 1)),
+        ((5, 3), (3, 2), (2, 1)),
+    )
+    for slot in range(2):
+        own[slot].wait()
+        swap.take(slot, lambda sender: r["grad_in"].at[slot, token_rows(sender), :])
+        attend_back(slot, 0)
+        stages(*between[2 * slot])
+        attend_back(slot, 1)
+        r["dk"][slot] = r["dk_sum"][...].astype(bf16)
+        r["dv"][slot] = r["dv_sum"][...].astype(bf16)
+        to_rows(2 + 3 * slot, slot, "dq", "dq_rows", 256)
+        to_rows(3 + 3 * slot, slot, "dk", "dk_rows", 128)
+        to_rows(4 + 3 * slot, slot, "dv", "dv_rows", 128)
+        stages(*between[2 * slot + 1])
+    g_attn, g_query, g_key, _ = gain_rows(r["gain_tiles"])
+    for name in ("q_flat", "k_flat", "x_in", "weights_qkv"):
+        loads[name].wait()
+    stages((6, 3), (4, 2), (3, 1), (7, 3), (5, 2), (8, 3), (4, 1), (9, 3), (6, 2), (5, 1))
+    for slot in range(2):
+        swap.take(2 + 3 * slot, lambda sender: r["dq_rows"].at[slot, :, head_cols(sender, 256)])
+        swap.take(3 + 3 * slot, lambda sender: r["dk_rows"].at[slot, :, head_cols(sender, 128)])
+        swap.take(4 + 3 * slot, lambda sender: r["dv_rows"].at[slot, :, head_cols(sender, 128)])
+
+    cos, sin = r["cos"], r["sin"]
+    r["d_x"][...] = jnp.zeros((256, 1024), f32)
+    r["dg_query"][...] = jnp.zeros((1, 128), f32)
+    r["dg_key"][...] = jnp.zeros((1, 128), f32)
+
+    def project_back(d_flat, first):
+        cols = pl.ds(pl.multiple_of(first, 128), 512)
+        weights = r["buf_qkv"][:, :, :, :, :, cols].reshape(1024, 512)
+        r["d_x"][...] += mm_nt(d_flat, weights)
+        grad = mm_tn(r["x_in_in"][...], d_flat).astype(bf16)
+        r["buf_qkv"][:, :, :, :, :, cols] = grad.reshape(2, 4, 2, 4, 16, 512)
+
+    def head_tile(j, rows_ref, flat_ref, first, gain, dg_ref):
+        cols = pl.ds(pl.multiple_of(j * 512, 128), 512)
+        grads_in = rows_ref[:, :, cols].reshape(256, 512).astype(f32)
+        flat = flat_ref[:, cols]
+        done = []
+        for h in range(4):
+            e = grads_in[:, h * 128 : (h + 1) * 128]
+            v = flat[:, h * 128 : (h + 1) * 128]
+            e = e * cos[...] - pltpu.roll(e, 64, 1) * sin[...]
+            scale = inv_rms(v)
+            weighed = gain * e
+            d = scale * weighed - v * (scale * scale * scale) * jnp.mean(v * weighed, axis=-1, keepdims=True)
+            dg_ref[...] += jnp.sum(e * v * scale, axis=0, keepdims=True)
+            done.append(d.astype(bf16))
+        project_back(jnp.concatenate(done, axis=-1), first + j * 512)
+
+    def query_tile(j, carry):
+        head_tile(j, r["dq_rows"], r["q_flat_in"], 0, g_query, r["dg_query"])
+        return carry
+
+    def key_tile(j, carry):
+        head_tile(j, r["dk_rows"], r["k_flat_in"], 2048, g_key, r["dg_key"])
+        return carry
+
+    def value_tile(j, carry):
+        cols = pl.ds(pl.multiple_of(j * 512, 128), 512)
+        project_back(r["dv_rows"][:, :, cols].reshape(256, 512), 3072 + j * 512)
+        return carry
+
+    def swap_cores(half):
+        reduce.send(
+            0, 36 + 6 * half,
+            r["buf_qkv"].at[:, :, 1 - place.core, :, :, pl.ds(half * 2048, 2048)],
+            reduce.total(0).at[half],
+            place.to_core,
+        )
+
+    lax.fori_loop(0, 4, query_tile, 0)
+    swap_cores(0)
+    lax.fori_loop(0, 2, key_tile, 0)
+    lax.fori_loop(0, 2, value_tile, 0)
+    swap_cores(1)
+    for half in range(2):
+        reduce.take(0, 36 + 6 * half, reduce.total(0).at[half])
+        accumulate(
+            reduce.total(0).at[half],
+            r["buf_qkv"].at[:, :, place.core, :, :, pl.ds(half * 2048, 2048)],
+        )
+    reduce.send_far(0, 0)
+
+    x, d_x = r["hidden"][...].reshape(256, 1024).astype(f32), r["d_x"][...]
+    scale = inv_rms(x)
+    weighed = g_attn * d_x
+    d_norm = scale * weighed - x * (scale * scale * scale) * jnp.mean(x * weighed, axis=-1, keepdims=True)
+    r["d_input"][...] = r["d_residual"][...] + d_norm
+    dg_attn = jnp.sum(d_x * x * scale, axis=0, keepdims=True)
+    rows = [dg_attn[:, at * 128 : (at + 1) * 128] for at in range(8)]
+    rows += [r["dg_query"][...], r["dg_key"][...]]
+    rows += [r["dg_ffn"][:, at * 128 : (at + 1) * 128] for at in range(8)]
+    rows += [jnp.zeros((6, 128), f32)]
+    little.put(0, jnp.concatenate(rows, axis=0))
+    stages((1, 0), (7, 2), (6, 1))
+    little.put(1, little.sum(0))
+    stages((2, 0), (8, 2), (7, 1))
+    little.put(2, little.sum(1))
+    stages((3, 0), (9, 2), (8, 1))
+    little.put(3, little.sum(2))
+    stages((4, 0), (9, 1))
+    little.put(4, little.sum(3))
+    stages((5, 0), (6, 0))
+    r["gains_sum"][...] = little.sum(4)
+    stages((7, 0), (8, 0), (9, 0))
+    reduce.finish()
+    swap.finish()
+    for g in range(4):
+        pltpu.make_async_copy(reduce.result(g), outs[g], r["out_sem"].at[g]).wait()
+
+
+def backward(inputs):
+    def shape(*dims, dtype=bf16):
+        return jax.ShapeDtypeStruct(dims, dtype)
+
+    outs = [shape(256, 1024, dtype=f32), shape(24, 128, dtype=f32)] + [
+        shape(2, 4, rows // 4, cols // 2) for rows, cols in zip(SHARD_ROWS, COLUMNS)
+    ]
+    vmem = pl.BlockSpec(memory_space=pltpu.VMEM)
+    hbm = pl.BlockSpec(memory_space=pl.ANY)
+    in_hbm = set(BACKWARD_IN[:11])
+    buffers = [
+        pltpu.VMEM(dims, dtype)
+        for dims, dtype in (
+            ((2, 4, 2, 4, 16, 4096), bf16),
+            ((2, 1024, 256), bf16),
+            ((2, 1024, 128), bf16),
+            ((2, 1024, 128), bf16),
+            ((2, 1024, 256), bf16),
+            ((2, 1024, 256), bf16),
+            ((2, 1024, 128), bf16),
+            ((2, 1024, 128), bf16),
+            ((1024, 128), f32),
+            ((1024, 128), f32),
+            ((2, 128, 2048), bf16),
+            ((2, 128, 1024), bf16),
+            ((2, 128, 1024), bf16),
+            ((256, 2048), f32),
+            ((256, 1024), f32),
+            ((256, 1024), bf16),
+            ((256, 1024), f32),
+            ((1, 128), f32),
+            ((1, 128), f32),
+            ((5, 4, 24, 128), f32),
+        )
+    ]
+    dma = pltpu.SemaphoreType.DMA
+    sems = [
+        dma((4, 44)),
+        dma((4, 44)),
+        dma((4,)),
+        dma((5, 3)),
+        dma((5, 3)),
+        dma((4,)),
+        dma((8, 7)),
+        dma((8, 7)),
+        dma((9,)),
+    ]
+    results = pl.pallas_call(
+        functools.partial(backward_kernel),
+        out_shape=outs,
+        in_specs=[hbm if name in in_hbm else vmem for name in BACKWARD_IN],
+        out_specs=[vmem] * 2 + [hbm] * 4,
+        scratch_shapes=reduce_scratch() + buffers + sems,
+        compiler_params=pltpu.CompilerParams(
+            collective_id=2, has_side_effects=True, vmem_limit_bytes=63 * 1024 * 1024
+        ),
+        name="backward",
+    )(*[inputs[name] for name in BACKWARD_IN])
+    return dict(zip(BACKWARD_OUT, results))
+
+
+def rotary_tables(positions):
+    frequency = jnp.exp(jnp.arange(64, dtype=f32) * (-2.0 * math.log(rope_base) / 128))
     angles = positions.astype(f32)[:, None] * frequency[None, :]
     cos_half, sin_half = jnp.cos(angles), jnp.sin(angles)
     return (
         jnp.concatenate([cos_half, cos_half], axis=-1),
-        jnp.concatenate([sin_half, sin_half], axis=-1),
+        jnp.concatenate([-sin_half, sin_half], axis=-1),
     )
-
-
-def turn(v):
-    half = v.shape[-1] // 2
-    return jnp.concatenate([-v[..., half:], v[..., :half]], axis=-1)
-
-
-def turn_back(v):
-    half = v.shape[-1] // 2
-    return jnp.concatenate([v[..., half:], -v[..., :half]], axis=-1)
-
-
-def inverse_rms(v):
-    return lax.rsqrt(jnp.mean(v * v, axis=-1, keepdims=True) + epsilon)
-
-
-def rms_back(v, gain, grad):
-    r = inverse_rms(v)
-    ge = gain * grad
-    dv = r * ge - v * (r * r * r) * jnp.mean(v * ge, axis=-1, keepdims=True)
-    return dv, grad * v * r
-
-
-def attend_forward(q, k, v):
-    rows, heads, width = q.shape
-    kv = k.shape[1]
-    q = q.reshape(rows, kv, heads // kv, width)
-    scores = jnp.einsum("qkgd,skd->kgqs", q, k, preferred_element_type=f32) * width ** (-0.5)
-    order = jnp.arange(rows, dtype=jnp.int32)
-    scores = jnp.where(order[None, :] <= order[:, None], scores, -1e30)
-    top = jnp.max(scores, axis=-1, keepdims=True)
-    shifted = jnp.exp(scores - top)
-    total = jnp.sum(shifted, axis=-1, keepdims=True)
-    prob = (shifted / total).astype(bf16)
-    out = jnp.einsum("kgqs,skd->qkgd", prob, v, preferred_element_type=f32)
-    return out.astype(bf16).reshape(rows, heads, width), top + jnp.log(total)
-
-
-def attend_backward(q, k, v, grad, lse):
-    rows, heads, width = q.shape
-    kv = k.shape[1]
-    scale = width ** (-0.5)
-    q = q.reshape(rows, kv, heads // kv, width)
-    grad = grad.reshape(rows, kv, heads // kv, width)
-    scores = jnp.einsum("qkgd,skd->kgqs", q, k, preferred_element_type=f32) * scale
-    order = jnp.arange(rows, dtype=jnp.int32)
-    scores = jnp.where(order[None, :] <= order[:, None], scores, -1e30)
-    prob = jnp.exp(scores - lse)
-    d_prob = jnp.einsum("qkgd,skd->kgqs", grad, v, preferred_element_type=f32)
-    row_dot = jnp.sum(prob * d_prob, axis=-1, keepdims=True)
-    d_score = (prob * (d_prob - row_dot) * scale).astype(bf16)
-    dq = jnp.einsum("kgqs,skd->qkgd", d_score, k, preferred_element_type=f32)
-    dk = jnp.einsum("kgqs,qkgd->skd", d_score, q, preferred_element_type=f32)
-    dv = jnp.einsum("kgqs,qkgd->skd", prob.astype(bf16), grad, preferred_element_type=f32)
-    return dq.astype(bf16).reshape(rows, heads, width), dk.astype(bf16), dv.astype(bf16)
-
-
-def to_heads(rows_in, slots):
-    parts = rows_in.reshape(slots, -1, rows_in.shape[1] // 128, 128)
-    return lax.all_to_all(parts, "seq", split_axis=2, concat_axis=1, tiled=True)
-
-
-def to_rows(heads_in):
-    out = lax.all_to_all(heads_in, "seq", split_axis=1, concat_axis=2, tiled=True)
-    return out.reshape(out.shape[0] * out.shape[1], -1)
-
-
-def layer(hidden, cotangent, lengths, positions, gains, weights):
-    g_attn, g_query, g_key, g_ffn = [g.astype(f32) for g in gains]
-    w_query, w_key, w_value, w_output, w_gate, w_up, w_down = weights
-    slots, tokens, width = hidden.shape
-    rows = slots * tokens
-    head = g_query.shape[0]
-    hq, hkv = w_query.shape[1] // head, w_key.shape[1] // head
-    index = lax.axis_index("seq") * tokens + jnp.arange(tokens, dtype=jnp.int32)
-    valid = (index[None, :] < lengths[:, None]).reshape(rows, 1)
-    cos, sin = rotary_tables(positions.reshape(rows), head)
-    cos, sin = cos[:, None, :], sin[:, None, :]
-    x = hidden.reshape(rows, width).astype(f32)
-    x_in = (x * inverse_rms(x) * g_attn).astype(bf16)
-    q_flat = product(x_in, w_query).reshape(rows, hq, head)
-    k_flat = product(x_in, w_key).reshape(rows, hkv, head)
-    v_rows = product(x_in, w_value).astype(bf16)
-
-    def rope(v):
-        return v * cos + turn(v) * sin
-
-    q_rows = rope(q_flat * inverse_rms(q_flat) * g_query).astype(bf16).reshape(rows, -1)
-    k_rows = rope(k_flat * inverse_rms(k_flat) * g_key).astype(bf16).reshape(rows, -1)
-    q, k, v = to_heads(q_rows, slots), to_heads(k_rows, slots), to_heads(v_rows, slots)
-    attended, lse = zip(*[attend_forward(q[i], k[i], v[i]) for i in range(slots)])
-    context = to_rows(jnp.stack(attended))
-    residual = x + product(context, w_output)
-    mid_in = (residual * inverse_rms(residual) * g_ffn).astype(bf16)
-    gate, up = product(mid_in, w_gate), product(mid_in, w_up)
-    sig = 1.0 / (1.0 + jnp.exp(-gate))
-    silu = gate * sig
-    unit = (silu * up).astype(bf16)
-    result = residual + product(unit, w_down)
-    out = jnp.where(valid, result, 0.0).astype(bf16)
-    d_result = jnp.where(valid, cotangent.reshape(rows, width).astype(f32), 0.0)
-    d_branch = d_result.astype(bf16)
-    grad_down = cross_rows(unit, d_branch)
-    d_unit = times_trans(d_branch, w_down)
-    d_gate = (d_unit * up * sig * (1.0 + gate * (1.0 - sig))).astype(bf16)
-    d_up = (d_unit * silu).astype(bf16)
-    grad_gate, grad_up = cross_rows(mid_in, d_gate), cross_rows(mid_in, d_up)
-    d_mid = times_trans(d_gate, w_gate) + times_trans(d_up, w_up)
-    dv_mid, dg_ffn = rms_back(residual, g_ffn, d_mid)
-    d_residual = d_result + dv_mid
-    d_attn = d_residual.astype(bf16)
-    grad_output = cross_rows(context, d_attn)
-    d_attended = times_trans(d_attn, w_output).astype(bf16)
-    grad_heads = to_heads(d_attended, slots)
-    back = [attend_backward(q[i], k[i], v[i], grad_heads[i], lse[i]) for i in range(slots)]
-    dq, dk, dv = [to_rows(jnp.stack(part)) for part in zip(*back)]
-
-    def head_back(flat, gain, grad):
-        grad = grad.reshape(flat.shape).astype(f32)
-        grad = grad * cos + turn_back(grad * sin)
-        d_flat, dg = rms_back(flat, gain, grad)
-        return d_flat.astype(bf16).reshape(rows, -1), jnp.sum(dg, axis=(0, 1))
-
-    d_query, dg_query = head_back(q_flat, g_query, dq)
-    d_key, dg_key = head_back(k_flat, g_key, dk)
-    grad_query, grad_key, grad_value = (
-        cross_rows(x_in, d_query),
-        cross_rows(x_in, d_key),
-        cross_rows(x_in, dv),
-    )
-    d_x_in = (
-        times_trans(d_query, w_query) + times_trans(d_key, w_key) + times_trans(dv, w_value)
-    )
-    dv_x, dg_attn = rms_back(x, g_attn, d_x_in)
-    d_input = d_residual + dv_x
-    gain_grads = (jnp.sum(dg_attn, axis=0), dg_query, dg_key, jnp.sum(dg_ffn, axis=0))
-    weight_grads = (
-        grad_query,
-        grad_key,
-        grad_value,
-        grad_output,
-        grad_gate,
-        grad_up,
-        grad_down,
-    )
-    shape = (slots, tokens, width)
-    return out.reshape(shape), d_input.reshape(shape), gain_grads, weight_grads
 
 
 def per_device(
@@ -860,46 +1272,20 @@
         ((attn_gain, dp % 2 * 64), (query_gain, dp * 8), (key_gain, dp * 8), (ffn_gain, dp % 2 * 64))
     ):
         tile = lax.dynamic_update_slice(tile, gain[None, :], (row, lane))
+    index = lax.axis_index("seq") * 128 + jnp.arange(128, dtype=jnp.int32)
+    valid = (index[None, :] < slot_lengths[:, None]).astype(f32).reshape(256, 1)
+    cos, sin = rotary_tables(position_ids.reshape(256))
     shards = (w_query, key_weight, value_weight, w_output, w_gate, w_up, w_down)
-    qkv, output, gate_up, down, small = gather_all(shards, tile)
-    qkv, gate_up = qkv.reshape(1024, 4096), gate_up.reshape(1024, 6144)
-    weights = (
-        qkv[:, :2048],
-        qkv[:, 2048:3072],
-        qkv[:, 3072:],
-        output.reshape(2048, 1024),
-        gate_up[:, :3072],
-        gate_up[:, 3072:],
-        down.reshape(3072, 1024),
-    )
-    small = small.astype(f32).reshape(8, 2, 16, 128)
-    gains = (
-        jnp.sum(small[:, :, 0], axis=1).reshape(1024),
-        jnp.sum(small[:, :, 1], axis=(0, 1)),
-        jnp.sum(small[:, :, 2], axis=(0, 1)),
-        jnp.sum(small[:, :, 3], axis=1).reshape(1024),
-    )
-    out, d_input, gain_grads, weight_grads = layer(
-        hidden_in, out_cotangent, slot_lengths, position_ids, gains, weights
-    )
-
-    gq, gk, gv, go, gg, gu, gd = [part.astype(bf16) for part in weight_grads]
-    halves = (
-        (gq, jnp.concatenate([gk, gv], axis=1)),
-        (go[:, :512], go[:, 512:]),
-        (gg, gu),
-        (gd[:, :512], gd[:, 512:]),
-    )
-    grads = [
-        jnp.stack(pair).reshape(2, 2, 4, 2, 4, rows // 4, cols // 2)
-        for pair, rows, cols in zip(halves, SHARD_ROWS, COLUMNS)
-    ]
-    flat = jnp.concatenate(gain_grads)
-    flat = jnp.pad(flat, (0, 24 * 128 - flat.shape[0])).reshape(24, 128)
-    *sums, gains_sum = reduce_all(grads, flat)
+    done = forward(shards, tile, hidden_in, out_cotangent, cos, sin, valid)
+    done.update(hidden=hidden_in, cos=cos, sin=sin)
+    for name, rows, cols in (("total_output", 32, 512), ("total_gate_up", 16, 3072), ("total_down", 48, 512)):
+        done[name] = done[name].reshape(2, 2, 4, 4, rows, cols)
+    done["weights_qkv"] = done["weights_qkv"].reshape(2, 4, 2, 4, 16, 4096)
+    last = backward(done)
+    sums = [last[name] for name in ("sum_qkv", "sum_output", "sum_gate_up", "sum_down")]
+    d_input, gains_sum = last["d_input"].reshape(2, 128, 1024), last["gains_sum"]
     qkv, output, gate_up, down = [
-        part.reshape(2, rows, cols // 2).astype(f32)
-        for part, rows, cols in zip(sums, SHARD_ROWS, COLUMNS)
+        part.reshape(2, rows, cols // 2).astype(f32) for part, rows, cols in zip(sums, SHARD_ROWS, COLUMNS)
     ]
     gq, gk, gv, gg, gu = qkv[0], qkv[1, :, :1024], qkv[1, :, 1024:], gate_up[0], gate_up[1]
     go, gd = jnp.concatenate([output[0], output[1]], 1), jnp.concatenate([down[0], down[1]], 1)
@@ -908,7 +1294,7 @@
         lax.dynamic_slice(gains_sum, (start + dp * size,), (size,))
         for start, size in ((0, 64), (1024, 8), (1152, 8), (1280, 64))
     ]
-    return (out, d_input, dg_attn, gq, gk, gv, dg_query, dg_key, go, dg_ffn, gg, gu, gd)
+    return (done["out"], d_input, dg_attn, gq, gk, gv, dg_query, dg_key, go, dg_ffn, gg, gu, gd)
 
 
 def solution(mesh):

time: 509 us -> 340 us (0.67)
  Pallas kernels: 191 us -> 316 us
  matrix products: 97.9 us -> 0 us
  local copies, waits for them, and re-layouts: 89.5 us -> 12.5 us
  other arithmetic: 55.8 us -> 5.71 us
  starting transfers between devices: 37.4 us -> 0 us
  waiting for transfers between devices: 25.2 us -> 0 us
    pallas_call x2, Pallas kernels: 191 us -> 316 us  [the longest x1 161 us: backward(): pl.pallas_call(functools.partial(backward_kernel), out_shape=outs, in_spe...]
    dot_general x33 -> x0, matrix products: 97.9 us -> none  [the longest x7 27.6 us: product(): return jnp.dot(left, right, preferred_element_type=f32)]
    all_to_all x8 -> x0, starting transfers between devices: 37.4 us -> none  [the longest x4 19.5 us: to_rows(): lax.all_to_all(heads_in, 'seq', split_axis=1, concat_axis=2, tiled=True)]
    another operation x10 -> x0, other arithmetic: 28.1 us -> none  [the longest x4 18.1 us: per_device(): jnp.stack(pair).reshape(2, 2, 4, 2, 4, rows // 4, cols // 2)]
    all_to_all x8 -> x0, waiting for transfers between devices: 25.2 us -> none  [the longest x4 15 us: to_heads(): return lax.all_to_all(parts, 'seq', split_axis=2, concat_axis=1, tiled=True)]
    dot_general x4 -> x0, local copies, waits for them, and re-layouts: 17.3 us -> none  [product(): return jnp.dot(left, right, preferred_element_type=f32)]
    unnamed x154 -> x14, local copies, waits for them, and re-layouts: 18.6 us -> 1.79 us
    convert_element_type x4 -> x1, local copies, waits for them, and re-layouts: 13.4 us -> 0.8 us  [per_device(): valid = (index[None, :] < slot_lengths[:, None]).astype(f32).reshape(256, 1)]
  transfers between devices with their start and end apart: 8 -> 0, of which waited for: 4 -> 0; matrix products, arithmetic and copies ran while one was open for 20% -> 0% of each run, Pallas kernels for 0% -> 0%
where the time goes in v3:
time: 340 us; the launch traced here: 335 us
  Pallas kernels  316 us (93%)
  local copies, waits for them, and re-layouts  12.5 us (4%)
  other arithmetic  5.71 us (2%)
    pallas_call x1, Pallas kernels, backward(): pl.pallas_call(functools.partial(backward_kernel), out_shape=outs, in_spe...  161 us
    pallas_call x1, Pallas kernels, forward(): pl.pallas_call(functools.partial(forward_kernel), out_shape=list(outs.val...  155 us

profile of v3, /device:TPU:0, one launch (start us, length us, event | category | flops | bytes accessed | tf_op | source)
XLA Modules:
  0.0 335.2 jit_solution(13699752972756395010)
XLA Ops:
  0.7 0.8 dynamic_update_slice.12
  1.5 0.8 dynamic_update_slice.13
  2.3 0.8 dynamic_update_slice.14
  3.1 0.8 dynamic_update_slice.15.refs_7_
  3.9 0.0 copy-start.5
  3.9 0.7 convert_bitcast_fusion
  4.6 0.5 fusion
  5.1 0.8 pad_maximum_fusion.2
  6.0 0.7 compare_convert_fusion
  6.7 0.8 copy.28.refs_12_
  7.5 0.0 copy-done.5
  7.5 154.7 %forward.1 = (bf16[2,128,1024]{2,1,0:T(8,128)(2,1)}, f32[256,1024]{1,0:T(8,128)}, bf16[2,128,2048]{2,1,0:T(8,128)(2,1)}, f32[1,1024]{1,0:T(1,128)}, bf16[256,102...) custom-call(bf16[64,2048]{1,0:T(8,128)(2,1)} %refs_0_.1, ...), custom_call_target="tpu_custom_call" | custom-call | tf_op jit(solution)/shard_map/forward/pallas_call | solution.py:941
  162.2 161.3 %backward.1 = (f32[256,1024]{1,0:T(8,128)}, f32[24,128]{1,0:T(8,128)}, bf16[2,4,16,2048]{3,2,1,0:T(8,128)(2,1)}, bf16[2,4,32,512]{3,2,1,0:T(8,128)(2,1)}, bf16[2...) custom-call(bf16[2,2,4,4,32,512]{5,4,3,2,1,0:T(8,128)(2,1)} %bitcast.29, ...), custom_call_target="tpu_custom_call" | custom-call | tf_op jit(solution)/shard_map/backward/pallas_call | solution.py:1228
  323.5 1.4 fusion.4
  324.8 1.8 slice.43
  326.6 1.1 convert_element_type.45
  327.8 0.8 slice_bitcast_fusion
  328.6 1.3 fusion.5
  330.0 0.8 pad_maximum_fusion.1
  330.8 1.3 fusion.1
  332.1 0.1 fusion.2
  332.2 0.9 pad_maximum_fusion
  333.2 0.8 copy.35
  334.0 1.0 copy.36
  (14 shorter events, 0.1 us)
Async XLA Ops:
  3.9 3.6 %copy-start.5 = (bf16[16,128]{1,0:T(8,128)(2,1)}, bf16[16,128]{1,0:T(8,128)(2,1)S(1)}, u32[]{:S(2)}) copy-start(bf16[16,128]{1,0:T(8,128)(2,1)S(1)} %dynamic_update_slice.15.refs_7_) | copy-start | bytes 12292
  323.4 6.5 %copy-start.3 = (bf16[2,4,32,512]{3,2,1,0:T(8,128)(2,1)S(1)}, bf16[2,4,32,512]{3,2,1,0:T(8,128)(2,1)}, u32[]{:S(2)}) copy-start(bf16[2,4,32,512]{3,2,1,0:T(8,128)(2,1)} %get-tuple-element.52) | copy-start | bytes 786436
  323.5 7.4 %copy-start = (bf16[2,4,16,3072]{3,2,1,0:T(8,128)(2,1)S(1)}, bf16[2,4,16,3072]{3,2,1,0:T(8,128)(2,1)}, u32[]{:S(2)}) copy-start(bf16[2,4,16,3072]{3,2,1,0:T(8,128)(2,1)} %get-tuple-element.53) | copy-start | bytes 2359300
  327.8 4.4 %copy-start.1 = (bf16[2,4,48,512]{3,2,1,0:T(8,128)(2,1)S(1)}, bf16[2,4,48,512]{3,2,1,0:T(8,128)(2,1)}, u32[]{:S(2)}) copy-start(bf16[2,4,48,512]{3,2,1,0:T(8,128)(2,1)} %get-tuple-element.54) | copy-start | bytes 1179652
  330.8 2.3 copy-start.4
  330.8 3.1 copy-start.2

commit v4 on v3

--- a/solution.py
+++ b/solution.py
@@ -18,6 +18,12 @@
 SHARD_ROWS = (64, 128, 64, 192)
 COLUMNS = (4096, 1024, 6144, 1024)
 THIRDS = ((640, 640, 768), (256, 128, 128), (1024, 1024, 1024), (128, 256, 128))
+
+
+GATHER_ROWS = (64, 128, 64, 64, 192)
+GATHER_COLUMNS = (4096, 1024, 3072, 3072, 1024)
+SHARED = (1280, 384, 1024, 1024, 384)
+SHARES = ((384, 384, 512), (128, 128, 128), (384, 256, 384), (256, 384, 384), (128, 128, 128))
 
 
 class Place:
@@ -82,8 +88,8 @@
 
     def region(self, g, kind, receiving):
         p = self.place
-        rows, cols = SHARD_ROWS[g], COLUMNS[g]
-        half = cols // 2
+        rows, cols = GATHER_ROWS[g], GATHER_COLUMNS[g]
+        shared = SHARED[g]
         here, there = p.y_hi, 1 - p.y_hi
         whole, top, low = pl.ds(0, rows), pl.ds(0, rows // 2), pl.ds(rows // 2, rows // 2)
         low_first = pl.ds(rows // 2, rows // 4)
@@ -91,8 +97,7 @@
         color = p.color
         if kind.startswith("share") and receiving:
             color = 1 - color
-        first = color * half
-        mine = pl.ds(pl.multiple_of(first, 128), half)
+        mine = pl.ds(pl.multiple_of(color * shared, 128), cols - shared)
         below, above = p.z_down, p.z_up
         z, far = p.z, p.z_far
         buf = self.buffers[g]
@@ -125,8 +130,8 @@
         if kind.startswith("share"):
             _, n, which = kind.split("_")
             n = int(n)
-            start = sum(THIRDS[g][:n])
-            part = pl.ds(pl.multiple_of(first + start, 128), THIRDS[g][n])
+            start = color * (cols - shared) + sum(SHARES[g][:n])
+            part = pl.ds(pl.multiple_of(start, 128), SHARES[g][n])
             to = (p.to_x_up, p.to_x_down, p.to_pair)[n]
             if which == "other":
                 return buf.at[there, :, p.core, :, part], to
@@ -175,6 +180,7 @@
         elif number == 2:
             self.take(g, "cross_own")
             self.send(g, "other_up", "other_down")
+        elif number == 8:
             self.take(g, "on_up", "on_down")
             self.send(g, "cross_far")
             self.share(g, "far")
@@ -194,22 +200,27 @@
         else:
             self.take(g, "core_own", "core_up", "core_down", "core_far", "core_other")
 
-    def finish(self):
+    def finish(self, *groups):
         for g, kind in self.sent:
-            self.copy(g, kind).wait_send()
-        self.sent = []
-
-
-def own_places(place, buffers):
+            if g in groups:
+                self.copy(g, kind).wait_send()
+        self.sent = [one for one in self.sent if one[0] not in groups]
+
+
+def own_copies(place, shards, buffers):
     mine = [buf.at[place.y_hi, place.z, place.core] for buf in buffers]
+    query, key, value, output, gate, up, down = shards
+    first, last = pl.ds(0, 1536), pl.ds(1536, 1536)
     return (
-        mine[0].at[:, pl.ds(0, 2048)],
-        mine[0].at[:, pl.ds(2048, 1024)],
-        mine[0].at[:, pl.ds(3072, 1024)],
-        mine[1],
-        mine[2].at[:, pl.ds(0, 3072)],
-        mine[2].at[:, pl.ds(3072, 3072)],
-        mine[3],
+        (query, mine[0].at[:, pl.ds(0, 2048)]),
+        (key, mine[0].at[:, pl.ds(2048, 1024)]),
+        (value, mine[0].at[:, pl.ds(3072, 1024)]),
+        (output, mine[1]),
+        (gate.at[:, first], mine[2].at[:, first]),
+        (up.at[:, first], mine[2].at[:, last]),
+        (gate.at[:, last], mine[3].at[:, first]),
+        (up.at[:, last], mine[3].at[:, last]),
+        (down, mine[4]),
     )
 
 
@@ -592,10 +603,11 @@
     "total_output", "total_gate_up", "total_down", "weights_qkv", "q_heads", "k_heads", "v_heads", "gain_tiles",
 )
 FORWARD_SCRATCH = (
-    "buf_qkv", "buf_output", "buf_gate_up", "buf_down", "tiles", "rows", "core_down",
+    "buf_qkv", "buf_output", "buf_gate_up_0", "buf_gate_up_1", "buf_down", "tiles", "rows", "core_down",
     "q_in", "k_in", "v_in", "att", "context", "residual", "mid_in", "result", "d_mid", "d_branch",
     "gather_send", "gather_recv", "small_send", "small_recv", "local_sem", "swap_send", "swap_recv", "out_sem",
     "core_free", "core_send", "core_recv",
+    "out_out", "d_residual_out", "d_attended_out", "x_in_out", "q_flat_out", "k_flat_out",
 )
 FF_TILE = 768
 
@@ -604,14 +616,12 @@
     r = dict(zip(FORWARD_IN + FORWARD_OUT + FORWARD_SCRATCH, refs))
     place = Place()
     me = place.seq
-    buffers = [r["buf_qkv"], r["buf_output"], r["buf_gate_up"], r["buf_down"]]
+    buffers = [r["buf_qkv"], r["buf_output"], r["buf_gate_up_0"], r["buf_gate_up_1"], r["buf_down"]]
     tiles = r["tiles"]
-    sources = [r[name] for name in FORWARD_IN[:8]]
+    pairs = own_copies(place, [r[name] for name in FORWARD_IN[:7]], buffers)
+    pairs += ((r["gains"], tiles.at[place.y_hi, place.z, place.core]),)
     copies = [
-        pltpu.make_async_copy(shard, there, r["local_sem"].at[at])
-        for at, (shard, there) in enumerate(
-            zip(sources, own_places(place, buffers) + (tiles.at[place.y_hi, place.z, place.core],))
-        )
+        pltpu.make_async_copy(shard, there, r["local_sem"].at[at]) for at, (shard, there) in enumerate(pairs)
     ]
     for copy in copies:
         copy.start()
@@ -650,12 +660,12 @@
     little.take(2)
     little.take(3)
     little.start(4)
-    phases((1, 0), (0, 1), (2, 0), (3, 0), (0, 3), (4, 0), (5, 0), (1, 1), (6, 0))
+    phases((0, 1), (1, 0), (2, 0), (8, 0), (3, 0), (0, 2), (1, 1), (2, 1), (4, 0))
     little.take(4)
     g_attn, g_query, g_key, g_ffn = gain_rows(tiles)
     x = r["hidden"][...].reshape(256, 1024).astype(f32)
-    r["x_in"][...] = (x * inv_rms(x) * g_attn).astype(bf16)
-    phases((0, 2), (7, 0))
+    r["x_in_out"][...] = (x * inv_rms(x) * g_attn).astype(bf16)
+    phases((5, 0), (6, 0), (8, 1), (3, 1), (1, 2), (4, 1), (5, 1), (0, 4), (7, 0))
     save("weights_qkv", buffers[0])
     save("gain_tiles", tiles)
 
@@ -665,7 +675,7 @@
         return buffers[0][:, :, :, :, pl.ds(pl.multiple_of(first, 128), 512)].reshape(1024, 512)
 
     def head_tile(j, flat_ref, rows_ref, first, gain):
-        flat = mm(r["x_in"][...], qkv_weights(first + j * 512))
+        flat = mm(r["x_in_out"][...], qkv_weights(first + j * 512))
         cols = pl.ds(pl.multiple_of(j * 512, 128), 512)
         flat_ref[:, cols] = flat
         done = []
@@ -676,16 +686,16 @@
         rows_ref[...] = jnp.concatenate(done, axis=-1).reshape(2, 128, 512)
 
     def query_tile(j, carry):
-        head_tile(j, r["q_flat"], r["rows"].at[0, :, :, pl.ds(pl.multiple_of(j * 512, 128), 512)], 0, g_query)
+        head_tile(j, r["q_flat_out"], r["rows"].at[0, :, :, pl.ds(pl.multiple_of(j * 512, 128), 512)], 0, g_query)
         return carry
 
     def key_tile(j, carry):
-        head_tile(j, r["k_flat"], r["rows"].at[1, :, :, pl.ds(pl.multiple_of(j * 512, 128), 512)], 2048, g_key)
+        head_tile(j, r["k_flat_out"], r["rows"].at[1, :, :, pl.ds(pl.multiple_of(j * 512, 128), 512)], 2048, g_key)
         return carry
 
     def value_tile(j, carry):
         cols = pl.ds(pl.multiple_of(1024 + j * 512, 128), 512)
-        r["rows"][1, :, :, cols] = mm(r["x_in"][...], qkv_weights(3072 + j * 512)).astype(bf16).reshape(2, 128, 512)
+        r["rows"][1, :, :, cols] = mm(r["x_in_out"][...], qkv_weights(3072 + j * 512)).astype(bf16).reshape(2, 128, 512)
         return carry
 
     def to_heads(kind, at, first, heads, width):
@@ -705,7 +715,10 @@
     to_heads(1, 1, 0, "k_in", 128)
     lax.fori_loop(0, 2, value_tile, 0)
     to_heads(2, 1, 1024, "v_in", 128)
-    phases((2, 1), (1, 3), (3, 1), (1, 2), (4, 1), (2, 3), (2, 2), (5, 1), (3, 3), (6, 1), (3, 2))
+    phases((0, 3), (2, 2), (3, 2), (8, 2), (1, 3), (1, 4), (2, 4), (2, 3), (4, 2), (8, 4), (3, 4), (6, 1))
+    save("x_in", r["x_in_out"])
+    save("q_flat", r["q_flat_out"])
+    save("k_flat", r["k_flat_out"])
     swap.take(0, lambda sender: r["q_in"].at[:, token_rows(sender), :])
     swap.take(1, lambda sender: r["k_in"].at[:, token_rows(sender), :])
     swap.take(2, lambda sender: r["v_in"].at[:, token_rows(sender), :])
@@ -735,8 +748,8 @@
         )
         r["context"][slot, :, head_cols(me, 256)] = r["att"][slot, token_rows(me), :]
         if slot == 0:
-            phases((4, 3), (4, 2))
-    phases((7, 1), (5, 3), (5, 2), (6, 3), (6, 2))
+            phases((7, 1), (5, 2), (3, 3))
+    phases((4, 4), (8, 3), (5, 4))
     for slot in range(2):
         swap.take(3 + slot, lambda sender: r["context"].at[slot, :, head_cols(sender, 256)])
 
@@ -749,8 +762,8 @@
     r["mid_in"][...] = (residual * inv_rms(residual) * g_ffn).astype(bf16)
     d_result = jnp.where(r["valid"][...] > 0.5, r["cot"][...].reshape(256, 1024).astype(f32), 0.0)
     r["d_branch"][...] = d_result.astype(bf16)
-    phases((7, 2), (7, 3))
-    gather.finish()
+    phases((6, 2), (4, 3), (6, 4), (5, 3), (7, 4), (7, 2), (6, 3))
+    gather.finish(0, 2, 4)
     little.finish()
     swap.finish()
     for copy in saved:
@@ -770,38 +783,38 @@
             device_id_type=MESH,
         )
 
-    def ffn_copies(f):
-        here = pl.ds(pl.multiple_of(f * FF_TILE, 128), FF_TILE)
-        up = pl.ds(pl.multiple_of(3072 + f * FF_TILE, 128), FF_TILE)
-        y, z = f // 2, pl.ds(f % 2 * 2, 2)
+    def ffn_places(f):
+        here = pl.ds(pl.multiple_of(f % 2 * FF_TILE, 128), FF_TILE)
+        up = pl.ds(pl.multiple_of(1536 + f % 2 * FF_TILE, 128), FF_TILE)
+        there = pl.ds(pl.multiple_of(f * FF_TILE, 128), FF_TILE)
+        return here, up, there, pl.ds(f % 2 * 2, 2)
+
+    def ffn_copies(b, f):
+        here, up, there, z = ffn_places(f)
+        weights = buffers[2 + b]
         return (
-            to_core(buffers[2].at[:, :, other, :, here], buffers[0].at[:, :, 0, :, here], f, 0),
-            to_core(buffers[2].at[:, :, other, :, up], buffers[0].at[:, :, 1, :, here], f, 1),
-            to_core(buffers[3].at[y, z, other], r["core_down"].at[y, z], f, 2),
-        )
-
-    def ffn_join(f):
-        here = pl.ds(pl.multiple_of(f * FF_TILE, 128), FF_TILE)
-        up = pl.ds(pl.multiple_of(3072 + f * FF_TILE, 128), FF_TILE)
-        y, z = f // 2, pl.ds(f % 2 * 2, 2)
-        for copy in ffn_copies(f):
+            to_core(weights.at[:, :, other, :, here], buffers[0].at[:, :, 0, :, there], f, 0),
+            to_core(weights.at[:, :, other, :, up], buffers[0].at[:, :, 1, :, there], f, 1),
+            to_core(buffers[4].at[b, z, other], r["core_down"].at[b, z], f, 2),
+        )
+
+    def ffn_join(b, f):
+        here, up, there, z = ffn_places(f)
+        weights = buffers[2 + b]
+        for copy in ffn_copies(b, f):
             copy.wait_recv()
-        buffers[2][:, :, core, :, here] = buffers[2][:, :, core, :, here] + buffers[0][:, :, 0, :, here]
-        buffers[2][:, :, core, :, up] = buffers[2][:, :, core, :, up] + buffers[0][:, :, 1, :, here]
-        buffers[3][y, z, core] = buffers[3][y, z, core] + r["core_down"][y, z]
+        weights[:, :, core, :, here] = weights[:, :, core, :, here] + buffers[0][:, :, 0, :, there]
+        weights[:, :, core, :, up] = weights[:, :, core, :, up] + buffers[0][:, :, 1, :, there]
+        buffers[4][b, z, core] = buffers[4][b, z, core] + r["core_down"][b, z]
 
     r["result"][...] = residual
     r["d_mid"][...] = jnp.zeros((256, 1024), f32)
 
-    def ffn_tile(f, carry):
-        def weights(first):
-            cols = pl.ds(pl.multiple_of(first + f * FF_TILE, 128), FF_TILE)
-            return cols, buffers[2][:, :, :, :, cols].reshape(1024, FF_TILE)
-
-        gate_cols, w_gate = weights(0)
-        up_cols, w_up = weights(3072)
-        y, z = f // 2, pl.ds(f % 2 * 2, 2)
-        w_down = buffers[3][y, z].reshape(FF_TILE, 1024)
+    def ffn_tile(b, f):
+        gate_cols, up_cols, _, z = ffn_places(f)
+        w_gate = buffers[2 + b][:, :, :, :, gate_cols].reshape(1024, FF_TILE)
+        w_up = buffers[2 + b][:, :, :, :, up_cols].reshape(1024, FF_TILE)
+        w_down = buffers[4][b, z].reshape(FF_TILE, 1024)
         mid, d_branch = r["mid_in"][...], r["d_branch"][...]
         gate, up = mm(mid, w_gate), mm(mid, w_up)
         sig = 1.0 / (1.0 + jnp.exp(-gate))
@@ -815,21 +828,38 @@
         shape = (4, 2, 64, FF_TILE)
         for part in range(2):
             mid_part = mid[:, part * 512 : (part + 1) * 512]
-            buffers[2][part, :, :, :, gate_cols] = mm_tn(mid_part, d_gate).astype(bf16).reshape(shape)
-            buffers[2][part, :, :, :, up_cols] = mm_tn(mid_part, d_up).astype(bf16).reshape(shape)
-        buffers[3][y, z] = mm_tn(unit, d_branch).astype(bf16).reshape(2, 2, 192, 1024)
-        for copy in ffn_copies(f):
+            buffers[2 + b][part, :, :, :, gate_cols] = mm_tn(mid_part, d_gate).astype(bf16).reshape(shape)
+            buffers[2 + b][part, :, :, :, up_cols] = mm_tn(mid_part, d_up).astype(bf16).reshape(shape)
+        buffers[4][b, z] = mm_tn(unit, d_branch).astype(bf16).reshape(2, 2, 192, 1024)
+        for copy in ffn_copies(b, f):
             copy.start()
+
+    def first_half(f, carry):
+        ffn_tile(0, f)
 
         @pl.when(f > 0)
         def _():
-            ffn_join(f - 1)
+            ffn_join(0, f - 1)
 
         return carry
 
-    lax.fori_loop(0, 3072 // FF_TILE, ffn_tile, 0)
+    def last_half(f, carry):
+        ffn_tile(1, f)
+
+        @pl.when(f > 2)
+        def _():
+            ffn_join(1, f - 1)
+
+        return carry
+
+    lax.fori_loop(0, 2, first_half, 0)
+    phases((7, 3))
+    gather.finish(1, 3)
+    ffn_join(0, 1)
+    lax.fori_loop(2, 4, last_half, 0)
     valid = r["valid"][...] > 0.5
-    r["out"][...] = jnp.where(valid, r["result"][...], 0.0).astype(bf16).reshape(2, 128, 1024)
+    r["out_out"][...] = jnp.where(valid, r["result"][...], 0.0).astype(bf16).reshape(2, 128, 1024)
+    save("out", r["out_out"])
 
     residual, d_mid = r["residual"][...], r["d_mid"][...]
     scale = inv_rms(residual)
@@ -839,15 +869,15 @@
     )
     r["dg_ffn"][...] = jnp.sum(d_mid * residual * scale, axis=0, keepdims=True)
     d_result = jnp.where(valid, r["cot"][...].reshape(256, 1024).astype(f32), 0.0)
-    r["d_residual"][...] = d_result + d_norm
-    r["d_branch"][...] = r["d_residual"][...].astype(bf16)
+    r["d_residual_out"][...] = d_result + d_norm
+    r["d_branch"][...] = r["d_residual_out"][...].astype(bf16)
 
     def output_tile(j, carry):
         y, z = j // 2, j % 2 * 2
         cols = pl.ds(pl.multiple_of(j * 512, 128), 512)
         d_attn = r["d_branch"][...]
         weights = buffers[1][y, pl.ds(z, 2)].reshape(512, 1024)
-        r["d_attended"][:, :, cols] = mm_nt(d_attn, weights).astype(bf16).reshape(2, 128, 512)
+        r["d_attended_out"][:, :, cols] = mm_nt(d_attn, weights).astype(bf16).reshape(2, 128, 512)
         context = r["context"][:, :, cols].reshape(256, 512)
         buffers[1][y, pl.ds(z, 2)] = mm_tn(context, d_attn).astype(bf16).reshape(2, 2, 128, 1024)
         for copy in output_copies(j):
@@ -867,10 +897,17 @@
         )
 
     lax.fori_loop(0, 4, output_tile, 0)
-    ffn_join(3)
+    save("d_residual", r["d_residual_out"])
+    save("d_attended", r["d_attended_out"])
+    ffn_join(1, 3)
     for half in range(2):
-        save("total_gate_up", buffers[2].at[:, :, core, :, pl.ds(half * 3072, 3072)], r["total_gate_up"].at[half])
-        save("total_down", buffers[3].at[:, :, core, :, pl.ds(half * 512, 512)], r["total_down"].at[half])
+        for b in range(2):
+            save(
+                "total_gate_up",
+                buffers[2 + b].at[:, :, core, :, pl.ds(half * 1536, 1536)],
+                r["total_gate_up"].at[half, :, :, :, pl.ds(b * 1536, 1536)],
+            )
+        save("total_down", buffers[4].at[:, :, core, :, pl.ds(half * 512, 512)], r["total_down"].at[half])
 
     def output_join(j, carry):
         y, z = j // 2, j % 2
@@ -884,7 +921,7 @@
     for half in range(2):
         save("total_output", buffers[1].at[:, :, core, :, pl.ds(half * 512, 512)], r["total_output"].at[half])
     for at in range(4):
-        for copy in ffn_copies(at) + output_copies(at):
+        for copy in ffn_copies(at // 2, at) + output_copies(at):
             copy.wait_send()
     for copy in saved:
         copy.wait()
@@ -916,7 +953,8 @@
     scratch = {
         "buf_qkv": (2, 4, 2, 64, 4096),
         "buf_output": (2, 4, 2, 128, 1024),
-        "buf_gate_up": (2, 4, 2, 64, 6144),
+        "buf_gate_up_0": (2, 4, 2, 64, 3072),
+        "buf_gate_up_1": (2, 4, 2, 64, 3072),
         "buf_down": (2, 4, 2, 192, 1024),
         "tiles": (2, 4, 2, 16, 128),
         "rows": (2, 2, 128, 2048),
@@ -933,7 +971,7 @@
         "d_branch": (256, 1024),
     }
     dma = pltpu.SemaphoreType.DMA
-    sems = [dma((4, KINDS)), dma((4, KINDS)), dma((5,)), dma((5,)), dma((8,)), dma((5, 7)), dma((5, 7)), dma((6,))]
+    sems = [dma((5, KINDS)), dma((5, KINDS)), dma((5,)), dma((5,)), dma((10,)), dma((5, 7)), dma((5, 7)), dma((11,))]
     sems += [pltpu.SemaphoreType.REGULAR, dma((8, 3)), dma((8, 3))]
     buffers = [
         pltpu.VMEM(*(dims if isinstance(dims[0], tuple) else (dims, bf16))) for dims in scratch.values()
@@ -941,9 +979,14 @@
     results = pl.pallas_call(
         functools.partial(forward_kernel),
         out_shape=list(outs.values()),
-        in_specs=[vmem] * 13,
-        out_specs=[vmem] * 7 + [hbm] * 8,
-        scratch_shapes=buffers + sems,
+        in_specs=[hbm] * 8 + [vmem] * 5,
+        out_specs=[vmem if name == "dg_ffn" else hbm for name in outs],
+        scratch_shapes=buffers
+        + sems
+        + [
+            pltpu.VMEM(outs[name].shape, outs[name].dtype)
+            for name in ("out", "d_residual", "d_attended", "x_in", "q_flat", "k_flat")
+        ],
         compiler_params=pltpu.CompilerParams(
             collective_id=1, has_side_effects=True, vmem_limit_bytes=63 * 1024 * 1024
         ),
@@ -959,10 +1002,12 @@
 BACKWARD_OUT = ("d_input", "gains_sum", "sum_qkv", "sum_output", "sum_gate_up", "sum_down")
 BACKWARD_SCRATCH = (
     "buf_qkv", "q_in", "k_in", "v_in", "grad_in", "dq", "dk", "dv", "dk_sum", "dv_sum", "dq_rows", "dk_rows", "dv_rows",
-    "q_flat_in", "k_flat_in", "x_in_in", "d_x", "dg_query", "dg_key", "slots",
+    "q_flat_in", "k_flat_in", "x_in_in", "hidden_in", "d_residual_in", "cos_in", "sin_in", "tiles_in", "dg_ffn_in", "d_x", "dg_query", "dg_key", "slots",
     "reduce_send", "reduce_recv", "load_sem", "small_send", "small_recv", "out_sem", "swap_send", "swap_recv", "in_sem",
 )
-FAR_STAGES = 10
+LATE_LOADS = (
+    "q_flat", "k_flat", "x_in", "weights_qkv", "hidden", "d_residual", "cos", "sin", "gain_tiles", "dg_ffn",
+)
 
 
 def backward_kernel(*refs):
@@ -984,6 +1029,12 @@
                 ("k_flat", "k_flat_in"),
                 ("x_in", "x_in_in"),
                 ("weights_qkv", "buf_qkv"),
+                ("hidden", "hidden_in"),
+                ("d_residual", "d_residual_in"),
+                ("cos", "cos_in"),
+                ("sin", "sin_in"),
+                ("gain_tiles", "tiles_in"),
+                ("dg_ffn", "dg_ffn_in"),
             )
         )
     }
@@ -1012,13 +1063,13 @@
             lambda sender: r["grad_in"].at[slot, token_rows(sender), :],
         )
         copy = pltpu.make_async_copy(
-            r["d_attended"].at[slot, :, head_cols(me, 256)], r["grad_in"].at[slot, token_rows(me), :], r["in_sem"].at[7 + slot]
+            r["d_attended"].at[slot, :, head_cols(me, 256)], r["grad_in"].at[slot, token_rows(me), :], r["in_sem"].at[13 + slot]
         )
         copy.start()
         own.append(copy)
     reduce.load(2).start()
     reduce.load(1).start()
-    for name in ("q_flat", "k_flat", "x_in", "weights_qkv"):
+    for name in LATE_LOADS:
         loads[name].start()
 
     def stages(*steps):
@@ -1027,7 +1078,7 @@
             if number == 9:
                 pltpu.make_async_copy(reduce.result(g), outs[g], r["out_sem"].at[g]).start()
 
-    stages((0, 3), (0, 2))
+    stages((0, 3))
     for name in ("q_heads", "k_heads", "v_heads"):
         loads[name].wait()
 
@@ -1061,34 +1112,28 @@
         )
         r[rows][slot, :, head_cols(me, width)] = r[heads][slot, token_rows(me), :]
 
-    between = (
-        ((1, 3), (0, 1)),
-        ((2, 3), (1, 2), (3, 3)),
-        ((4, 3), (2, 2), (1, 1)),
-        ((5, 3), (3, 2), (2, 1)),
-    )
     for slot in range(2):
         own[slot].wait()
         swap.take(slot, lambda sender: r["grad_in"].at[slot, token_rows(sender), :])
         attend_back(slot, 0)
-        stages(*between[2 * slot])
         attend_back(slot, 1)
         r["dk"][slot] = r["dk_sum"][...].astype(bf16)
         r["dv"][slot] = r["dv_sum"][...].astype(bf16)
         to_rows(2 + 3 * slot, slot, "dq", "dq_rows", 256)
         to_rows(3 + 3 * slot, slot, "dk", "dk_rows", 128)
         to_rows(4 + 3 * slot, slot, "dv", "dv_rows", 128)
-        stages(*between[2 * slot + 1])
-    g_attn, g_query, g_key, _ = gain_rows(r["gain_tiles"])
-    for name in ("q_flat", "k_flat", "x_in", "weights_qkv"):
+        if slot == 0:
+            stages((1, 3))
+    for name in LATE_LOADS:
         loads[name].wait()
-    stages((6, 3), (4, 2), (3, 1), (7, 3), (5, 2), (8, 3), (4, 1), (9, 3), (6, 2), (5, 1))
+    g_attn, g_query, g_key, _ = gain_rows(r["tiles_in"])
+    stages((0, 1), (2, 3), (0, 2), (1, 1), (3, 3))
     for slot in range(2):
         swap.take(2 + 3 * slot, lambda sender: r["dq_rows"].at[slot, :, head_cols(sender, 256)])
         swap.take(3 + 3 * slot, lambda sender: r["dk_rows"].at[slot, :, head_cols(sender, 128)])
         swap.take(4 + 3 * slot, lambda sender: r["dv_rows"].at[slot, :, head_cols(sender, 128)])
 
-    cos, sin = r["cos"], r["sin"]
+    cos, sin = r["cos_in"], r["sin_in"]
     r["d_x"][...] = jnp.zeros((256, 1024), f32)
     r["dg_query"][...] = jnp.zeros((1, 128), f32)
     r["dg_key"][...] = jnp.zeros((1, 128), f32)
@@ -1137,11 +1182,14 @@
             place.to_core,
         )
 
+    stages((1, 2), (4, 3))
     lax.fori_loop(0, 4, query_tile, 0)
     swap_cores(0)
+    stages((2, 1), (5, 3))
     lax.fori_loop(0, 2, key_tile, 0)
     lax.fori_loop(0, 2, value_tile, 0)
     swap_cores(1)
+    stages((2, 2), (3, 1), (6, 3))
     for half in range(2):
         reduce.take(0, 36 + 6 * half, reduce.total(0).at[half])
         accumulate(
@@ -1150,30 +1198,33 @@
         )
     reduce.send_far(0, 0)
 
-    x, d_x = r["hidden"][...].reshape(256, 1024).astype(f32), r["d_x"][...]
+    x, d_x = r["hidden_in"][...].reshape(256, 1024).astype(f32), r["d_x"][...]
     scale = inv_rms(x)
     weighed = g_attn * d_x
     d_norm = scale * weighed - x * (scale * scale * scale) * jnp.mean(x * weighed, axis=-1, keepdims=True)
-    r["d_input"][...] = r["d_residual"][...] + d_norm
     dg_attn = jnp.sum(d_x * x * scale, axis=0, keepdims=True)
+    r["d_x"][...] = r["d_residual_in"][...] + d_norm
+    give = pltpu.make_async_copy(r["d_x"], r["d_input"], r["in_sem"].at[15])
+    give.start()
     rows = [dg_attn[:, at * 128 : (at + 1) * 128] for at in range(8)]
     rows += [r["dg_query"][...], r["dg_key"][...]]
-    rows += [r["dg_ffn"][:, at * 128 : (at + 1) * 128] for at in range(8)]
+    rows += [r["dg_ffn_in"][:, at * 128 : (at + 1) * 128] for at in range(8)]
     rows += [jnp.zeros((6, 128), f32)]
     little.put(0, jnp.concatenate(rows, axis=0))
-    stages((1, 0), (7, 2), (6, 1))
+    stages((3, 2), (4, 1), (7, 3), (1, 0))
     little.put(1, little.sum(0))
-    stages((2, 0), (8, 2), (7, 1))
+    stages((4, 2), (5, 1), (8, 3), (2, 0))
     little.put(2, little.sum(1))
-    stages((3, 0), (9, 2), (8, 1))
+    stages((5, 2), (6, 1), (9, 3), (3, 0))
     little.put(3, little.sum(2))
-    stages((4, 0), (9, 1))
+    stages((6, 2), (7, 1), (4, 0))
     little.put(4, little.sum(3))
-    stages((5, 0), (6, 0))
+    stages((7, 2), (8, 1), (5, 0), (8, 2), (9, 1), (6, 0))
     r["gains_sum"][...] = little.sum(4)
-    stages((7, 0), (8, 0), (9, 0))
+    stages((9, 2), (7, 0), (8, 0), (9, 0))
     reduce.finish()
     swap.finish()
+    give.wait()
     for g in range(4):
         pltpu.make_async_copy(reduce.result(g), outs[g], r["out_sem"].at[g]).wait()
 
@@ -1187,7 +1238,6 @@
     ]
     vmem = pl.BlockSpec(memory_space=pltpu.VMEM)
     hbm = pl.BlockSpec(memory_space=pl.ANY)
-    in_hbm = set(BACKWARD_IN[:11])
     buffers = [
         pltpu.VMEM(dims, dtype)
         for dims, dtype in (
@@ -1207,6 +1257,12 @@
             ((256, 2048), f32),
             ((256, 1024), f32),
             ((256, 1024), bf16),
+            ((2, 128, 1024), bf16),
+            ((256, 1024), f32),
+            ((256, 128), f32),
+            ((256, 128), f32),
+            ((2, 4, 2, 16, 128), bf16),
+            ((1, 1024), f32),
             ((256, 1024), f32),
             ((1, 128), f32),
             ((1, 128), f32),
@@ -1223,13 +1279,13 @@
         dma((4,)),
         dma((8, 7)),
         dma((8, 7)),
-        dma((9,)),
+        dma((16,)),
     ]
     results = pl.pallas_call(
         functools.partial(backward_kernel),
         out_shape=outs,
-        in_specs=[hbm if name in in_hbm else vmem for name in BACKWARD_IN],
-        out_specs=[vmem] * 2 + [hbm] * 4,
+        in_specs=[hbm] * len(BACKWARD_IN),
+        out_specs=[hbm, vmem] + [hbm] * 4,
         scratch_shapes=reduce_scratch() + buffers + sems,
         compiler_params=pltpu.CompilerParams(
             collective_id=2, has_side_effects=True, vmem_limit_bytes=63 * 1024 * 1024
@@ -1237,6 +1293,55 @@
         name="backward",
     )(*[inputs[name] for name in BACKWARD_IN])
     return dict(zip(BACKWARD_OUT, results))
+
+
+def finish_kernel(*refs):
+    qkv, output, gate_up, down, gains = refs[:5]
+    gq, gk, gv, go, gg, gu, gd, d_attn, d_query, d_key, d_ffn = refs[5:]
+    gq[...] = qkv[0].astype(f32)
+    gk[...] = qkv[1, :, :1024].astype(f32)
+    gv[...] = qkv[1, :, 1024:].astype(f32)
+    for half in range(2):
+        cols = slice(half * 512, (half + 1) * 512)
+        go[:, cols] = output[half].astype(f32)
+        gd[:, cols] = down[half].astype(f32)
+    gg[...] = gate_up[0].astype(f32)
+    gu[...] = gate_up[1].astype(f32)
+    dp = lax.axis_index("dp")
+    row, lane = dp // 2, dp % 2 * 64
+    for ref, at in ((d_attn, row), (d_ffn, 10 + row)):
+        ref[...] = pltpu.roll(gains[pl.ds(at, 1), :], lane, 1)[:, :64]
+    for ref, at in ((d_query, 8), (d_key, 9)):
+        ref[...] = pltpu.roll(gains[at : at + 1, :], (128 - dp * 8) % 128, 1)[:, :8]
+
+
+def finish(sums, gains):
+    def shape(*dims):
+        return jax.ShapeDtypeStruct(dims, f32)
+
+    outs = [
+        shape(64, 2048),
+        shape(64, 1024),
+        shape(64, 1024),
+        shape(128, 1024),
+        shape(64, 3072),
+        shape(64, 3072),
+        shape(192, 1024),
+        shape(1, 64),
+        shape(1, 8),
+        shape(1, 8),
+        shape(1, 64),
+    ]
+    vmem = pl.BlockSpec(memory_space=pltpu.VMEM)
+    sums = [part.reshape(2, rows, cols // 2) for part, rows, cols in zip(sums, SHARD_ROWS, COLUMNS)]
+    return pl.pallas_call(
+        functools.partial(finish_kernel),
+        out_shape=outs,
+        in_specs=[vmem] * 5,
+        out_specs=[vmem] * 11,
+        compiler_params=pltpu.CompilerParams(vmem_limit_bytes=32 * 1024 * 1024),
+        name="finish",
+    )(*sums, gains)
 
 
 def rotary_tables(positions):
@@ -1283,17 +1388,9 @@
     done["weights_qkv"] = done["weights_qkv"].reshape(2, 4, 2, 4, 16, 4096)
     last = backward(done)
     sums = [last[name] for name in ("sum_qkv", "sum_output", "sum_gate_up", "sum_down")]
-    d_input, gains_sum = last["d_input"].reshape(2, 128, 1024), last["gains_sum"]
-    qkv, output, gate_up, down = [
-        part.reshape(2, rows, cols // 2).astype(f32) for part, rows, cols in zip(sums, SHARD_ROWS, COLUMNS)
-    ]
-    gq, gk, gv, gg, gu = qkv[0], qkv[1, :, :1024], qkv[1, :, 1024:], gate_up[0], gate_up[1]
-    go, gd = jnp.concatenate([output[0], output[1]], 1), jnp.concatenate([down[0], down[1]], 1)
-    gains_sum = gains_sum.reshape(-1)
-    dg_attn, dg_query, dg_key, dg_ffn = [
-        lax.dynamic_slice(gains_sum, (start + dp * size,), (size,))
-        for start, size in ((0, 64), (1024, 8), (1152, 8), (1280, 64))
-    ]
+    d_input = last["d_input"].reshape(2, 128, 1024)
+    gq, gk, gv, go, gg, gu, gd, *gains = finish(sums, last["gains_sum"])
+    dg_attn, dg_query, dg_key, dg_ffn = [gain.reshape(-1) for gain in gains]
     return (done["out"], d_input, dg_attn, gq, gk, gv, dg_query, dg_key, go, dg_ffn, gg, gu, gd)
 
 

time: 340 us -> 305 us (0.90)
  Pallas kernels: 316 us -> 286 us
    pallas_call x1, Pallas kernels: 161 us -> 140 us  [backward(): pl.pallas_call(functools.partial(backward_kernel), out_shape=outs, in_spe...]
    pallas_call x1, Pallas kernels: 155 us -> 144 us  [forward(): pl.pallas_call(functools.partial(forward_kernel), out_shape=list(outs.val...]
    unnamed x14 -> x18, local copies, waits for them, and re-layouts: 1.79 us -> 6.6 us
where the time goes in v4:
time: 305 us; the launch traced here: 300 us
  Pallas kernels  286 us (94%)
  local copies, waits for them, and re-layouts  10.5 us (3%)
    pallas_call x1, Pallas kernels, forward(): pl.pallas_call(functools.partial(forward_kernel), out_shape=list(outs.val...  144 us
    pallas_call x1, Pallas kernels, backward(): pl.pallas_call(functools.partial(backward_kernel), out_shape=outs, in_spe...  140 us
    unnamed x18, local copies, waits for them, and re-layouts  6.6 us

profile of v4, /device:TPU:0, one launch (start us, length us, event | category | flops | bytes accessed | tf_op | source)
XLA Modules:
  0.0 300.4 jit_solution(13848466187154023378)
XLA Ops:
  0.7 0.7 compare_convert_fusion
  1.4 0.7 convert_bitcast_fusion
  2.1 0.8 dynamic_update_slice.12
  2.9 0.8 dynamic_update_slice.13
  3.7 0.8 dynamic_update_slice.14
  4.5 0.8 dynamic_update_slice.15.refs_7_
  5.3 0.0 copy-start.7
  5.3 0.8 copy.28.refs_12_
  6.1 0.5 fusion
  6.6 0.8 pad_maximum_fusion
  7.5 0.0 copy-done.7
  7.5 144.1 %forward.1 = (bf16[2,128,1024]{2,1,0:T(8,128)(2,1)}, f32[256,1024]{1,0:T(8,128)}, bf16[2,128,2048]{2,1,0:T(8,128)(2,1)}, f32[1,1024]{1,0:T(1,128)}, bf16[256,102...) custom-call(bf16[64,2048]{1,0:T(8,128)(2,1)} %refs_0_.1, ...), custom_call_target="tpu_custom_call" | custom-call | tf_op jit(solution)/shard_map/forward/pallas_call | solution.py:979
  151.6 0.0 copy-start.6
  151.6 140.1 %backward.1 = (f32[256,1024]{1,0:T(8,128)}, f32[24,128]{1,0:T(8,128)}, bf16[2,4,16,2048]{3,2,1,0:T(8,128)(2,1)}, bf16[2,4,32,512]{3,2,1,0:T(8,128)(2,1)}, bf16[2...) custom-call(bf16[2,2,4,4,32,512]{5,4,3,2,1,0:T(8,128)(2,1)} %bitcast.27, ...), custom_call_target="tpu_custom_call" | custom-call | tf_op jit(solution)/shard_map/backward/pallas_call | solution.py:1284
  291.7 0.0 copy-start
  291.7 1.1 copy-done
  292.8 1.0 copy-done.1
  293.9 1.0 copy-done.2
  294.9 0.9 copy-done.3
  295.8 0.7 copy-done.4
  296.5 2.0 finish.1
  298.5 0.0 copy-done.6
  298.5 0.8 copy.35
  299.3 1.0 copy.36
  (9 shorter events, 0.0 us)
Async XLA Ops:
  5.3 2.2 copy-start.7
  151.6 146.9 %copy-start.6 = (bf16[2,128,1024]{2,1,0:T(8,128)(2,1)S(1)}, bf16[2,128,1024]{2,1,0:T(8,128)(2,1)}, u32[]{:S(2)}) copy-start(bf16[2,128,1024]{2,1,0:T(8,128)(2,1)} %get-tuple-element.95) | copy-start | bytes 1572868
  291.7 1.1 copy-start
  292.8 1.0 copy-start.1
  293.9 1.0 copy-start.2
  294.9 0.9 copy-start.3
  295.8 0.7 copy-start.4
  296.5 2.8 copy-start.5
